TPU v7x, 32 devices: a whole 2x2x4 slice. The times are simulated.
32 devices in a mesh: parts: 2 (over y), gy: 8 (over z, x), gx: 2 (over core).
Axes of the slice: x: 2, y: 2, z: 4, core: 2. Of those that a mesh axis runs over, the one named last changes fastest.
Arguments:
- activations: bfloat16 [64, 16384], P(('parts', 'gy'), 'gx'), parts along dimension 0, may hold values from -6 to 6
- qkv_weight: bfloat16 [4, 2304, 16384], P(None, 'gy', 'gx'), may hold values from -0.046875 to 0.046875
- out_weight: bfloat16 [16384, 8192], P('gy', 'gx'), may hold values from -0.0625 to 0.0625
- key_cache: bfloat16 [64, 4, 512, 128], P(('parts', 'gy'), 'gx'), parts along dimension 0, may hold values from -360 to 360
- value_cache: bfloat16 [64, 4, 512, 128], P(('parts', 'gy'), 'gx'), parts along dimension 0, may hold values from -6 to 6
- lengths: int32 [64], P(('parts', 'gy')), parts along dimension 0, may hold values from 1 to 512, as said below
Outputs:
- attn_out: bfloat16 [64, 16384], P(('parts', 'gx'), 'gy'), parts along dimension 0
There are 2 independent parts, one for each index of `parts`. A program takes and returns all parts, laid end to end along the dimension named above; an argument that names none is the same for every part. Nothing has to cross between parts.
Inputs may be any that keep to these rules, and one draw needn't show every extreme that they name: Sequence b uses cache slots 0 to lengths[b] - 1; at least one sequence has exactly 512.
All inputs are finite; a program needn't handle non-finite values.
Results may differ from a plain program's by a relative error of at most 0.012.
The roundings to bfloat16 on the way count: a program that leaves them out, or rounds other values in their place, can miss the bound.
Values may be sent and summed in bfloat16 or wider, within the bound.
No kernel may reach another device: no remote copies, remote signals or barrier semaphores. Data moves between devices by JAX's collectives and lax.ppermute only.
A program may use at most 128 MiB of HBM per device.

v0:
```python
import jax
import jax.numpy as jnp
from jax import lax
from jax.sharding import PartitionSpec as P

HD = 128
GROUP = 16


NEG_FILL = -1e30


def normalize(scores, own_score, live):
    scores = jnp.where(live, scores, NEG_FILL)
    top = jnp.maximum(jnp.max(scores, axis=3), own_score)
    weights = jnp.where(live, jnp.exp(scores - top[..., None]), 0.0)
    own_weight = jnp.exp(own_score - top)
    denom = jnp.sum(weights, axis=3) + own_weight
    return (
        (weights / denom[..., None]).astype(jnp.bfloat16),
        (own_weight / denom).astype(jnp.bfloat16),
    )


def local(activations, qkv_weight, out_weight, key_cache, value_cache, lengths):
    head_count, col_part, half_width = qkv_weight.shape
    flat_weight = qkv_weight.reshape(head_count * col_part, half_width)
    row_piece = lax.all_gather(activations, "gy", axis=0, tiled=True)
    product = lax.dot_general(
        row_piece, flat_weight, (((1,), (1,)), ((), ())), preferred_element_type=jnp.float32
    )
    partial_value = product.reshape(row_piece.shape[0], head_count, col_part)
    summed = lax.psum_scatter(
        partial_value.astype(jnp.bfloat16), "gx", scatter_dimension=1, tiled=True
    )
    joined = lax.all_to_all(summed, "gy", split_axis=0, concat_axis=2, tiled=True)
    seq_local, kv_local, cache_len = (key_cache.shape[0], key_cache.shape[1], key_cache.shape[2])
    queries = joined[:, :, : GROUP * HD].reshape(seq_local, kv_local, GROUP, HD)
    new_key = joined[:, :, GROUP * HD : (GROUP + 1) * HD]
    new_value = joined[:, :, (GROUP + 1) * HD :]
    score_scale = HD ** (-0.5)
    own_score = (
        jnp.einsum("skgh,skh->skg", queries, new_key, preferred_element_type=jnp.float32)
        * score_scale
    )
    positions = jnp.arange(cache_len, dtype=jnp.int32)
    live = positions[None, None, None, :] < lengths[:, None, None, None]
    scores = (
        jnp.einsum("skgh,skth->skgt", queries, key_cache, preferred_element_type=jnp.float32)
        * score_scale
    )
    weights, own_weight = normalize(scores, own_score, live)
    mixed = jnp.einsum("skgt,skth->skgh", weights, value_cache, preferred_element_type=jnp.float32)
    mixed = (
        mixed
        + own_weight.astype(jnp.float32)[..., None] * new_value.astype(jnp.float32)[:, :, None, :]
    )
    attended = mixed.astype(jnp.bfloat16).reshape(seq_local, kv_local * GROUP * HD)
    terms = lax.dot_general(
        lax.all_gather(attended, "gy", axis=0, tiled=True),
        out_weight,
        (((1,), (1,)), ((), ())),
        preferred_element_type=jnp.float32,
    )
    return lax.psum_scatter(terms.astype(jnp.bfloat16), "gx", scatter_dimension=0, tiled=True)


def solution(mesh):
    in_specs = (
        P(("parts", "gy"), "gx"),
        P(None, "gy", "gx"),
        P("gy", "gx"),
        P(("parts", "gy"), "gx", None, None),
        P(("parts", "gy"), "gx", None, None),
        P(("parts", "gy")),
    )
    out_specs = P(("parts", "gx"), "gy")
    return jax.shard_map(local, mesh=mesh, in_specs=in_specs, out_specs=out_specs, check_vma=False)
```

profile of v0, /device:TPU:0, one launch (start us, length us, event | category | flops | bytes accessed | tf_op | source)
XLA Modules:
  0.0 129.4 jit_solution(17512597355810236325)
XLA Ops:
  6.5 0.0 copy-start
  6.5 0.0 copy-start.1
  6.5 0.0 copy-start.2
  6.5 0.0 reduce-scatter.3.cloned.1.call-start
  6.5 33.4 %all-gather = bf16[8,4,8192]{2,1,0:T(4,128)(2,1)S(1)} all-gather(bf16[1,4,8192]{2,1,0:T(4,128)(2,1)} %bitcast.23), channel_id=1, replica_groups=mesh['parts'=2,'gy'=8,'gx'=2] {'gy'}, dimensions={0}, use_global_device_ids=true | all-gather | bytes 589824 | tf_op jit(solution)/shard_map/all_gather | solution.py:28
  39.9 0.1 reshape.42
  40.0 10.8 %convolution_convert_fusion.1 = bf16[32,4,288]{2,0,1:T(8,128)(2,1)} fusion(bf16[32,8192,1]{1,0,2:T(8,128)(2,1)S(1)} %reshape.42, bf16[4,288,8192]{2,1,0:T(8,128)(2,1)} %param.7), kind=kOutput, calls=%fused_computation.3 | convolution fusion | flops 604016640 | bytes 19472384 | tf_op jit(solution)/shard_map/dot_general | solution.py:29
  50.8 0.0 reduce-scatter.3.cloned.1.call-update
  50.8 8.8 %reduce-scatter.3.cloned.1.call-done = bf16[32,2,288]{2,0,1:T(8,128)(2,1)} async-done(((bf16[32,4,288]{2,0,1:T(8,128)(2,1)}), bf16[32,2,288]{2,0,1:T(8,128)(2,1)}) %reduce-scatter.3.cloned.1.call-update) | async-done | bytes 36880 | tf_op jit(solution)/shard_map/reduce_scatter | solution.py:33
  59.6 1.5 %copy.8 = bf16[32,2,288]{2,1,0:T(2,128)(2,1)} copy(bf16[32,2,288]{2,0,1:T(8,128)(2,1)} %reduce-scatter.3.cloned.1.call-done) | data formatting | bytes 73728 | tf_op jit(solution)/shard_map/reduce_scatter | solution.py:33
  61.0 5.7 %all-to-all-start = ((bf16[32,2,288]{2,1,0:T(2,128)(2,1)}), bf16[32,2,288]{2,1,0:T(2,128)(2,1)S(1)}, u32[]{:S(2)}, u32[]{:S(2)}) async-start(bf16[32,2,288]{2,1,0:T(2,128)(2,1)} %copy.8), calls=%async_computation.1 | async-start | bytes 98304 | tf_op jit(solution)/shard_map/all_to_all | solution.py:36
  66.8 0.0 reduce-scatter.5.cloned.1.call-start
  66.8 0.0 copy-done.1
  66.8 0.1 iota_compare_fusion
  66.9 6.7 %all-to-all-done = bf16[32,2,288]{2,1,0:T(2,128)(2,1)S(1)} async-done(((bf16[32,2,288]{2,1,0:T(2,128)(2,1)}), bf16[32,2,288]{2,1,0:T(2,128)(2,1)S(1)}, u32[]{:S(2)}, u32[]{:S(2)}) %all-to-all-start) | async-done | bytes 36896 | tf_op jit(solution)/shard_map/all_to_all | solution.py:36
  73.6 0.1 all_to_all.16
  73.8 0.1 fusion.7
  73.9 0.0 copy-done
  73.9 0.5 fusion.12
  74.4 0.2 fusion.2
  74.6 0.0 copy-done.2
  74.6 0.3 fusion.1
  75.0 30.7 %all-gather.1 = bf16[8,4,4096]{2,1,0:T(4,128)(2,1)S(1)} all-gather(bf16[1,4,4096]{2,1,0:T(4,128)(2,1)S(1)} %reshape.39), channel_id=1, replica_groups=mesh['parts'=2,'gy'=8,'gx'=2] {'gy'}, dimensions={0}, use_global_device_ids=true | all-gather | bytes 294912 | tf_op jit(solution)/shard_map/all_gather | solution.py:60
  105.7 0.1 reshape.40
  105.8 11.5 %convolution_convert_fusion = bf16[32,2048]{1,0:T(8,128)(2,1)} fusion(bf16[32,4096]{1,0:T(8,128)(2,1)S(1)} %reshape.40, bf16[2048,4096]{1,0:T(8,128)(2,1)} %param.8), kind=kOutput, calls=%fused_computation | convolution fusion | flops 536936448 | bytes 17170432 | tf_op jit(solution)/shard_map/dot_general | solution.py:59
  117.3 0.0 reduce-scatter.5.cloned.1.call-update
  117.3 5.3 %reduce-scatter.5.cloned.1.call-done = bf16[16,2048]{1,0:T(8,128)(2,1)} async-done(((bf16[32,2048]{1,0:T(8,128)(2,1)}), bf16[16,2048]{1,0:T(8,128)(2,1)}) %reduce-scatter.5.cloned.1.call-update) | async-done | bytes 65552 | tf_op jit(solution)/shard_map/reduce_scatter | solution.py:65
  (7 shorter events, 0.1 us)
Async XLA Ops:
  6.5 67.4 %copy-start = (bf16[4,2,512,128]{3,2,1,0:T(8,128)(2,1)S(1)}, bf16[4,2,512,128]{3,2,1,0:T(8,128)(2,1)}, u32[]{:S(2)}) copy-start(bf16[4,2,512,128]{3,2,1,0:T(8,128)(2,1)} %param.9) | copy-start | bytes 3145732
  6.5 60.3 %copy-start.1 = (s32[4]{0:T(128)S(1)}, s32[4]{0:T(128)}, u32[]{:S(2)}) copy-start(s32[4]{0:T(128)} %param.11) | copy-start | bytes 52
  6.5 68.1 %copy-start.2 = (bf16[4,2,512,128]{3,2,1,0:T(8,128)(2,1)S(1)}, bf16[4,2,512,128]{3,2,1,0:T(8,128)(2,1)}, u32[]{:S(2)}) copy-start(bf16[4,2,512,128]{3,2,1,0:T(8,128)(2,1)} %param.10) | copy-start | bytes 3145732
  6.5 53.0 %reduce-scatter.3.cloned.1.call-start = ((), (), s32[]{:S(2)}) async-start(), calls=%async_computation.3 | async-start | bytes 147456 | tf_op jit(solution)/shard_map/reduce_scatter | solution.py:33
  61.0 12.5 %all-to-all-start = ((bf16[32,2,288]{2,1,0:T(2,128)(2,1)}), bf16[32,2,288]{2,1,0:T(2,128)(2,1)S(1)}, u32[]{:S(2)}, u32[]{:S(2)}) async-start(bf16[32,2,288]{2,1,0:T(2,128)(2,1)} %copy.8), calls=%async_computation.1 | async-start | bytes 98304 | tf_op jit(solution)/shard_map/all_to_all | solution.py:36
  66.8 55.8 %reduce-scatter.5.cloned.1.call-start = ((), (), s32[]{:S(2)}) async-start(), calls=%async_computation.4 | async-start | bytes 196608 | tf_op jit(solution)/shard_map/reduce_scatter | solution.py:65
Sparse Core Ops, SparseCore 0:
  50.9 8.5 reduce-scatter.2
  117.4 5.0 reduce-scatter.4
where the time goes:
time: 130 us; the launch traced here: 129 us
  blocking collectives  64.1 us (49%)
  matrix products  23.1 us (18%)
  waiting for transfers between devices  20.7 us (16%)
  between operations  13.5 us (10%)
  starting transfers between devices  5.78 us (4%)
  local copies, waits for them, and re-layouts  1.86 us (1%)
    all_gather x1, blocking collectives, local(): row_piece = lax.all_gather(activations, 'gy', axis=0, tiled=True)  33.4 us
    all_gather x1, blocking collectives, local(): lax.all_gather(attended, 'gy', axis=0, tiled=True)  30.7 us
    dot_general x1, matrix products, local(): lax.dot_general(lax.all_gather(attended, 'gy', axis=0, tiled=True), out_w...  11.5 us
    dot_general x1, matrix products, local(): lax.dot_general(row_piece, flat_weight, (((1,), (1,)), ((), ())), preferr...  10.8 us
    reduce_scatter x1, waiting for transfers between devices, local(): lax.psum_scatter(partial_value.astype(jnp.bfloat16), 'gx', scatter_dimens...  8.75 us
    all_to_all x1, waiting for transfers between devices, local(): lax.all_to_all(summed, 'gy', split_axis=0, concat_axis=2, tiled=True)  6.67 us
    all_to_all x1, starting transfers between devices, local(): lax.all_to_all(summed, 'gy', split_axis=0, concat_axis=2, tiled=True)  5.74 us
    reduce_scatter x1, waiting for transfers between devices, local(): lax.psum_scatter(terms.astype(jnp.bfloat16), 'gx', scatter_dimension=0, t...  5.25 us
  transfers between devices with their start and end apart: 3, of which 3 were waited for; matrix products, arithmetic and copies ran while one was open for 0% of the time, Pallas kernels for 0%

commit v1 on v0

--- a/solution.py
+++ b/solution.py
@@ -1,13 +1,17 @@
+import functools
+
 import jax
 import jax.numpy as jnp
 from jax import lax
+from jax.experimental import pallas as pl
+from jax.experimental.pallas import tpu as pltpu
 from jax.sharding import PartitionSpec as P
 
 HD = 128
 GROUP = 16
-
-
+MIB = 1 << 20
 NEG_FILL = -1e30
+NT = (((1,), (1,)), ((), ()))
 
 
 def normalize(scores, own_score, live):
@@ -22,13 +26,11 @@
     )
 
 
-def local(activations, qkv_weight, out_weight, key_cache, value_cache, lengths):
+def local_plain(activations, qkv_weight, out_weight, key_cache, value_cache, lengths):
     head_count, col_part, half_width = qkv_weight.shape
     flat_weight = qkv_weight.reshape(head_count * col_part, half_width)
     row_piece = lax.all_gather(activations, "gy", axis=0, tiled=True)
-    product = lax.dot_general(
-        row_piece, flat_weight, (((1,), (1,)), ((), ())), preferred_element_type=jnp.float32
-    )
+    product = lax.dot_general(row_piece, flat_weight, NT, preferred_element_type=jnp.float32)
     partial_value = product.reshape(row_piece.shape[0], head_count, col_part)
     summed = lax.psum_scatter(
         partial_value.astype(jnp.bfloat16), "gx", scatter_dimension=1, tiled=True
@@ -59,10 +61,162 @@
     terms = lax.dot_general(
         lax.all_gather(attended, "gy", axis=0, tiled=True),
         out_weight,
-        (((1,), (1,)), ((), ())),
+        NT,
         preferred_element_type=jnp.float32,
     )
     return lax.psum_scatter(terms.astype(jnp.bfloat16), "gx", scatter_dimension=0, tiled=True)
+
+
+def swap(x):
+    return lax.ppermute(x, "gx", [(0, 1), (1, 0)])
+
+
+def hop(x, chips, step):
+    half = chips // 2
+    pairs = []
+    for chip in range(chips):
+        for core in range(2):
+            pairs.append((2 * chip + core, 2 * (chip ^ (step + core * half)) + core))
+    return lax.ppermute(x, ("gy", "gx"), pairs)
+
+
+def gather_rows(block, chips):
+    rows = block.shape[0]
+    both = jnp.concatenate([block, swap(block)], axis=0)
+    got = [hop(both, chips, step) for step in range(chips // 2)]
+    theirs = swap(jnp.concatenate([piece[rows:] for piece in got], axis=0))
+    return jnp.concatenate([piece[:rows] for piece in got] + [theirs], axis=0)
+
+
+def project_kernel(x_ref, w_ref, keep_ref, send_ref):
+    half = keep_ref.shape[1]
+    for head in range(w_ref.shape[0]):
+        value = lax.dot_general(x_ref[...], w_ref[head], NT, preferred_element_type=jnp.float32)
+        value = value.astype(jnp.bfloat16)
+        keep_ref[head] = value[:half]
+        send_ref[head] = value[half:]
+
+
+def attend_kernel(place_ref, lengths_ref, mine_ref, theirs_ref, key_ref, value_ref, out_ref, wide, tall):
+    chips = 2 * mine_ref.shape[0]
+    seqs, heads, slots = key_ref.shape[0], key_ref.shape[1], key_ref.shape[2]
+    part = mine_ref.shape[3]
+    chip, core = place_ref[0], place_ref[1]
+    half = chips // 2
+    for head in range(heads):
+        at = core * heads + head
+        for other in range(chips):
+            mask = chip ^ other
+            step = mask & (half - 1)
+            near = (mask // half) == core
+            piece = jnp.where(
+                near,
+                mine_ref[step, at].astype(jnp.float32),
+                theirs_ref[step, at].astype(jnp.float32),
+            )
+            wide[:, other * part : (other + 1) * part] = piece
+        for column in range(GROUP + 2):
+            tall[head, :, column, :] = wide[:, column * HD : (column + 1) * HD]
+    scale = HD ** (-0.5)
+    position = lax.broadcasted_iota(jnp.int32, (GROUP, slots), 1)
+    for seq in range(seqs):
+        live = position < lengths_ref[seq]
+        for head in range(heads):
+            query = tall[head, seq, :GROUP, :]
+            new_key = tall[head, seq, GROUP : GROUP + 1, :]
+            new_value = tall[head, seq, GROUP + 1 : GROUP + 2, :]
+            own = jnp.sum(query * new_key, axis=1, keepdims=True) * scale
+            scores = lax.dot_general(
+                query.astype(jnp.bfloat16), key_ref[seq, head], NT, preferred_element_type=jnp.float32
+            )
+            scores = jnp.where(live, scores * scale, NEG_FILL)
+            top = jnp.maximum(jnp.max(scores, axis=1, keepdims=True), own)
+            weights = jnp.where(live, jnp.exp(scores - top), 0.0)
+            own_weight = jnp.exp(own - top)
+            denom = jnp.sum(weights, axis=1, keepdims=True) + own_weight
+            weights = (weights / denom).astype(jnp.bfloat16)
+            own_weight = (own_weight / denom).astype(jnp.bfloat16).astype(jnp.float32)
+            mixed = jnp.dot(weights, value_ref[seq, head], preferred_element_type=jnp.float32)
+            mixed = mixed + own_weight * new_value
+            for query_head in range(GROUP):
+                column = (head * GROUP + query_head) * HD
+                wide2 = mixed[query_head : query_head + 1]
+                out_ref[seq : seq + 1, column : column + HD] = wide2
+
+
+def output_kernel(place_ref, x_ref, w_ref, keep_ref, send_ref, *, rows):
+    total = x_ref.shape[0]
+    half = total // 2
+    row = lax.broadcasted_iota(jnp.int32, (total, total), 0)
+    column = lax.broadcasted_iota(jnp.int32, (total, total), 1)
+    order = jnp.where((row ^ (place_ref[0] * rows)) == column, 1.0, 0.0).astype(jnp.bfloat16)
+    x = jnp.dot(order, x_ref[...], preferred_element_type=jnp.float32).astype(jnp.bfloat16)
+    value = lax.dot_general(x, w_ref[...], NT, preferred_element_type=jnp.float32)
+    value = value.astype(jnp.bfloat16)
+    keep_ref[...] = value[:half]
+    send_ref[...] = value[half:]
+
+
+def in_vmem(count):
+    return [pl.BlockSpec(memory_space=pltpu.VMEM)] * count
+
+
+def in_smem(count):
+    return [pl.BlockSpec(memory_space=pltpu.SMEM)] * count
+
+
+def hold(x):
+    return pltpu.with_memory_space_constraint(x, pltpu.VMEM)
+
+
+def local(activations, qkv_weight, out_weight, key_cache, value_cache, lengths, *, chips):
+    heads, part, _ = qkv_weight.shape
+    seqs, kv_local, slots, _ = key_cache.shape
+    out_cols = out_weight.shape[0]
+    half = chips // 2 * seqs
+    place = jnp.stack([lax.axis_index("gy"), lax.axis_index("gx")]).astype(jnp.int32)
+
+    x = gather_rows(activations, chips)
+    piece = jax.ShapeDtypeStruct((heads, half, part), jnp.bfloat16)
+    keep, send = pl.pallas_call(
+        project_kernel,
+        out_shape=(piece, piece),
+        in_specs=in_vmem(2),
+        out_specs=tuple(in_vmem(2)),
+        compiler_params=pltpu.CompilerParams(vmem_limit_bytes=8 * MIB),
+        name="project",
+    )(hold(x), hold(qkv_weight))
+    joined = (keep.astype(jnp.float32) + swap(send).astype(jnp.float32)).astype(jnp.bfloat16)
+    got = [hop(joined[:, step * seqs : (step + 1) * seqs], chips, step) for step in range(chips // 2)]
+    mine = jnp.stack(got)
+    theirs = swap(mine)
+
+    feats = kv_local * GROUP * HD
+    attended = pl.pallas_call(
+        attend_kernel,
+        out_shape=jax.ShapeDtypeStruct((seqs, feats), jnp.float32),
+        in_specs=in_smem(2) + in_vmem(4),
+        out_specs=in_vmem(1)[0],
+        scratch_shapes=[
+            pltpu.VMEM((seqs, chips * part), jnp.float32),
+            pltpu.VMEM((kv_local, seqs, GROUP + 8, HD), jnp.float32),
+        ],
+        compiler_params=pltpu.CompilerParams(vmem_limit_bytes=8 * MIB),
+        name="attend",
+    )(place, lengths, hold(mine), hold(theirs), hold(key_cache), hold(value_cache))
+    attended = attended.astype(jnp.bfloat16)
+
+    x = gather_rows(attended, chips)
+    piece = jax.ShapeDtypeStruct((half, out_cols), jnp.bfloat16)
+    keep, send = pl.pallas_call(
+        functools.partial(output_kernel, rows=seqs),
+        out_shape=(piece, piece),
+        in_specs=in_smem(1) + in_vmem(2),
+        out_specs=tuple(in_vmem(2)),
+        compiler_params=pltpu.CompilerParams(vmem_limit_bytes=8 * MIB),
+        name="output",
+    )(place, hold(x), hold(out_weight))
+    return (keep.astype(jnp.float32) + swap(send).astype(jnp.float32)).astype(jnp.bfloat16)
 
 
 def solution(mesh):
@@ -75,4 +229,16 @@
         P(("parts", "gy")),
     )
     out_specs = P(("parts", "gx"), "gy")
-    return jax.shard_map(local, mesh=mesh, in_specs=in_specs, out_specs=out_specs, check_vma=False)
+    chips = mesh.shape["gy"]
+
+    def whole(activations, qkv_weight, *rest):
+        part = qkv_weight.shape[1] // chips
+        seqs = activations.shape[0] // (mesh.shape["parts"] * chips)
+        paired = mesh.shape["gx"] == 2 and chips in (2, 4, 8, 16) and part % 16 == 0
+        paired = paired and seqs & (seqs - 1) == 0 and (chips // 2 * seqs) % 16 == 0
+        body = functools.partial(local, chips=chips) if paired else local_plain
+        return jax.shard_map(
+            body, mesh=mesh, in_specs=in_specs, out_specs=out_specs, check_vma=False
+        )(activations, qkv_weight, *rest)
+
+    return whole

time: 130 us -> 81.6 us (0.63)
  blocking collectives: 64.1 us -> 0 us
  starting transfers between devices: 5.78 us -> 29.8 us
  matrix products: 23.1 us -> 0 us
  Pallas kernels: 0 us -> 14.5 us
  between operations: 13.5 us -> 0.15 us
  local copies, waits for them, and re-layouts: 1.86 us -> 12.8 us
  other arithmetic: 0.32 us -> 1.98 us
  waiting for transfers between devices: 20.7 us -> 22.1 us
    all_gather x2 -> x0, blocking collectives: 64.1 us -> none  [the longest x1 33.4 us: local(): row_piece = lax.all_gather(activations, 'gy', axis=0, tiled=True)]
    ppermute x0 -> x19, starting transfers between devices: none -> 29.8 us  [the longest x7 15.8 us: swap(): return lax.ppermute(x, 'gx', [(0, 1), (1, 0)])]
    dot_general x5 -> x0, matrix products: 23.1 us -> none  [the longest x1 11.5 us: local(): lax.dot_general(lax.all_gather(attended, 'gy', axis=0, tiled=True), out_w...]
    ppermute x0 -> x19, waiting for transfers between devices: none -> 22.1 us  [the longest x12 15.3 us: hop(): return lax.ppermute(x, ('gy', 'gx'), pairs)]
    pallas_call x0 -> x3, Pallas kernels: none -> 14.5 us  [the longest x1 5.67 us: local(): pl.pallas_call(functools.partial(output_kernel, rows=seqs), out_shape=(pi...]
    reduce_scatter x2 -> x0, waiting for transfers between devices: 14 us -> none  [the longest x1 8.75 us: local(): lax.psum_scatter(partial_value.astype(jnp.bfloat16), 'gx', scatter_dimens...]
    unnamed x9 -> x10, local copies, waits for them, and re-layouts: 0.22 us -> 12.1 us
    all_to_all x1 -> x0, waiting for transfers between devices: 6.67 us -> none  [local(): lax.all_to_all(summed, 'gy', split_axis=0, concat_axis=2, tiled=True)]
  transfers between devices with their start and end apart: 3 -> 19, of which waited for: 3 -> 15; matrix products, arithmetic and copies ran while one was open for 0% -> 0% of each run, Pallas kernels for 0% -> 0%
where the time goes in v1:
time: 81.6 us; the launch traced here: 81.3 us
  starting transfers between devices  29.8 us (37%)
  waiting for transfers between devices  22.1 us (27%)
  Pallas kernels  14.5 us (18%)
  local copies, waits for them, and re-layouts  12.8 us (16%)
  other arithmetic  1.98 us (2%)
    ppermute x7, starting transfers between devices, swap(): return lax.ppermute(x, 'gx', [(0, 1), (1, 0)])  15.8 us
    ppermute x12, waiting for transfers between devices, hop(): return lax.ppermute(x, ('gy', 'gx'), pairs)  15.3 us
    ppermute x12, starting transfers between devices, hop(): return lax.ppermute(x, ('gy', 'gx'), pairs)  14 us
    unnamed x10, local copies, waits for them, and re-layouts  12.1 us
    ppermute x7, waiting for transfers between devices, swap(): return lax.ppermute(x, 'gx', [(0, 1), (1, 0)])  6.71 us
    pallas_call x1, Pallas kernels, local(): pl.pallas_call(functools.partial(output_kernel, rows=seqs), out_shape=(pi...  5.67 us
    pallas_call x1, Pallas kernels, local(): pl.pallas_call(project_kernel, out_shape=(piece, piece), in_specs=in_vmem...  5.47 us
    pallas_call x1, Pallas kernels, local(): pl.pallas_call(attend_kernel, out_shape=jax.ShapeDtypeStruct((seqs, feats...  3.39 us
  transfers between devices with their start and end apart: 19, of which 15 were waited for; matrix products, arithmetic and copies ran while one was open for 0% of the time, Pallas kernels for 0%

profile of v1, /device:TPU:0, one launch (start us, length us, event | category | flops | bytes accessed | tf_op | source)
XLA Modules:
  0.0 81.3 jit_solution(14740364924292110341)
XLA Ops:
  0.5 1.1 %collective-permute-done = bf16[4,8192]{1,0:T(4,128)(2,1)S(1)} collective-permute-done((bf16[4,8192]{1,0:T(4,128)(2,1)}, bf16[4,8192]{1,0:T(4,128)(2,1)S(1)}, u32[]{:S(2)}, u32[]{:S(2)}) %collective-permute-start) | collective-permute-done | bytes 65568 | tf_op jit(solution)/shard_map/ppermute | solution.py:71
  1.6 0.9 %pad_maximum_fusion.1 = bf16[8,8192]{1,0:T(8,128)(2,1)S(1)} fusion(bf16[4,8192]{1,0:T(4,128)(2,1)S(1)} %collective-permute-done, bf16[4,8192]{1,0:T(4,128)(2,1)} %param.6), kind=kLoop, calls=%fused_computation.1 | loop fusion | flops 262144 | bytes 262144 | tf_op jit(solution)/shard_map/concatenate | solution.py:85
  2.6 0.7 collective-permute-start.1
  3.2 2.9 %collective-permute-start.2 = (bf16[8,8192]{1,0:T(8,128)(2,1)S(1)}, bf16[8,8192]{1,0:T(8,128)(2,1)S(1)}, u32[]{:S(2)}, u32[]{:S(2)}) collective-permute-start(bf16[8,8192]{1,0:T(8,128)(2,1)S(1)} %pad_maximum_fusion.1), channel_id=1, source_target_pairs={{0,2},{1,11},{2,0},{3,9},{4,6},{5,15},{6,4},{7,13},{8,10},{9,3},{1... | collective-permute-start | bytes 393224 | tf_op jit(solution)/shard_map/ppermute | solution.py:80
  6.1 1.6 %collective-permute-start.3 = (bf16[8,8192]{1,0:T(8,128)(2,1)S(1)}, bf16[8,8192]{1,0:T(8,128)(2,1)S(1)}, u32[]{:S(2)}, u32[]{:S(2)}) collective-permute-start(bf16[8,8192]{1,0:T(8,128)(2,1)S(1)} %pad_maximum_fusion.1), channel_id=1, source_target_pairs={{0,4},{1,13},{2,6},{3,15},{4,0},{5,9},{6,2},{7,11},{8,12},{9,5},{1... | collective-permute-start | bytes 393224 | tf_op jit(solution)/shard_map/ppermute | solution.py:80
  7.8 1.3 %collective-permute-done.2 = bf16[8,8192]{1,0:T(8,128)(2,1)S(1)} collective-permute-done((bf16[8,8192]{1,0:T(8,128)(2,1)S(1)}, bf16[8,8192]{1,0:T(8,128)(2,1)S(1)}, u32[]{:S(2)}, u32[]{:S(2)}) %collective-permute-start.2) | collective-permute-done | bytes 131104 | tf_op jit(solution)/shard_map/ppermute | solution.py:80
  9.1 2.9 %collective-permute-done.3 = bf16[8,8192]{1,0:T(8,128)(2,1)S(1)} collective-permute-done((bf16[8,8192]{1,0:T(8,128)(2,1)S(1)}, bf16[8,8192]{1,0:T(8,128)(2,1)S(1)}, u32[]{:S(2)}, u32[]{:S(2)}) %collective-permute-start.3) | collective-permute-done | bytes 131104 | tf_op jit(solution)/shard_map/ppermute | solution.py:80
  12.1 2.7 %collective-permute-done.4 = bf16[8,8192]{1,0:T(8,128)(2,1)S(1)} collective-permute-done((bf16[8,8192]{1,0:T(8,128)(2,1)S(1)}, bf16[8,8192]{1,0:T(8,128)(2,1)S(1)}, u32[]{:S(2)}, u32[]{:S(2)}) %collective-permute-start.4) | collective-permute-done | bytes 131104 | tf_op jit(solution)/shard_map/ppermute | solution.py:80
  15.0 4.9 %collective-permute-start.5 = (bf16[16,8192]{1,0:T(8,128)(2,1)S(1)}, bf16[16,8192]{1,0:T(8,128)(2,1)S(1)}, u32[]{:S(2)}, u32[]{:S(2)}) collective-permute-start(bf16[16,8192]{1,0:T(8,128)(2,1)S(1)} %pad_maximum_fusion), channel_id=1, source_target_pairs={{0,1},{1,0},{2,3},{3,2},{4,5},{5,4},{6,7},{7,6},{8,9},{9,8},{10,11... | collective-permute-start | bytes 786440 | tf_op jit(solution)/shard_map/ppermute | solution.py:71
  20.0 1.2 %collective-permute-done.5 = bf16[16,8192]{1,0:T(8,128)(2,1)S(1)} collective-permute-done((bf16[16,8192]{1,0:T(8,128)(2,1)S(1)}, bf16[16,8192]{1,0:T(8,128)(2,1)S(1)}, u32[]{:S(2)}, u32[]{:S(2)}) %collective-permute-start.5) | collective-permute-done | bytes 262176 | tf_op jit(solution)/shard_map/ppermute | solution.py:71
  21.4 6.4 %copy-done = bf16[4,288,8192]{2,1,0:T(8,128)(2,1)S(1)} copy-done((bf16[4,288,8192]{2,1,0:T(8,128)(2,1)S(1)}, bf16[4,288,8192]{2,1,0:T(8,128)(2,1)}, u32[]{:S(2)}) %copy-start) | copy-done | bytes 18874392
  27.8 5.5 %project.1 = (bf16[4,16,288]{2,1,0:T(8,128)(2,1)S(1)}, bf16[4,16,288]{2,1,0:T(8,128)(2,1)S(1)}) custom-call(bf16[32,8192]{1,0:T(8,128)(2,1)S(1)} %concatenate.20.x_ref, bf16[4,288,8192]{2,1,0:T(8,128)(2,1)S(1)} %copy-done), custom_call_target="tpu_custom_call" | custom-call | tf_op jit(solution)/shard_map/project/pallas_call | solution.py:181
  33.6 0.9 %collective-permute-done.6 = bf16[4,16,288]{2,1,0:T(8,128)(2,1)S(1)} collective-permute-done((bf16[4,16,288]{2,1,0:T(8,128)(2,1)S(1)}, bf16[4,16,288]{2,1,0:T(8,128)(2,1)S(1)}, u32[]{:S(2)}, u32[]{:S(2)}) %collective-permute-start.6) | collective-permute-done | bytes 36896 | tf_op jit(solution)/shard_map/ppermute | solution.py:71
  35.2 0.7 collective-permute-start.8
  35.9 2.8 %collective-permute-start.9 = (bf16[4,4,288]{2,1,0:T(4,128)(2,1)S(1)}, bf16[4,4,288]{2,1,0:T(4,128)(2,1)S(1)}, u32[]{:S(2)}, u32[]{:S(2)}) collective-permute-start(bf16[4,4,288]{2,1,0:T(4,128)(2,1)S(1)} %get-tuple-element.31), channel_id=1, source_target_pairs={{0,4},{1,13},{2,6},{3,15},{4,0},{5,9},{6,2},{7,11},{8,12},{9,5},{1... | collective-permute-start | bytes 27656 | tf_op jit(solution)/shard_map/ppermute | solution.py:80
  39.2 1.2 %collective-permute-done.9 = bf16[4,4,288]{2,1,0:T(4,128)(2,1)S(1)} collective-permute-done((bf16[4,4,288]{2,1,0:T(4,128)(2,1)S(1)}, bf16[4,4,288]{2,1,0:T(4,128)(2,1)S(1)}, u32[]{:S(2)}, u32[]{:S(2)}) %collective-permute-start.9) | collective-permute-done | bytes 9248 | tf_op jit(solution)/shard_map/ppermute | solution.py:80
  40.4 2.9 %collective-permute-done.10 = bf16[4,4,288]{2,1,0:T(4,128)(2,1)S(1)} collective-permute-done((bf16[4,4,288]{2,1,0:T(4,128)(2,1)S(1)}, bf16[4,4,288]{2,1,0:T(4,128)(2,1)S(1)}, u32[]{:S(2)}, u32[]{:S(2)}) %collective-permute-start.10) | collective-permute-done | bytes 9248 | tf_op jit(solution)/shard_map/ppermute | solution.py:80
  43.3 4.0 %collective-permute-start.11 = (bf16[4,4,4,288]{3,2,1,0:T(4,128)(2,1)S(1)}, bf16[4,4,4,288]{3,2,1,0:T(4,128)(2,1)S(1)}, u32[]{:S(2)}, u32[]{:S(2)}) collective-permute-start(bf16[4,4,4,288]{3,2,1,0:T(4,128)(2,1)S(1)} %pad_maximum_fusion.4.mine_ref), channel_id=1, source_target_pairs={{0,1},{1,0},{2,3},{3,2},{4,5},{5,4},{6,7},{7,6},{8,9},{9,8},{10,11... | collective-permute-start | bytes 110600 | tf_op jit(solution)/shard_map/ppermute | solution.py:71
  47.4 0.8 collective-permute-done.11.theirs_ref
  48.2 3.4 %attend.1 = f32[4,4096]{1,0:T(4,128)S(1)} custom-call(s32[2]{0:T(128)S(1)} %pad_add_fusion.place_ref, s32[4]{0:T(128)S(1)} %copy-done.4, bf16[4,4,4,288]{3,2,1,0:T(4,128)(2,1)S(1)} %pad_maximum_fusion.4.mine_ref, bf16[4,4,4,288]{3,2,1,0:T(4,128)(2,1)S(1)} %collective-permute-done.11.theirs_ref, bf16[4,2,512,128]{3,2,1,0:T(8,128)(2,1)S(1)} %copy-done.2, ...), custom_call_target="tpu_custom_call" | custom-call | tf_op jit(solution)/shard_map/attend/pallas_call | solution.py:195
  52.0 0.9 %collective-permute-done.12 = bf16[4,4096]{1,0:T(4,128)(2,1)S(1)} collective-permute-done((bf16[4,4096]{1,0:T(4,128)(2,1)S(1)}, bf16[4,4096]{1,0:T(4,128)(2,1)S(1)}, u32[]{:S(2)}, u32[]{:S(2)}) %collective-permute-start.12) | collective-permute-done | bytes 32800 | tf_op jit(solution)/shard_map/ppermute | solution.py:71
  52.9 0.7 collective-permute-start.13
  53.6 1.2 %collective-permute-start.14 = (bf16[8,4096]{1,0:T(8,128)(2,1)S(1)}, bf16[8,4096]{1,0:T(8,128)(2,1)S(1)}, u32[]{:S(2)}, u32[]{:S(2)}) collective-permute-start(bf16[8,4096]{1,0:T(8,128)(2,1)S(1)} %pad_maximum_fusion.3), channel_id=1, source_target_pairs={{0,2},{1,11},{2,0},{3,9},{4,6},{5,15},{6,4},{7,13},{8,10},{9,3},{1... | collective-permute-start | bytes 196616 | tf_op jit(solution)/shard_map/ppermute | solution.py:80
  55.4 1.7 %collective-permute-start.16 = (bf16[8,4096]{1,0:T(8,128)(2,1)S(1)}, bf16[8,4096]{1,0:T(8,128)(2,1)S(1)}, u32[]{:S(2)}, u32[]{:S(2)}) collective-permute-start(bf16[8,4096]{1,0:T(8,128)(2,1)S(1)} %pad_maximum_fusion.3), channel_id=1, source_target_pairs={{0,6},{1,15},{2,4},{3,13},{4,2},{5,11},{6,0},{7,9},{8,14},{9,7},{1... | collective-permute-start | bytes 196616 | tf_op jit(solution)/shard_map/ppermute | solution.py:80
  57.2 0.7 collective-permute-done.14
  58.0 1.3 %collective-permute-done.15 = bf16[8,4096]{1,0:T(8,128)(2,1)S(1)} collective-permute-done((bf16[8,4096]{1,0:T(8,128)(2,1)S(1)}, bf16[8,4096]{1,0:T(8,128)(2,1)S(1)}, u32[]{:S(2)}, u32[]{:S(2)}) %collective-permute-start.15) | collective-permute-done | bytes 65568 | tf_op jit(solution)/shard_map/ppermute | solution.py:80
  59.2 2.3 %collective-permute-done.16 = bf16[8,4096]{1,0:T(8,128)(2,1)S(1)} collective-permute-done((bf16[8,4096]{1,0:T(8,128)(2,1)S(1)}, bf16[8,4096]{1,0:T(8,128)(2,1)S(1)}, u32[]{:S(2)}, u32[]{:S(2)}) %collective-permute-start.16) | collective-permute-done | bytes 65568 | tf_op jit(solution)/shard_map/ppermute | solution.py:80
  61.7 5.1 %collective-permute-start.17 = (bf16[16,4096]{1,0:T(8,128)(2,1)S(1)}, bf16[16,4096]{1,0:T(8,128)(2,1)S(1)}, u32[]{:S(2)}, u32[]{:S(2)}) collective-permute-start(bf16[16,4096]{1,0:T(8,128)(2,1)S(1)} %pad_maximum_fusion.2), channel_id=1, source_target_pairs={{0,1},{1,0},{2,3},{3,2},{4,5},{5,4},{6,7},{7,6},{8,9},{9,8},{10,11... | collective-permute-start | bytes 393224 | tf_op jit(solution)/shard_map/ppermute | solution.py:71
  66.8 1.0 %collective-permute-done.17 = bf16[16,4096]{1,0:T(8,128)(2,1)S(1)} collective-permute-done((bf16[16,4096]{1,0:T(8,128)(2,1)S(1)}, bf16[16,4096]{1,0:T(8,128)(2,1)S(1)}, u32[]{:S(2)}, u32[]{:S(2)}) %collective-permute-start.17) | collective-permute-done | bytes 131104 | tf_op jit(solution)/shard_map/ppermute | solution.py:71
  67.9 5.8 %copy-done.1 = bf16[2048,4096]{1,0:T(8,128)(2,1)S(1)} copy-done((bf16[2048,4096]{1,0:T(8,128)(2,1)S(1)}, bf16[2048,4096]{1,0:T(8,128)(2,1)}, u32[]{:S(2)}) %copy-start.1) | copy-done | bytes 16777240
  73.7 5.7 %output.1 = (bf16[16,2048]{1,0:T(8,128)(2,1)S(1)}, bf16[16,2048]{1,0:T(8,128)(2,1)S(1)}) custom-call(s32[2]{0:T(128)S(1)} %pad_add_fusion.place_ref, bf16[32,4096]{1,0:T(8,128)(2,1)S(1)} %concatenate.23.x_ref, bf16[2048,4096]{1,0:T(8,128)(2,1)S(1)} %copy-done.1), custom_call_target="tpu_custom_call" | custom-call | tf_op jit(solution)/shard_map/output/pallas_call | solution.py:211
  79.8 0.9 %collective-permute-done.18 = bf16[16,2048]{1,0:T(8,128)(2,1)S(1)} collective-permute-done((bf16[16,2048]{1,0:T(8,128)(2,1)S(1)}, bf16[16,2048]{1,0:T(8,128)(2,1)S(1)}, u32[]{:S(2)}, u32[]{:S(2)}) %collective-permute-start.18) | collective-permute-done | bytes 65568 | tf_op jit(solution)/shard_map/ppermute | solution.py:71
  (39 shorter events, 5.3 us)
Async XLA Ops:
  0.0 48.2 %copy-start.3 = (bf16[4,2,512,128]{3,2,1,0:T(8,128)(2,1)S(1)}, bf16[4,2,512,128]{3,2,1,0:T(8,128)(2,1)}, u32[]{:S(2)}) copy-start(bf16[4,2,512,128]{3,2,1,0:T(8,128)(2,1)} %value_ref.1) | copy-start | bytes 3145732
  0.0 48.2 %copy-start.4 = (s32[4]{0:T(128)S(1)}, s32[4]{0:T(128)}, u32[]{:S(2)}) copy-start(s32[4]{0:T(128)} %lengths_ref.1) | copy-start | bytes 52
  0.0 48.2 %copy-start.2 = (bf16[4,2,512,128]{3,2,1,0:T(8,128)(2,1)S(1)}, bf16[4,2,512,128]{3,2,1,0:T(8,128)(2,1)}, u32[]{:S(2)}) copy-start(bf16[4,2,512,128]{3,2,1,0:T(8,128)(2,1)} %key_ref.1) | copy-start | bytes 3145732
  0.0 1.6 %collective-permute-start = (bf16[4,8192]{1,0:T(4,128)(2,1)}, bf16[4,8192]{1,0:T(4,128)(2,1)S(1)}, u32[]{:S(2)}, u32[]{:S(2)}) collective-permute-start(bf16[4,8192]{1,0:T(4,128)(2,1)} %param.6), channel_id=1, source_target_pairs={{0,1},{1,0},{2,3},{3,2},{4,5},{5,4},{6,7},{7,6},{8,9},{9,8},{10,11... | collective-permute-start | bytes 196616 | tf_op jit(solution)/shard_map/ppermute | solution.py:71
  2.6 5.2 %collective-permute-start.1 = (bf16[8,8192]{1,0:T(8,128)(2,1)S(1)}, bf16[8,8192]{1,0:T(8,128)(2,1)S(1)}, u32[]{:S(2)}, u32[]{:S(2)}) collective-permute-start(bf16[8,8192]{1,0:T(8,128)(2,1)S(1)} %pad_maximum_fusion.1), channel_id=1, source_target_pairs={{0,0},{1,9},{2,2},{3,11},{4,4},{5,13},{6,6},{7,15},{8,8},{9,1},{10... | collective-permute-start | bytes 393224 | tf_op jit(solution)/shard_map/ppermute | solution.py:80
  3.2 5.9 %collective-permute-start.2 = (bf16[8,8192]{1,0:T(8,128)(2,1)S(1)}, bf16[8,8192]{1,0:T(8,128)(2,1)S(1)}, u32[]{:S(2)}, u32[]{:S(2)}) collective-permute-start(bf16[8,8192]{1,0:T(8,128)(2,1)S(1)} %pad_maximum_fusion.1), channel_id=1, source_target_pairs={{0,2},{1,11},{2,0},{3,9},{4,6},{5,15},{6,4},{7,13},{8,10},{9,3},{1... | collective-permute-start | bytes 393224 | tf_op jit(solution)/shard_map/ppermute | solution.py:80
  6.1 5.9 %collective-permute-start.3 = (bf16[8,8192]{1,0:T(8,128)(2,1)S(1)}, bf16[8,8192]{1,0:T(8,128)(2,1)S(1)}, u32[]{:S(2)}, u32[]{:S(2)}) collective-permute-start(bf16[8,8192]{1,0:T(8,128)(2,1)S(1)} %pad_maximum_fusion.1), channel_id=1, source_target_pairs={{0,4},{1,13},{2,6},{3,15},{4,0},{5,9},{6,2},{7,11},{8,12},{9,5},{1... | collective-permute-start | bytes 393224 | tf_op jit(solution)/shard_map/ppermute | solution.py:80
  7.7 7.1 %collective-permute-start.4 = (bf16[8,8192]{1,0:T(8,128)(2,1)S(1)}, bf16[8,8192]{1,0:T(8,128)(2,1)S(1)}, u32[]{:S(2)}, u32[]{:S(2)}) collective-permute-start(bf16[8,8192]{1,0:T(8,128)(2,1)S(1)} %pad_maximum_fusion.1), channel_id=1, source_target_pairs={{0,6},{1,15},{2,4},{3,13},{4,2},{5,11},{6,0},{7,9},{8,14},{9,7},{1... | collective-permute-start | bytes 393224 | tf_op jit(solution)/shard_map/ppermute | solution.py:80
  15.0 6.1 %collective-permute-start.5 = (bf16[16,8192]{1,0:T(8,128)(2,1)S(1)}, bf16[16,8192]{1,0:T(8,128)(2,1)S(1)}, u32[]{:S(2)}, u32[]{:S(2)}) collective-permute-start(bf16[16,8192]{1,0:T(8,128)(2,1)S(1)} %pad_maximum_fusion), channel_id=1, source_target_pairs={{0,1},{1,0},{2,3},{3,2},{4,5},{5,4},{6,7},{7,6},{8,9},{9,8},{10,11... | collective-permute-start | bytes 786440 | tf_op jit(solution)/shard_map/ppermute | solution.py:71
  21.4 6.4 %copy-start = (bf16[4,288,8192]{2,1,0:T(8,128)(2,1)S(1)}, bf16[4,288,8192]{2,1,0:T(8,128)(2,1)}, u32[]{:S(2)}) copy-start(bf16[4,288,8192]{2,1,0:T(8,128)(2,1)} %w_ref.2) | copy-start | bytes 56623108
  33.2 1.3 %collective-permute-start.6 = (bf16[4,16,288]{2,1,0:T(8,128)(2,1)S(1)}, bf16[4,16,288]{2,1,0:T(8,128)(2,1)S(1)}, u32[]{:S(2)}, u32[]{:S(2)}) collective-permute-start(bf16[4,16,288]{2,1,0:T(8,128)(2,1)S(1)} %get-tuple-element.10), channel_id=1, source_target_pairs={{0,1},{1,0},{2,3},{3,2},{4,5},{5,4},{6,7},{7,6},{8,9},{9,8},{10,11... | collective-permute-start | bytes 110600 | tf_op jit(solution)/shard_map/ppermute | solution.py:71
  34.6 4.6 %collective-permute-start.7 = (bf16[4,4,288]{2,1,0:T(4,128)(2,1)S(1)}, bf16[4,4,288]{2,1,0:T(4,128)(2,1)S(1)}, u32[]{:S(2)}, u32[]{:S(2)}) collective-permute-start(bf16[4,4,288]{2,1,0:T(4,128)(2,1)S(1)} %get-tuple-element.29), channel_id=1, source_target_pairs={{0,0},{1,9},{2,2},{3,11},{4,4},{5,13},{6,6},{7,15},{8,8},{9,1},{10... | collective-permute-start | bytes 27656 | tf_op jit(solution)/shard_map/ppermute | solution.py:80
  35.2 4.0 %collective-permute-start.8 = (bf16[4,4,288]{2,1,0:T(4,128)(2,1)S(1)}, bf16[4,4,288]{2,1,0:T(4,128)(2,1)S(1)}, u32[]{:S(2)}, u32[]{:S(2)}) collective-permute-start(bf16[4,4,288]{2,1,0:T(4,128)(2,1)S(1)} %get-tuple-element.32), channel_id=1, source_target_pairs={{0,2},{1,11},{2,0},{3,9},{4,6},{5,15},{6,4},{7,13},{8,10},{9,3},{1... | collective-permute-start | bytes 27656 | tf_op jit(solution)/shard_map/ppermute | solution.py:80
  35.9 4.4 %collective-permute-start.9 = (bf16[4,4,288]{2,1,0:T(4,128)(2,1)S(1)}, bf16[4,4,288]{2,1,0:T(4,128)(2,1)S(1)}, u32[]{:S(2)}, u32[]{:S(2)}) collective-permute-start(bf16[4,4,288]{2,1,0:T(4,128)(2,1)S(1)} %get-tuple-element.31), channel_id=1, source_target_pairs={{0,4},{1,13},{2,6},{3,15},{4,0},{5,9},{6,2},{7,11},{8,12},{9,5},{1... | collective-permute-start | bytes 27656 | tf_op jit(solution)/shard_map/ppermute | solution.py:80
  38.7 4.6 %collective-permute-start.10 = (bf16[4,4,288]{2,1,0:T(4,128)(2,1)S(1)}, bf16[4,4,288]{2,1,0:T(4,128)(2,1)S(1)}, u32[]{:S(2)}, u32[]{:S(2)}) collective-permute-start(bf16[4,4,288]{2,1,0:T(4,128)(2,1)S(1)} %get-tuple-element.30), channel_id=1, source_target_pairs={{0,6},{1,15},{2,4},{3,13},{4,2},{5,11},{6,0},{7,9},{8,14},{9,7},{1... | collective-permute-start | bytes 27656 | tf_op jit(solution)/shard_map/ppermute | solution.py:80
  43.3 4.9 %collective-permute-start.11 = (bf16[4,4,4,288]{3,2,1,0:T(4,128)(2,1)S(1)}, bf16[4,4,4,288]{3,2,1,0:T(4,128)(2,1)S(1)}, u32[]{:S(2)}, u32[]{:S(2)}) collective-permute-start(bf16[4,4,4,288]{3,2,1,0:T(4,128)(2,1)S(1)} %pad_maximum_fusion.4.mine_ref), channel_id=1, source_target_pairs={{0,1},{1,0},{2,3},{3,2},{4,5},{5,4},{6,7},{7,6},{8,9},{9,8},{10,11... | collective-permute-start | bytes 110600 | tf_op jit(solution)/shard_map/ppermute | solution.py:71
  51.6 1.3 %collective-permute-start.12 = (bf16[4,4096]{1,0:T(4,128)(2,1)S(1)}, bf16[4,4096]{1,0:T(4,128)(2,1)S(1)}, u32[]{:S(2)}, u32[]{:S(2)}) collective-permute-start(bf16[4,4096]{1,0:T(4,128)(2,1)S(1)} %convert_element_type.24), channel_id=1, source_target_pairs={{0,1},{1,0},{2,3},{3,2},{4,5},{5,4},{6,7},{7,6},{8,9},{9,8},{10,11... | collective-permute-start | bytes 98312 | tf_op jit(solution)/shard_map/ppermute | solution.py:71
  52.9 4.2 %collective-permute-start.13 = (bf16[8,4096]{1,0:T(8,128)(2,1)S(1)}, bf16[8,4096]{1,0:T(8,128)(2,1)S(1)}, u32[]{:S(2)}, u32[]{:S(2)}) collective-permute-start(bf16[8,4096]{1,0:T(8,128)(2,1)S(1)} %pad_maximum_fusion.3), channel_id=1, source_target_pairs={{0,0},{1,9},{2,2},{3,11},{4,4},{5,13},{6,6},{7,15},{8,8},{9,1},{10... | collective-permute-start | bytes 196616 | tf_op jit(solution)/shard_map/ppermute | solution.py:80
  53.6 4.3 %collective-permute-start.14 = (bf16[8,4096]{1,0:T(8,128)(2,1)S(1)}, bf16[8,4096]{1,0:T(8,128)(2,1)S(1)}, u32[]{:S(2)}, u32[]{:S(2)}) collective-permute-start(bf16[8,4096]{1,0:T(8,128)(2,1)S(1)} %pad_maximum_fusion.3), channel_id=1, source_target_pairs={{0,2},{1,11},{2,0},{3,9},{4,6},{5,15},{6,4},{7,13},{8,10},{9,3},{1... | collective-permute-start | bytes 196616 | tf_op jit(solution)/shard_map/ppermute | solution.py:80
  54.8 4.4 %collective-permute-start.15 = (bf16[8,4096]{1,0:T(8,128)(2,1)S(1)}, bf16[8,4096]{1,0:T(8,128)(2,1)S(1)}, u32[]{:S(2)}, u32[]{:S(2)}) collective-permute-start(bf16[8,4096]{1,0:T(8,128)(2,1)S(1)} %pad_maximum_fusion.3), channel_id=1, source_target_pairs={{0,4},{1,13},{2,6},{3,15},{4,0},{5,9},{6,2},{7,11},{8,12},{9,5},{1... | collective-permute-start | bytes 196616 | tf_op jit(solution)/shard_map/ppermute | solution.py:80
  55.4 6.1 %collective-permute-start.16 = (bf16[8,4096]{1,0:T(8,128)(2,1)S(1)}, bf16[8,4096]{1,0:T(8,128)(2,1)S(1)}, u32[]{:S(2)}, u32[]{:S(2)}) collective-permute-start(bf16[8,4096]{1,0:T(8,128)(2,1)S(1)} %pad_maximum_fusion.3), channel_id=1, source_target_pairs={{0,6},{1,15},{2,4},{3,13},{4,2},{5,11},{6,0},{7,9},{8,14},{9,7},{1... | collective-permute-start | bytes 196616 | tf_op jit(solution)/shard_map/ppermute | solution.py:80
  61.7 6.1 %collective-permute-start.17 = (bf16[16,4096]{1,0:T(8,128)(2,1)S(1)}, bf16[16,4096]{1,0:T(8,128)(2,1)S(1)}, u32[]{:S(2)}, u32[]{:S(2)}) collective-permute-start(bf16[16,4096]{1,0:T(8,128)(2,1)S(1)} %pad_maximum_fusion.2), channel_id=1, source_target_pairs={{0,1},{1,0},{2,3},{3,2},{4,5},{5,4},{6,7},{7,6},{8,9},{9,8},{10,11... | collective-permute-start | bytes 393224 | tf_op jit(solution)/shard_map/ppermute | solution.py:71
  67.9 5.8 %copy-start.1 = (bf16[2048,4096]{1,0:T(8,128)(2,1)S(1)}, bf16[2048,4096]{1,0:T(8,128)(2,1)}, u32[]{:S(2)}) copy-start(bf16[2048,4096]{1,0:T(8,128)(2,1)} %w_ref.3) | copy-start | bytes 50331652
  79.4 1.3 %collective-permute-start.18 = (bf16[16,2048]{1,0:T(8,128)(2,1)S(1)}, bf16[16,2048]{1,0:T(8,128)(2,1)S(1)}, u32[]{:S(2)}, u32[]{:S(2)}) collective-permute-start(bf16[16,2048]{1,0:T(8,128)(2,1)S(1)} %get-tuple-element.12), channel_id=1, source_target_pairs={{0,1},{1,0},{2,3},{3,2},{4,5},{5,4},{6,7},{7,6},{8,9},{9,8},{10,11... | collective-permute-start | bytes 196616 | tf_op jit(solution)/shard_map/ppermute | solution.py:71

commit v2 on v1

--- a/solution.py
+++ b/solution.py
@@ -71,50 +71,63 @@
     return lax.ppermute(x, "gx", [(0, 1), (1, 0)])
 
 
-def hop(x, chips, step):
-    half = chips // 2
-    pairs = []
-    for chip in range(chips):
-        for core in range(2):
-            pairs.append((2 * chip + core, 2 * (chip ^ (step + core * half)) + core))
-    return lax.ppermute(x, ("gy", "gx"), pairs)
-
-
-def gather_rows(block, chips):
-    rows = block.shape[0]
-    both = jnp.concatenate([block, swap(block)], axis=0)
-    got = [hop(both, chips, step) for step in range(chips // 2)]
-    theirs = swap(jnp.concatenate([piece[rows:] for piece in got], axis=0))
-    return jnp.concatenate([piece[:rows] for piece in got] + [theirs], axis=0)
-
-
-def project_kernel(x_ref, w_ref, keep_ref, send_ref):
-    half = keep_ref.shape[1]
-    for head in range(w_ref.shape[0]):
-        value = lax.dot_general(x_ref[...], w_ref[head], NT, preferred_element_type=jnp.float32)
-        value = value.astype(jnp.bfloat16)
-        keep_ref[head] = value[:half]
-        send_ref[head] = value[half:]
-
-
-def attend_kernel(place_ref, lengths_ref, mine_ref, theirs_ref, key_ref, value_ref, out_ref, wide, tall):
-    chips = 2 * mine_ref.shape[0]
+def hop(x, chips, mask):
+    return lax.ppermute(x, "gy", [(chip, chip ^ mask) for chip in range(chips)])
+
+
+def stage_kernel(mine_ref, out_ref):
+    out_ref[...] = mine_ref[...]
+
+
+def pair_kernel(mine_ref, theirs_ref, out_ref):
+    out_ref[...] = jnp.concatenate([mine_ref[...], theirs_ref[...]], axis=0)
+
+
+def stage(block):
+    return pl.pallas_call(
+        stage_kernel,
+        out_shape=jax.ShapeDtypeStruct(block.shape, block.dtype),
+        in_specs=in_vmem(1),
+        out_specs=in_vmem(1)[0],
+        compiler_params=pltpu.CompilerParams(vmem_limit_bytes=2 * MIB),
+        cost_estimate=pl.CostEstimate(flops=1 << 35, bytes_accessed=1 << 17, transcendentals=0),
+        name="stage",
+    )(block)
+
+
+def gather_rows(block, far, chips):
+    pair = pl.pallas_call(
+        pair_kernel,
+        out_shape=jax.ShapeDtypeStruct((2 * block.shape[0], block.shape[1]), block.dtype),
+        in_specs=in_vmem(2),
+        out_specs=in_vmem(1)[0],
+        compiler_params=pltpu.CompilerParams(vmem_limit_bytes=2 * MIB),
+        name="pair",
+    )(hold(block), hold(far))
+    return [pair] + [hop(pair, chips, mask) for mask in range(1, chips // 2)]
+
+
+def project_kernel(*refs, swapped):
+    *x_refs, w_ref, out_ref = refs
+    heads = out_ref.shape[0]
+    x = jnp.concatenate([x_ref[...] for x_ref in x_refs], axis=0)
+    core = lax.axis_index("gx")
+    first = heads * ((1 - core) if swapped else core)
+    for head in range(heads):
+        value = lax.dot_general(x, w_ref[first + head], NT, preferred_element_type=jnp.float32)
+        out_ref[head] = value.astype(jnp.bfloat16)
+
+
+def attend_kernel(lengths_ref, got_ref, key_ref, value_ref, out_ref, wide, tall, flat):
+    half = got_ref.shape[0]
     seqs, heads, slots = key_ref.shape[0], key_ref.shape[1], key_ref.shape[2]
-    part = mine_ref.shape[3]
-    chip, core = place_ref[0], place_ref[1]
-    half = chips // 2
+    part = got_ref.shape[4]
+    chip = lax.axis_index("gy")
     for head in range(heads):
-        at = core * heads + head
-        for other in range(chips):
+        for other in range(2 * half):
             mask = chip ^ other
-            step = mask & (half - 1)
-            near = (mask // half) == core
-            piece = jnp.where(
-                near,
-                mine_ref[step, at].astype(jnp.float32),
-                theirs_ref[step, at].astype(jnp.float32),
-            )
-            wide[:, other * part : (other + 1) * part] = piece
+            piece = got_ref[mask & (half - 1), mask // half, head]
+            wide[:, other * part : (other + 1) * part] = piece.astype(jnp.float32)
         for column in range(GROUP + 2):
             tall[head, :, column, :] = wide[:, column * HD : (column + 1) * HD]
     scale = HD ** (-0.5)
@@ -140,82 +153,94 @@
             mixed = mixed + own_weight * new_value
             for query_head in range(GROUP):
                 column = (head * GROUP + query_head) * HD
-                wide2 = mixed[query_head : query_head + 1]
-                out_ref[seq : seq + 1, column : column + HD] = wide2
-
-
-def output_kernel(place_ref, x_ref, w_ref, keep_ref, send_ref, *, rows):
-    total = x_ref.shape[0]
-    half = total // 2
+                flat[seq : seq + 1, column : column + HD] = mixed[query_head : query_head + 1]
+    out_ref[...] = flat[...].astype(jnp.bfloat16)
+
+
+def output_kernel(*refs, rows):
+    *x_refs, w_ref, keep_ref, send_ref = refs
+    x = jnp.concatenate([x_ref[...] for x_ref in x_refs], axis=0)
+    total = x.shape[0]
+    half = len(x_refs)
+    chip, core = lax.axis_index("gy"), lax.axis_index("gx")
     row = lax.broadcasted_iota(jnp.int32, (total, total), 0)
     column = lax.broadcasted_iota(jnp.int32, (total, total), 1)
-    order = jnp.where((row ^ (place_ref[0] * rows)) == column, 1.0, 0.0).astype(jnp.bfloat16)
-    x = jnp.dot(order, x_ref[...], preferred_element_type=jnp.float32).astype(jnp.bfloat16)
+    side, within = row // (half * rows), row % (half * rows)
+    mask = chip ^ ((core ^ side) * half + within // rows)
+    source = (mask % half) * (2 * rows) + (mask // half) * rows + within % rows
+    order = jnp.where(column == source, 1.0, 0.0).astype(jnp.bfloat16)
+    x = jnp.dot(order, x, preferred_element_type=jnp.float32).astype(jnp.bfloat16)
     value = lax.dot_general(x, w_ref[...], NT, preferred_element_type=jnp.float32)
     value = value.astype(jnp.bfloat16)
-    keep_ref[...] = value[:half]
-    send_ref[...] = value[half:]
+    keep_ref[...] = value[: half * rows]
+    send_ref[...] = value[half * rows :]
 
 
 def in_vmem(count):
     return [pl.BlockSpec(memory_space=pltpu.VMEM)] * count
 
 
-def in_smem(count):
-    return [pl.BlockSpec(memory_space=pltpu.SMEM)] * count
-
-
 def hold(x):
     return pltpu.with_memory_space_constraint(x, pltpu.VMEM)
 
 
 def local(activations, qkv_weight, out_weight, key_cache, value_cache, lengths, *, chips):
-    heads, part, _ = qkv_weight.shape
+    _, part, width = qkv_weight.shape
     seqs, kv_local, slots, _ = key_cache.shape
-    out_cols = out_weight.shape[0]
-    half = chips // 2 * seqs
-    place = jnp.stack([lax.axis_index("gy"), lax.axis_index("gx")]).astype(jnp.int32)
-
-    x = gather_rows(activations, chips)
-    piece = jax.ShapeDtypeStruct((heads, half, part), jnp.bfloat16)
-    keep, send = pl.pallas_call(
-        project_kernel,
-        out_shape=(piece, piece),
-        in_specs=in_vmem(2),
-        out_specs=tuple(in_vmem(2)),
-        compiler_params=pltpu.CompilerParams(vmem_limit_bytes=8 * MIB),
-        name="project",
-    )(hold(x), hold(qkv_weight))
-    joined = (keep.astype(jnp.float32) + swap(send).astype(jnp.float32)).astype(jnp.bfloat16)
-    got = [hop(joined[:, step * seqs : (step + 1) * seqs], chips, step) for step in range(chips // 2)]
-    mine = jnp.stack(got)
-    theirs = swap(mine)
-
-    feats = kv_local * GROUP * HD
+    out_cols, feats = out_weight.shape
+    half = chips // 2
+    rows = chips * seqs
+    limits = pltpu.CompilerParams(vmem_limit_bytes=8 * MIB)
+    qkv_weight, out_weight = hold(qkv_weight), hold(out_weight)
+    key_cache, value_cache = hold(key_cache), hold(value_cache)
+
+    pieces = [hold(piece) for piece in gather_rows(stage(activations), hop(activations, chips, half), chips)]
+
+    def project(swapped):
+        return pl.pallas_call(
+            functools.partial(project_kernel, swapped=swapped),
+            out_shape=jax.ShapeDtypeStruct((kv_local, rows, part), jnp.bfloat16),
+            in_specs=in_vmem(half + 1),
+            out_specs=in_vmem(1)[0],
+            compiler_params=limits,
+            cost_estimate=pl.CostEstimate(
+                flops=2 * kv_local * 256 * part * width, bytes_accessed=1 << 20, transcendentals=0
+            ),
+            name="project",
+        )(*pieces, qkv_weight)
+
+    arrived = swap(project(True))
+    joined = (project(False).astype(jnp.float32) + arrived.astype(jnp.float32)).astype(jnp.bfloat16)
+    joined = joined.reshape(kv_local, half, 2, seqs, part)
+    near = [joined[:, mask, 0] for mask in range(half)]
+    far = hop(jnp.stack([joined[:, mask, 1] for mask in range(half)]), chips, half)
+    got = [jnp.stack([near[mask], far[mask]]) for mask in range(half)]
+    got = [got[0]] + [hop(got[mask], chips, mask) for mask in range(1, half)]
+
     attended = pl.pallas_call(
         attend_kernel,
-        out_shape=jax.ShapeDtypeStruct((seqs, feats), jnp.float32),
-        in_specs=in_smem(2) + in_vmem(4),
+        out_shape=jax.ShapeDtypeStruct((seqs, feats), jnp.bfloat16),
+        in_specs=[pl.BlockSpec(memory_space=pltpu.SMEM)] + in_vmem(3),
         out_specs=in_vmem(1)[0],
         scratch_shapes=[
             pltpu.VMEM((seqs, chips * part), jnp.float32),
             pltpu.VMEM((kv_local, seqs, GROUP + 8, HD), jnp.float32),
+            pltpu.VMEM((seqs, feats), jnp.float32),
         ],
-        compiler_params=pltpu.CompilerParams(vmem_limit_bytes=8 * MIB),
+        compiler_params=limits,
         name="attend",
-    )(place, lengths, hold(mine), hold(theirs), hold(key_cache), hold(value_cache))
-    attended = attended.astype(jnp.bfloat16)
-
-    x = gather_rows(attended, chips)
-    piece = jax.ShapeDtypeStruct((half, out_cols), jnp.bfloat16)
+    )(lengths, hold(jnp.stack(got)), key_cache, value_cache)
+
+    pieces = [hold(piece) for piece in gather_rows(attended, hop(attended, chips, half), chips)]
+    piece = jax.ShapeDtypeStruct((rows // 2, out_cols), jnp.bfloat16)
     keep, send = pl.pallas_call(
         functools.partial(output_kernel, rows=seqs),
         out_shape=(piece, piece),
-        in_specs=in_smem(1) + in_vmem(2),
+        in_specs=in_vmem(half + 1),
         out_specs=tuple(in_vmem(2)),
-        compiler_params=pltpu.CompilerParams(vmem_limit_bytes=8 * MIB),
+        compiler_params=limits,
         name="output",
-    )(place, hold(x), hold(out_weight))
+    )(*pieces, out_weight)
     return (keep.astype(jnp.float32) + swap(send).astype(jnp.float32)).astype(jnp.bfloat16)
 
 

time: 81.6 us -> 57.1 us (0.70)
  local copies, waits for them, and re-layouts: 12.8 us -> 1.77 us
  starting transfers between devices: 29.8 us -> 20.8 us
  waiting for transfers between devices: 22.1 us -> 19.1 us
  other arithmetic: 1.98 us -> 0.8 us
    ppermute x7 -> x2, starting transfers between devices: 15.8 us -> 0.11 us  [swap(): return lax.ppermute(x, 'gx', [(0, 1), (1, 0)])]
    unnamed x10 -> x22, local copies, waits for them, and re-layouts: 12.1 us -> 1.66 us
    ppermute x12, starting transfers between devices: 14 us -> 20.7 us  [hop(): return lax.ppermute(x, 'gy', [(chip, chip ^ mask) for chip in range(chips)])]
    ppermute x7 -> x2, waiting for transfers between devices: 6.71 us -> 1.25 us  [swap(): return lax.ppermute(x, 'gx', [(0, 1), (1, 0)])]
    ppermute x12, waiting for transfers between devices: 15.3 us -> 17.9 us  [hop(): return lax.ppermute(x, 'gy', [(chip, chip ^ mask) for chip in range(chips)])]
    concatenate x4 -> x0, other arithmetic: 1.19 us -> none  [the longest x2 0.94 us: gather_rows(): both = jnp.concatenate([block, swap(block)], axis=0)]
    pallas_call x1 -> x5, Pallas kernels: 5.47 us -> 5.75 us  [the longest x2 5.68 us: project(): pl.pallas_call(functools.partial(project_kernel, swapped=swapped), out_sh...]
  transfers between devices with their start and end apart: 19 -> 14, of which waited for: 15 -> 11; matrix products, arithmetic and copies ran while one was open for 0% -> 0% of each run, Pallas kernels for 0% -> 5%
where the time goes in v2:
time: 57.1 us; the launch traced here: 57 us
  starting transfers between devices  20.8 us (36%)
  waiting for transfers between devices  19.1 us (33%)
  Pallas kernels  14.3 us (25%)
  local copies, waits for them, and re-layouts  1.77 us (3%)
  other arithmetic  0.8 us (1%)
    ppermute x12, starting transfers between devices, hop(): return lax.ppermute(x, 'gy', [(chip, chip ^ mask) for chip in range(chips)])  20.7 us
    ppermute x12, waiting for transfers between devices, hop(): return lax.ppermute(x, 'gy', [(chip, chip ^ mask) for chip in range(chips)])  17.9 us
    pallas_call x2, Pallas kernels, project(): pl.pallas_call(functools.partial(project_kernel, swapped=swapped), out_sh...  5.68 us
    pallas_call x1, Pallas kernels, local(): pl.pallas_call(functools.partial(output_kernel, rows=seqs), out_shape=(pi...  5.13 us
    pallas_call x1, Pallas kernels, local(): pl.pallas_call(attend_kernel, out_shape=jax.ShapeDtypeStruct((seqs, feats...  3.4 us
    unnamed x22, local copies, waits for them, and re-layouts  1.66 us
    ppermute x2, waiting for transfers between devices, swap(): return lax.ppermute(x, 'gx', [(0, 1), (1, 0)])  1.25 us
  transfers between devices with their start and end apart: 14, of which 11 were waited for; matrix products, arithmetic and copies ran while one was open for 0% of the time, Pallas kernels for 5%

profile of v2, /device:TPU:0, one launch (start us, length us, event | category | flops | bytes accessed | tf_op | source)
XLA Modules:
  0.0 57.0 jit_solution(2070604772279699717)
XLA Ops:
  0.0 4.0 %collective-permute-start = (bf16[4,8192]{1,0:T(4,128)(2,1)}, bf16[4,8192]{1,0:T(4,128)(2,1)S(1)}, u32[]{:S(2)}, u32[]{:S(2)}) collective-permute-start(bf16[4,8192]{1,0:T(4,128)(2,1)} %mine_ref.1), channel_id=1, source_target_pairs={{0,8},{2,10},{4,12},{6,14},{8,0},{10,2},{12,4},{14,6},{1,9},{3,11}... | collective-permute-start | bytes 196616 | tf_op jit(solution)/shard_map/ppermute | solution.py:75
  4.0 1.6 %copy-done.4 = bf16[4,8192]{1,0:T(4,128)(2,1)S(1)} copy-done((bf16[4,8192]{1,0:T(4,128)(2,1)S(1)}, bf16[4,8192]{1,0:T(4,128)(2,1)}, u32[]{:S(2)}) %copy-start.4) | copy-done | bytes 65560
  5.6 2.3 %collective-permute-done.theirs_ref = bf16[4,8192]{1,0:T(4,128)(2,1)S(1)} collective-permute-done((bf16[4,8192]{1,0:T(4,128)(2,1)}, bf16[4,8192]{1,0:T(4,128)(2,1)S(1)}, u32[]{:S(2)}, u32[]{:S(2)}) %collective-permute-start) | collective-permute-done | bytes 65568 | tf_op jit(solution)/shard_map/ppermute | solution.py:75
  8.0 1.7 %collective-permute-start.3 = (bf16[8,8192]{1,0:T(8,128)(2,1)S(1)}, bf16[8,8192]{1,0:T(8,128)(2,1)S(1)}, u32[]{:S(2)}, u32[]{:S(2)}) collective-permute-start(bf16[8,8192]{1,0:T(8,128)(2,1)S(1)} %pair.2.refs_0_), channel_id=1, source_target_pairs={{0,6},{2,4},{4,2},{6,0},{8,14},{10,12},{12,10},{14,8},{1,7},{3,5},... | collective-permute-start | bytes 393224 | tf_op jit(solution)/shard_map/ppermute | solution.py:75
  9.7 1.6 %collective-permute-start.2 = (bf16[8,8192]{1,0:T(8,128)(2,1)S(1)}, bf16[8,8192]{1,0:T(8,128)(2,1)S(1)}, u32[]{:S(2)}, u32[]{:S(2)}) collective-permute-start(bf16[8,8192]{1,0:T(8,128)(2,1)S(1)} %pair.2.refs_0_), channel_id=1, source_target_pairs={{0,4},{2,6},{4,0},{6,2},{8,12},{10,14},{12,8},{14,10},{1,5},{3,7},... | collective-permute-start | bytes 393224 | tf_op jit(solution)/shard_map/ppermute | solution.py:75
  11.2 0.3 collective-permute-start.1
  11.6 2.8 %collective-permute-done.3.refs_3_ = bf16[8,8192]{1,0:T(8,128)(2,1)S(1)} collective-permute-done((bf16[8,8192]{1,0:T(8,128)(2,1)S(1)}, bf16[8,8192]{1,0:T(8,128)(2,1)S(1)}, u32[]{:S(2)}, u32[]{:S(2)}) %collective-permute-start.3) | collective-permute-done | bytes 131104 | tf_op jit(solution)/shard_map/ppermute | solution.py:75
  14.3 1.4 %collective-permute-done.2.refs_2_ = bf16[8,8192]{1,0:T(8,128)(2,1)S(1)} collective-permute-done((bf16[8,8192]{1,0:T(8,128)(2,1)S(1)}, bf16[8,8192]{1,0:T(8,128)(2,1)S(1)}, u32[]{:S(2)}, u32[]{:S(2)}) %collective-permute-start.2) | collective-permute-done | bytes 131104 | tf_op jit(solution)/shard_map/ppermute | solution.py:75
  15.7 0.5 collective-permute-done.1.refs_1_
  16.2 2.8 %project.3 = bf16[2,32,288]{2,1,0:T(8,128)(2,1)S(1)} custom-call(bf16[8,8192]{1,0:T(8,128)(2,1)S(1)} %pair.2.refs_0_, bf16[8,8192]{1,0:T(8,128)(2,1)S(1)} %collective-permute-done.1.refs_1_, bf16[8,8192]{1,0:T(8,128)(2,1)S(1)} %collective-permute-done.2.refs_2_, bf16[8,8192]{1,0:T(8,128)(2,1)S(1)} %collective-permute-done.3.refs_3_, ...), custom_call_target="tpu_custom_call" | custom-call | flops 2415919104 | bytes 1048576 | tf_op jit(solution)/shard_map/project/pallas_call | solution.py:200
  19.1 0.1 collective-permute-start.4
  19.1 2.8 %project.2 = bf16[2,32,288]{2,1,0:T(8,128)(2,1)S(1)} custom-call(bf16[8,8192]{1,0:T(8,128)(2,1)S(1)} %pair.2.refs_0_, bf16[8,8192]{1,0:T(8,128)(2,1)S(1)} %collective-permute-done.1.refs_1_, bf16[8,8192]{1,0:T(8,128)(2,1)S(1)} %collective-permute-done.2.refs_2_, bf16[8,8192]{1,0:T(8,128)(2,1)S(1)} %collective-permute-done.3.refs_3_, ...), custom_call_target="tpu_custom_call" | custom-call | flops 2415919104 | bytes 1048576 | tf_op jit(solution)/shard_map/project/pallas_call | solution.py:200
  22.2 3.0 %collective-permute-start.5 = (bf16[4,2,4,288]{3,2,1,0:T(4,128)(2,1)S(1)}, bf16[4,2,4,288]{3,2,1,0:T(4,128)(2,1)S(1)}, u32[]{:S(2)}, u32[]{:S(2)}) collective-permute-start(bf16[4,2,4,288]{3,2,1,0:T(4,128)(2,1)S(1)} %pad_maximum_fusion.1), channel_id=1, source_target_pairs={{0,8},{2,10},{4,12},{6,14},{8,0},{10,2},{12,4},{14,6},{1,9},{3,11}... | collective-permute-start | bytes 55304 | tf_op jit(solution)/shard_map/ppermute | solution.py:75
  25.2 1.8 %collective-permute-done.5 = bf16[4,2,4,288]{3,2,1,0:T(4,128)(2,1)S(1)} collective-permute-done((bf16[4,2,4,288]{3,2,1,0:T(4,128)(2,1)S(1)}, bf16[4,2,4,288]{3,2,1,0:T(4,128)(2,1)S(1)}, u32[]{:S(2)}, u32[]{:S(2)}) %collective-permute-start.5) | collective-permute-done | bytes 18464 | tf_op jit(solution)/shard_map/ppermute | solution.py:75
  27.0 1.0 %collective-permute-start.6 = (bf16[2,2,4,288]{3,2,1,0:T(4,128)(2,1)S(1)}, bf16[2,2,4,288]{3,2,1,0:T(4,128)(2,1)S(1)}, u32[]{:S(2)}, u32[]{:S(2)}) collective-permute-start(bf16[2,2,4,288]{3,2,1,0:T(4,128)(2,1)S(1)} %pad_maximum_fusion.2), channel_id=1, source_target_pairs={{0,2},{2,0},{4,6},{6,4},{8,10},{10,8},{12,14},{14,12},{1,3},{3,1},... | collective-permute-start | bytes 27656 | tf_op jit(solution)/shard_map/ppermute | solution.py:75
  28.1 2.3 %collective-permute-start.7 = (bf16[2,2,4,288]{3,2,1,0:T(4,128)(2,1)S(1)}, bf16[2,2,4,288]{3,2,1,0:T(4,128)(2,1)S(1)}, u32[]{:S(2)}, u32[]{:S(2)}) collective-permute-start(bf16[2,2,4,288]{3,2,1,0:T(4,128)(2,1)S(1)} %pad_maximum_fusion.3), channel_id=1, source_target_pairs={{0,4},{2,6},{4,0},{6,2},{8,12},{10,14},{12,8},{14,10},{1,5},{3,7},... | collective-permute-start | bytes 27656 | tf_op jit(solution)/shard_map/ppermute | solution.py:75
  30.4 0.4 collective-permute-start.8
  30.8 0.0 collective-permute-done.6
  30.8 1.3 %collective-permute-done.7 = bf16[2,2,4,288]{3,2,1,0:T(4,128)(2,1)S(1)} collective-permute-done((bf16[2,2,4,288]{3,2,1,0:T(4,128)(2,1)S(1)}, bf16[2,2,4,288]{3,2,1,0:T(4,128)(2,1)S(1)}, u32[]{:S(2)}, u32[]{:S(2)}) %collective-permute-start.7) | collective-permute-done | bytes 9248 | tf_op jit(solution)/shard_map/ppermute | solution.py:75
  32.1 3.0 %collective-permute-done.8 = bf16[2,2,4,288]{3,2,1,0:T(4,128)(2,1)S(1)} collective-permute-done((bf16[2,2,4,288]{3,2,1,0:T(4,128)(2,1)S(1)}, bf16[2,2,4,288]{3,2,1,0:T(4,128)(2,1)S(1)}, u32[]{:S(2)}, u32[]{:S(2)}) %collective-permute-start.8) | collective-permute-done | bytes 9248 | tf_op jit(solution)/shard_map/ppermute | solution.py:75
  35.1 3.4 %attend.1.mine_ref = bf16[4,4096]{1,0:T(4,128)(2,1)S(1)} custom-call(s32[4]{0:T(128)S(1)} %copy-done.3, bf16[4,2,2,4,288]{4,3,2,1,0:T(4,128)(2,1)S(1)} %pad_maximum_fusion.got_ref, bf16[4,2,512,128]{3,2,1,0:T(8,128)(2,1)S(1)} %copy-done.1, bf16[4,2,512,128]{3,2,1,0:T(8,128)(2,1)S(1)} %copy-done.2), custom_call_target="tpu_custom_call" | custom-call | tf_op jit(solution)/shard_map/attend/pallas_call | solution.py:220
  38.6 2.9 %collective-permute-start.9 = (bf16[4,4096]{1,0:T(4,128)(2,1)S(1)}, bf16[4,4096]{1,0:T(4,128)(2,1)S(1)}, u32[]{:S(2)}, u32[]{:S(2)}) collective-permute-start(bf16[4,4096]{1,0:T(4,128)(2,1)S(1)} %attend.1.mine_ref), channel_id=1, source_target_pairs={{0,8},{2,10},{4,12},{6,14},{8,0},{10,2},{12,4},{14,6},{1,9},{3,11}... | collective-permute-start | bytes 98312 | tf_op jit(solution)/shard_map/ppermute | solution.py:75
  41.5 2.0 %collective-permute-done.9.theirs_ref = bf16[4,4096]{1,0:T(4,128)(2,1)S(1)} collective-permute-done((bf16[4,4096]{1,0:T(4,128)(2,1)S(1)}, bf16[4,4096]{1,0:T(4,128)(2,1)S(1)}, u32[]{:S(2)}, u32[]{:S(2)}) %collective-permute-start.9) | collective-permute-done | bytes 32800 | tf_op jit(solution)/shard_map/ppermute | solution.py:75
  43.5 0.3 collective-permute-start.12
  43.8 1.8 %collective-permute-start.11 = (bf16[8,4096]{1,0:T(8,128)(2,1)S(1)}, bf16[8,4096]{1,0:T(8,128)(2,1)S(1)}, u32[]{:S(2)}, u32[]{:S(2)}) collective-permute-start(bf16[8,4096]{1,0:T(8,128)(2,1)S(1)} %pair.3.refs_0_), channel_id=1, source_target_pairs={{0,4},{2,6},{4,0},{6,2},{8,12},{10,14},{12,8},{14,10},{1,5},{3,7},... | collective-permute-start | bytes 196616 | tf_op jit(solution)/shard_map/ppermute | solution.py:75
  45.6 1.4 %collective-permute-start.10 = (bf16[8,4096]{1,0:T(8,128)(2,1)S(1)}, bf16[8,4096]{1,0:T(8,128)(2,1)S(1)}, u32[]{:S(2)}, u32[]{:S(2)}) collective-permute-start(bf16[8,4096]{1,0:T(8,128)(2,1)S(1)} %pair.3.refs_0_), channel_id=1, source_target_pairs={{0,2},{2,0},{4,6},{6,4},{8,10},{10,8},{12,14},{14,12},{1,3},{3,1},... | collective-permute-start | bytes 196616 | tf_op jit(solution)/shard_map/ppermute | solution.py:75
  47.0 1.7 %collective-permute-done.12.refs_3_ = bf16[8,4096]{1,0:T(8,128)(2,1)S(1)} collective-permute-done((bf16[8,4096]{1,0:T(8,128)(2,1)S(1)}, bf16[8,4096]{1,0:T(8,128)(2,1)S(1)}, u32[]{:S(2)}, u32[]{:S(2)}) %collective-permute-start.12) | collective-permute-done | bytes 65568 | tf_op jit(solution)/shard_map/ppermute | solution.py:75
  48.7 1.2 %collective-permute-done.10.refs_1_ = bf16[8,4096]{1,0:T(8,128)(2,1)S(1)} collective-permute-done((bf16[8,4096]{1,0:T(8,128)(2,1)S(1)}, bf16[8,4096]{1,0:T(8,128)(2,1)S(1)}, u32[]{:S(2)}, u32[]{:S(2)}) %collective-permute-start.10) | collective-permute-done | bytes 65568 | tf_op jit(solution)/shard_map/ppermute | solution.py:75
  49.9 5.1 %output.1 = (bf16[16,2048]{1,0:T(8,128)(2,1)S(1)}, bf16[16,2048]{1,0:T(8,128)(2,1)S(1)}) custom-call(bf16[8,4096]{1,0:T(8,128)(2,1)S(1)} %pair.3.refs_0_, bf16[8,4096]{1,0:T(8,128)(2,1)S(1)} %collective-permute-done.10.refs_1_, bf16[8,4096]{1,0:T(8,128)(2,1)S(1)} %collective-permute-done.11.refs_2_, bf16[8,4096]{1,0:T(8,128)(2,1)S(1)} %collective-permute-done.12.refs_3_, ...), custom_call_target="tpu_custom_call" | custom-call | tf_op jit(solution)/shard_map/output/pallas_call | solution.py:236
  55.1 0.0 collective-permute-start.13
  55.1 1.2 %collective-permute-done.13 = bf16[16,2048]{1,0:T(8,128)(2,1)S(1)} collective-permute-done((bf16[16,2048]{1,0:T(8,128)(2,1)S(1)}, bf16[16,2048]{1,0:T(8,128)(2,1)S(1)}, u32[]{:S(2)}, u32[]{:S(2)}) %collective-permute-start.13) | collective-permute-done | bytes 65568 | tf_op jit(solution)/shard_map/ppermute | solution.py:71
  56.3 0.6 %add_convert_fusion = bf16[16,2048]{1,0:T(8,128)(2,1)} fusion(bf16[16,2048]{1,0:T(8,128)(2,1)S(1)} %collective-permute-done.13, bf16[16,2048]{1,0:T(8,128)(2,1)S(1)} %get-tuple-element.7), kind=kLoop, calls=%fused_computation | loop fusion | flops 131072 | bytes 196608 | tf_op jit(solution)/shard_map/convert_element_type | solution.py:244
  (39 shorter events, 0.4 us)
Async XLA Ops:
  0.0 16.2 %copy-start = (bf16[4,288,8192]{2,1,0:T(8,128)(2,1)S(1)}, bf16[4,288,8192]{2,1,0:T(8,128)(2,1)}, u32[]{:S(2)}) copy-start(bf16[4,288,8192]{2,1,0:T(8,128)(2,1)} %refs_4_.4) | copy-start | bytes 56623108
  0.0 7.9 %collective-permute-start = (bf16[4,8192]{1,0:T(4,128)(2,1)}, bf16[4,8192]{1,0:T(4,128)(2,1)S(1)}, u32[]{:S(2)}, u32[]{:S(2)}) collective-permute-start(bf16[4,8192]{1,0:T(4,128)(2,1)} %mine_ref.1), channel_id=1, source_target_pairs={{0,8},{2,10},{4,12},{6,14},{8,0},{10,2},{12,4},{14,6},{1,9},{3,11}... | collective-permute-start | bytes 196616 | tf_op jit(solution)/shard_map/ppermute | solution.py:75
  4.0 1.6 %copy-start.4 = (bf16[4,8192]{1,0:T(4,128)(2,1)S(1)}, bf16[4,8192]{1,0:T(4,128)(2,1)}, u32[]{:S(2)}) copy-start(bf16[4,8192]{1,0:T(4,128)(2,1)} %mine_ref.1) | copy-start | bytes 196612
  7.9 27.2 %copy-start.1 = (bf16[4,2,512,128]{3,2,1,0:T(8,128)(2,1)S(1)}, bf16[4,2,512,128]{3,2,1,0:T(8,128)(2,1)}, u32[]{:S(2)}) copy-start(bf16[4,2,512,128]{3,2,1,0:T(8,128)(2,1)} %key_ref.1) | copy-start | bytes 3145732
  8.0 27.2 %copy-start.2 = (bf16[4,2,512,128]{3,2,1,0:T(8,128)(2,1)S(1)}, bf16[4,2,512,128]{3,2,1,0:T(8,128)(2,1)}, u32[]{:S(2)}) copy-start(bf16[4,2,512,128]{3,2,1,0:T(8,128)(2,1)} %value_ref.1) | copy-start | bytes 3145732
  8.0 27.2 %copy-start.3 = (s32[4]{0:T(128)S(1)}, s32[4]{0:T(128)}, u32[]{:S(2)}) copy-start(s32[4]{0:T(128)} %lengths_ref.1) | copy-start | bytes 52
  8.0 41.9 %slice-start = ((s8[16777216]{0:T(1024)(128)(4,1)}), s8[4194304]{0:T(1024)(128)(4,1)S(1)}, s32[]{:S(2)}) async-start(s8[16777216]{0:T(1024)(128)(4,1)} %bitcast.26), calls=%async_computation | async-start | bytes 8388608
  8.0 41.9 %slice-start.1 = ((s8[16777216]{0:T(1024)(128)(4,1)}), s8[4194304]{0:T(1024)(128)(4,1)S(1)}, s32[]{:S(2)}) async-start(s8[16777216]{0:T(1024)(128)(4,1)} %bitcast.26), calls=%async_computation.1 | async-start | bytes 8388608
  8.0 6.3 %collective-permute-start.3 = (bf16[8,8192]{1,0:T(8,128)(2,1)S(1)}, bf16[8,8192]{1,0:T(8,128)(2,1)S(1)}, u32[]{:S(2)}, u32[]{:S(2)}) collective-permute-start(bf16[8,8192]{1,0:T(8,128)(2,1)S(1)} %pair.2.refs_0_), channel_id=1, source_target_pairs={{0,6},{2,4},{4,2},{6,0},{8,14},{10,12},{12,10},{14,8},{1,7},{3,5},... | collective-permute-start | bytes 393224 | tf_op jit(solution)/shard_map/ppermute | solution.py:75
  9.7 6.1 %collective-permute-start.2 = (bf16[8,8192]{1,0:T(8,128)(2,1)S(1)}, bf16[8,8192]{1,0:T(8,128)(2,1)S(1)}, u32[]{:S(2)}, u32[]{:S(2)}) collective-permute-start(bf16[8,8192]{1,0:T(8,128)(2,1)S(1)} %pair.2.refs_0_), channel_id=1, source_target_pairs={{0,4},{2,6},{4,0},{6,2},{8,12},{10,14},{12,8},{14,10},{1,5},{3,7},... | collective-permute-start | bytes 393224 | tf_op jit(solution)/shard_map/ppermute | solution.py:75
  11.2 5.0 %collective-permute-start.1 = (bf16[8,8192]{1,0:T(8,128)(2,1)S(1)}, bf16[8,8192]{1,0:T(8,128)(2,1)S(1)}, u32[]{:S(2)}, u32[]{:S(2)}) collective-permute-start(bf16[8,8192]{1,0:T(8,128)(2,1)S(1)} %pair.2.refs_0_), channel_id=1, source_target_pairs={{0,2},{2,0},{4,6},{6,4},{8,10},{10,8},{12,14},{14,12},{1,3},{3,1},... | collective-permute-start | bytes 393224 | tf_op jit(solution)/shard_map/ppermute | solution.py:75
  19.0 30.9 %slice-start.2 = ((s8[16777216]{0:T(1024)(128)(4,1)}), s8[4194304]{0:T(1024)(128)(4,1)S(1)}, s32[]{:S(2)}) async-start(s8[16777216]{0:T(1024)(128)(4,1)} %bitcast.26), calls=%async_computation.2 | async-start | bytes 8388608
  19.1 30.9 %slice-start.3 = ((s8[16777216]{0:T(1024)(128)(4,1)}), s8[4194304]{0:T(1024)(128)(4,1)S(1)}, s32[]{:S(2)}) async-start(s8[16777216]{0:T(1024)(128)(4,1)} %bitcast.26), calls=%async_computation.3 | async-start | bytes 8388608
  19.1 2.9 %collective-permute-start.4 = (bf16[2,32,288]{2,1,0:T(8,128)(2,1)S(1)}, bf16[2,32,288]{2,1,0:T(8,128)(2,1)S(1)}, u32[]{:S(2)}, u32[]{:S(2)}) collective-permute-start(bf16[2,32,288]{2,1,0:T(8,128)(2,1)S(1)} %project.3), channel_id=1, source_target_pairs={{0,1},{1,0},{2,3},{3,2},{4,5},{5,4},{6,7},{7,6},{8,9},{9,8},{10,11... | collective-permute-start | bytes 110600 | tf_op jit(solution)/shard_map/ppermute | solution.py:71
  22.2 4.8 %collective-permute-start.5 = (bf16[4,2,4,288]{3,2,1,0:T(4,128)(2,1)S(1)}, bf16[4,2,4,288]{3,2,1,0:T(4,128)(2,1)S(1)}, u32[]{:S(2)}, u32[]{:S(2)}) collective-permute-start(bf16[4,2,4,288]{3,2,1,0:T(4,128)(2,1)S(1)} %pad_maximum_fusion.1), channel_id=1, source_target_pairs={{0,8},{2,10},{4,12},{6,14},{8,0},{10,2},{12,4},{14,6},{1,9},{3,11}... | collective-permute-start | bytes 55304 | tf_op jit(solution)/shard_map/ppermute | solution.py:75
  27.0 3.8 %collective-permute-start.6 = (bf16[2,2,4,288]{3,2,1,0:T(4,128)(2,1)S(1)}, bf16[2,2,4,288]{3,2,1,0:T(4,128)(2,1)S(1)}, u32[]{:S(2)}, u32[]{:S(2)}) collective-permute-start(bf16[2,2,4,288]{3,2,1,0:T(4,128)(2,1)S(1)} %pad_maximum_fusion.2), channel_id=1, source_target_pairs={{0,2},{2,0},{4,6},{6,4},{8,10},{10,8},{12,14},{14,12},{1,3},{3,1},... | collective-permute-start | bytes 27656 | tf_op jit(solution)/shard_map/ppermute | solution.py:75
  28.1 4.0 %collective-permute-start.7 = (bf16[2,2,4,288]{3,2,1,0:T(4,128)(2,1)S(1)}, bf16[2,2,4,288]{3,2,1,0:T(4,128)(2,1)S(1)}, u32[]{:S(2)}, u32[]{:S(2)}) collective-permute-start(bf16[2,2,4,288]{3,2,1,0:T(4,128)(2,1)S(1)} %pad_maximum_fusion.3), channel_id=1, source_target_pairs={{0,4},{2,6},{4,0},{6,2},{8,12},{10,14},{12,8},{14,10},{1,5},{3,7},... | collective-permute-start | bytes 27656 | tf_op jit(solution)/shard_map/ppermute | solution.py:75
  30.4 4.7 %collective-permute-start.8 = (bf16[2,2,4,288]{3,2,1,0:T(4,128)(2,1)S(1)}, bf16[2,2,4,288]{3,2,1,0:T(4,128)(2,1)S(1)}, u32[]{:S(2)}, u32[]{:S(2)}) collective-permute-start(bf16[2,2,4,288]{3,2,1,0:T(4,128)(2,1)S(1)} %pad_maximum_fusion.4), channel_id=1, source_target_pairs={{0,6},{2,4},{4,2},{6,0},{8,14},{10,12},{12,10},{14,8},{1,7},{3,5},... | collective-permute-start | bytes 27656 | tf_op jit(solution)/shard_map/ppermute | solution.py:75
  38.6 4.9 %collective-permute-start.9 = (bf16[4,4096]{1,0:T(4,128)(2,1)S(1)}, bf16[4,4096]{1,0:T(4,128)(2,1)S(1)}, u32[]{:S(2)}, u32[]{:S(2)}) collective-permute-start(bf16[4,4096]{1,0:T(4,128)(2,1)S(1)} %attend.1.mine_ref), channel_id=1, source_target_pairs={{0,8},{2,10},{4,12},{6,14},{8,0},{10,2},{12,4},{14,6},{1,9},{3,11}... | collective-permute-start | bytes 98312 | tf_op jit(solution)/shard_map/ppermute | solution.py:75
  43.5 5.2 %collective-permute-start.12 = (bf16[8,4096]{1,0:T(8,128)(2,1)S(1)}, bf16[8,4096]{1,0:T(8,128)(2,1)S(1)}, u32[]{:S(2)}, u32[]{:S(2)}) collective-permute-start(bf16[8,4096]{1,0:T(8,128)(2,1)S(1)} %pair.3.refs_0_), channel_id=1, source_target_pairs={{0,6},{2,4},{4,2},{6,0},{8,14},{10,12},{12,10},{14,8},{1,7},{3,5},... | collective-permute-start | bytes 196616 | tf_op jit(solution)/shard_map/ppermute | solution.py:75
  43.8 4.9 %collective-permute-start.11 = (bf16[8,4096]{1,0:T(8,128)(2,1)S(1)}, bf16[8,4096]{1,0:T(8,128)(2,1)S(1)}, u32[]{:S(2)}, u32[]{:S(2)}) collective-permute-start(bf16[8,4096]{1,0:T(8,128)(2,1)S(1)} %pair.3.refs_0_), channel_id=1, source_target_pairs={{0,4},{2,6},{4,0},{6,2},{8,12},{10,14},{12,8},{14,10},{1,5},{3,7},... | collective-permute-start | bytes 196616 | tf_op jit(solution)/shard_map/ppermute | solution.py:75
  45.6 4.3 %collective-permute-start.10 = (bf16[8,4096]{1,0:T(8,128)(2,1)S(1)}, bf16[8,4096]{1,0:T(8,128)(2,1)S(1)}, u32[]{:S(2)}, u32[]{:S(2)}) collective-permute-start(bf16[8,4096]{1,0:T(8,128)(2,1)S(1)} %pair.3.refs_0_), channel_id=1, source_target_pairs={{0,2},{2,0},{4,6},{6,4},{8,10},{10,8},{12,14},{14,12},{1,3},{3,1},... | collective-permute-start | bytes 196616 | tf_op jit(solution)/shard_map/ppermute | solution.py:75
  55.1 1.3 %collective-permute-start.13 = (bf16[16,2048]{1,0:T(8,128)(2,1)S(1)}, bf16[16,2048]{1,0:T(8,128)(2,1)S(1)}, u32[]{:S(2)}, u32[]{:S(2)}) collective-permute-start(bf16[16,2048]{1,0:T(8,128)(2,1)S(1)} %get-tuple-element.8), channel_id=1, source_target_pairs={{0,1},{1,0},{2,3},{3,2},{4,5},{5,4},{6,7},{7,6},{8,9},{9,8},{10,11... | collective-permute-start | bytes 196616 | tf_op jit(solution)/shard_map/ppermute | solution.py:71

commit v3 on v2

--- a/solution.py
+++ b/solution.py
@@ -118,42 +118,57 @@
         out_ref[head] = value.astype(jnp.bfloat16)
 
 
-def attend_kernel(lengths_ref, got_ref, key_ref, value_ref, out_ref, wide, tall, flat):
-    half = got_ref.shape[0]
+def merge_kernel(near_ref, far_ref, *out_refs):
+    for mask, out_ref in enumerate(reversed(out_refs)):
+        out_ref[0] = near_ref[mask]
+        out_ref[1] = far_ref[mask]
+
+
+def attend_kernel(lengths_ref, *refs):
+    *got_refs, key_ref, value_ref, out_ref, got, wide, tall, flat = refs
+    half = len(got_refs)
     seqs, heads, slots = key_ref.shape[0], key_ref.shape[1], key_ref.shape[2]
-    part = got_ref.shape[4]
+    part = got.shape[4]
     chip = lax.axis_index("gy")
-    for head in range(heads):
-        for other in range(2 * half):
-            mask = chip ^ other
-            piece = got_ref[mask & (half - 1), mask // half, head]
-            wide[:, other * part : (other + 1) * part] = piece.astype(jnp.float32)
-        for column in range(GROUP + 2):
-            tall[head, :, column, :] = wide[:, column * HD : (column + 1) * HD]
+    for mask, got_ref in enumerate(reversed(got_refs)):
+        got[mask] = got_ref[...]
+    for other in range(2 * half):
+        mask = chip ^ other
+        piece = got[mask & (half - 1), mask // half]
+        wide[:, :, other * part : (other + 1) * part] = piece.astype(jnp.float32)
+    for column in range(GROUP + 2):
+        for head in range(heads):
+            tall[:, head, column, :] = wide[head, :, column * HD : (column + 1) * HD]
     scale = HD ** (-0.5)
+    pairs = [(seq, head) for seq in range(seqs) for head in range(heads)]
     position = lax.broadcasted_iota(jnp.int32, (GROUP, slots), 1)
-    for seq in range(seqs):
-        live = position < lengths_ref[seq]
-        for head in range(heads):
-            query = tall[head, seq, :GROUP, :]
-            new_key = tall[head, seq, GROUP : GROUP + 1, :]
-            new_value = tall[head, seq, GROUP + 1 : GROUP + 2, :]
-            own = jnp.sum(query * new_key, axis=1, keepdims=True) * scale
-            scores = lax.dot_general(
+    queries, own, scores, live = [], [], [], []
+    for seq, head in pairs:
+        query = tall[seq, head, :GROUP, :]
+        new_key = tall[seq, head, GROUP : GROUP + 1, :]
+        own.append(jnp.sum(query * new_key, axis=1, keepdims=True))
+        scores.append(
+            lax.dot_general(
                 query.astype(jnp.bfloat16), key_ref[seq, head], NT, preferred_element_type=jnp.float32
             )
-            scores = jnp.where(live, scores * scale, NEG_FILL)
-            top = jnp.maximum(jnp.max(scores, axis=1, keepdims=True), own)
-            weights = jnp.where(live, jnp.exp(scores - top), 0.0)
-            own_weight = jnp.exp(own - top)
-            denom = jnp.sum(weights, axis=1, keepdims=True) + own_weight
-            weights = (weights / denom).astype(jnp.bfloat16)
-            own_weight = (own_weight / denom).astype(jnp.bfloat16).astype(jnp.float32)
-            mixed = jnp.dot(weights, value_ref[seq, head], preferred_element_type=jnp.float32)
-            mixed = mixed + own_weight * new_value
-            for query_head in range(GROUP):
-                column = (head * GROUP + query_head) * HD
-                flat[seq : seq + 1, column : column + HD] = mixed[query_head : query_head + 1]
+        )
+        live.append(jnp.where(position < lengths_ref[seq], 1.0, 0.0))
+    live = jnp.concatenate(live, axis=0) > 0.5
+    own = jnp.concatenate(own, axis=0) * scale
+    scores = jnp.where(live, jnp.concatenate(scores, axis=0) * scale, NEG_FILL)
+    top = jnp.maximum(jnp.max(scores, axis=1, keepdims=True), own)
+    weights = jnp.where(live, jnp.exp(scores - top), 0.0)
+    own_weight = jnp.exp(own - top)
+    share = 1.0 / (jnp.sum(weights, axis=1, keepdims=True) + own_weight)
+    weights = (weights * share).astype(jnp.bfloat16)
+    own_weight = (own_weight * share).astype(jnp.bfloat16).astype(jnp.float32)
+    for at, (seq, head) in enumerate(pairs):
+        rows = slice(at * GROUP, (at + 1) * GROUP)
+        mixed = jnp.dot(weights[rows], value_ref[seq, head], preferred_element_type=jnp.float32)
+        mixed = mixed + own_weight[rows] * tall[seq, head, GROUP + 1 : GROUP + 2, :]
+        for query_head in range(GROUP):
+            column = (head * GROUP + query_head) * HD
+            flat[seq : seq + 1, column : column + HD] = mixed[query_head : query_head + 1]
     out_ref[...] = flat[...].astype(jnp.bfloat16)
 
 
@@ -212,24 +227,32 @@
     arrived = swap(project(True))
     joined = (project(False).astype(jnp.float32) + arrived.astype(jnp.float32)).astype(jnp.bfloat16)
     joined = joined.reshape(kv_local, half, 2, seqs, part)
-    near = [joined[:, mask, 0] for mask in range(half)]
+    near = jnp.stack([joined[:, mask, 0] for mask in range(half)])
     far = hop(jnp.stack([joined[:, mask, 1] for mask in range(half)]), chips, half)
-    got = [jnp.stack([near[mask], far[mask]]) for mask in range(half)]
-    got = [got[0]] + [hop(got[mask], chips, mask) for mask in range(1, half)]
+    *far_first, mine = pl.pallas_call(
+        merge_kernel,
+        out_shape=(jax.ShapeDtypeStruct((2, kv_local, seqs, part), jnp.bfloat16),) * half,
+        in_specs=in_vmem(2),
+        out_specs=tuple(in_vmem(half)),
+        compiler_params=pltpu.CompilerParams(vmem_limit_bytes=2 * MIB),
+        name="merge",
+    )(hold(near), hold(far))
+    got = [hop(piece, chips, half - 1 - at) for at, piece in enumerate(far_first)] + [mine]
 
     attended = pl.pallas_call(
         attend_kernel,
         out_shape=jax.ShapeDtypeStruct((seqs, feats), jnp.bfloat16),
-        in_specs=[pl.BlockSpec(memory_space=pltpu.SMEM)] + in_vmem(3),
+        in_specs=[pl.BlockSpec(memory_space=pltpu.SMEM)] + in_vmem(half + 2),
         out_specs=in_vmem(1)[0],
         scratch_shapes=[
-            pltpu.VMEM((seqs, chips * part), jnp.float32),
-            pltpu.VMEM((kv_local, seqs, GROUP + 8, HD), jnp.float32),
+            pltpu.VMEM((half, 2, kv_local, seqs, part), jnp.bfloat16),
+            pltpu.VMEM((kv_local, seqs, chips * part), jnp.float32),
+            pltpu.VMEM((seqs, kv_local, GROUP + 8, HD), jnp.float32),
             pltpu.VMEM((seqs, feats), jnp.float32),
         ],
         compiler_params=limits,
         name="attend",
-    )(lengths, hold(jnp.stack(got)), key_cache, value_cache)
+    )(lengths, *[hold(piece) for piece in got], key_cache, value_cache)
 
     pieces = [hold(piece) for piece in gather_rows(attended, hop(attended, chips, half), chips)]
     piece = jax.ShapeDtypeStruct((rows // 2, out_cols), jnp.bfloat16)

time: 57.1 us -> 53.7 us (0.940)
  Pallas kernels: 14.3 us -> 12.4 us
  waiting for transfers between devices: 19.1 us -> 17.9 us
    pallas_call x1, Pallas kernels: 3.4 us -> 1.52 us  [local(): pl.pallas_call(attend_kernel, out_shape=jax.ShapeDtypeStruct((seqs, feats...]
    ppermute x12, waiting for transfers between devices: 17.9 us -> 16.6 us  [hop(): return lax.ppermute(x, 'gy', [(chip, chip ^ mask) for chip in range(chips)])]
    unnamed x22 -> x18, local copies, waits for them, and re-layouts: 1.66 us -> 1.64 us
  transfers between devices with their start and end apart: 14 -> 14, of which waited for: 11 -> 12; matrix products, arithmetic and copies ran while one was open for 0% -> 0% of each run, Pallas kernels for 5% -> 5%
where the time goes in v3:
time: 53.7 us; the launch traced here: 53.6 us
  starting transfers between devices  20.7 us (39%)
  waiting for transfers between devices  17.9 us (33%)
  Pallas kernels  12.4 us (23%)
  local copies, waits for them, and re-layouts  1.75 us (3%)
  other arithmetic  0.72 us (1%)
    ppermute x12, starting transfers between devices, hop(): return lax.ppermute(x, 'gy', [(chip, chip ^ mask) for chip in range(chips)])  20.6 us
    ppermute x12, waiting for transfers between devices, hop(): return lax.ppermute(x, 'gy', [(chip, chip ^ mask) for chip in range(chips)])  16.6 us
    pallas_call x2, Pallas kernels, project(): pl.pallas_call(functools.partial(project_kernel, swapped=swapped), out_sh...  5.68 us
    pallas_call x1, Pallas kernels, local(): pl.pallas_call(functools.partial(output_kernel, rows=seqs), out_shape=(pi...  5.13 us
    unnamed x18, local copies, waits for them, and re-layouts  1.64 us
    pallas_call x1, Pallas kernels, local(): pl.pallas_call(attend_kernel, out_shape=jax.ShapeDtypeStruct((seqs, feats...  1.52 us
    ppermute x2, waiting for transfers between devices, swap(): return lax.ppermute(x, 'gx', [(0, 1), (1, 0)])  1.25 us
  transfers between devices with their start and end apart: 14, of which 12 were waited for; matrix products, arithmetic and copies ran while one was open for 0% of the time, Pallas kernels for 5%

profile of v3, /device:TPU:0, one launch (start us, length us, event | category | flops | bytes accessed | tf_op | source)
XLA Modules:
  0.0 53.6 jit_solution(3914652278205689605)
XLA Ops:
  0.0 4.0 %collective-permute-start = (bf16[4,8192]{1,0:T(4,128)(2,1)}, bf16[4,8192]{1,0:T(4,128)(2,1)S(1)}, u32[]{:S(2)}, u32[]{:S(2)}) collective-permute-start(bf16[4,8192]{1,0:T(4,128)(2,1)} %mine_ref.1), channel_id=1, source_target_pairs={{0,8},{2,10},{4,12},{6,14},{8,0},{10,2},{12,4},{14,6},{1,9},{3,11}... | collective-permute-start | bytes 196616 | tf_op jit(solution)/shard_map/ppermute | solution.py:75
  4.0 1.6 %copy-done.4 = bf16[4,8192]{1,0:T(4,128)(2,1)S(1)} copy-done((bf16[4,8192]{1,0:T(4,128)(2,1)S(1)}, bf16[4,8192]{1,0:T(4,128)(2,1)}, u32[]{:S(2)}) %copy-start.4) | copy-done | bytes 65560
  5.6 2.3 %collective-permute-done.theirs_ref = bf16[4,8192]{1,0:T(4,128)(2,1)S(1)} collective-permute-done((bf16[4,8192]{1,0:T(4,128)(2,1)}, bf16[4,8192]{1,0:T(4,128)(2,1)S(1)}, u32[]{:S(2)}, u32[]{:S(2)}) %collective-permute-start) | collective-permute-done | bytes 65568 | tf_op jit(solution)/shard_map/ppermute | solution.py:75
  8.0 1.7 %collective-permute-start.3 = (bf16[8,8192]{1,0:T(8,128)(2,1)S(1)}, bf16[8,8192]{1,0:T(8,128)(2,1)S(1)}, u32[]{:S(2)}, u32[]{:S(2)}) collective-permute-start(bf16[8,8192]{1,0:T(8,128)(2,1)S(1)} %pair.2.refs_0_), channel_id=1, source_target_pairs={{0,6},{2,4},{4,2},{6,0},{8,14},{10,12},{12,10},{14,8},{1,7},{3,5},... | collective-permute-start | bytes 393224 | tf_op jit(solution)/shard_map/ppermute | solution.py:75
  9.7 1.6 %collective-permute-start.2 = (bf16[8,8192]{1,0:T(8,128)(2,1)S(1)}, bf16[8,8192]{1,0:T(8,128)(2,1)S(1)}, u32[]{:S(2)}, u32[]{:S(2)}) collective-permute-start(bf16[8,8192]{1,0:T(8,128)(2,1)S(1)} %pair.2.refs_0_), channel_id=1, source_target_pairs={{0,4},{2,6},{4,0},{6,2},{8,12},{10,14},{12,8},{14,10},{1,5},{3,7},... | collective-permute-start | bytes 393224 | tf_op jit(solution)/shard_map/ppermute | solution.py:75
  11.2 0.3 collective-permute-start.1
  11.6 2.8 %collective-permute-done.3.refs_3_ = bf16[8,8192]{1,0:T(8,128)(2,1)S(1)} collective-permute-done((bf16[8,8192]{1,0:T(8,128)(2,1)S(1)}, bf16[8,8192]{1,0:T(8,128)(2,1)S(1)}, u32[]{:S(2)}, u32[]{:S(2)}) %collective-permute-start.3) | collective-permute-done | bytes 131104 | tf_op jit(solution)/shard_map/ppermute | solution.py:75
  14.3 1.4 %collective-permute-done.2.refs_2_ = bf16[8,8192]{1,0:T(8,128)(2,1)S(1)} collective-permute-done((bf16[8,8192]{1,0:T(8,128)(2,1)S(1)}, bf16[8,8192]{1,0:T(8,128)(2,1)S(1)}, u32[]{:S(2)}, u32[]{:S(2)}) %collective-permute-start.2) | collective-permute-done | bytes 131104 | tf_op jit(solution)/shard_map/ppermute | solution.py:75
  15.7 0.5 collective-permute-done.1.refs_1_
  16.2 2.8 %project.3 = bf16[2,32,288]{2,1,0:T(8,128)(2,1)S(1)} custom-call(bf16[8,8192]{1,0:T(8,128)(2,1)S(1)} %pair.2.refs_0_, bf16[8,8192]{1,0:T(8,128)(2,1)S(1)} %collective-permute-done.1.refs_1_, bf16[8,8192]{1,0:T(8,128)(2,1)S(1)} %collective-permute-done.2.refs_2_, bf16[8,8192]{1,0:T(8,128)(2,1)S(1)} %collective-permute-done.3.refs_3_, ...), custom_call_target="tpu_custom_call" | custom-call | flops 2415919104 | bytes 1048576 | tf_op jit(solution)/shard_map/project/pallas_call | solution.py:215
  19.1 0.1 collective-permute-start.4
  19.1 2.8 %project.2 = bf16[2,32,288]{2,1,0:T(8,128)(2,1)S(1)} custom-call(bf16[8,8192]{1,0:T(8,128)(2,1)S(1)} %pair.2.refs_0_, bf16[8,8192]{1,0:T(8,128)(2,1)S(1)} %collective-permute-done.1.refs_1_, bf16[8,8192]{1,0:T(8,128)(2,1)S(1)} %collective-permute-done.2.refs_2_, bf16[8,8192]{1,0:T(8,128)(2,1)S(1)} %collective-permute-done.3.refs_3_, ...), custom_call_target="tpu_custom_call" | custom-call | flops 2415919104 | bytes 1048576 | tf_op jit(solution)/shard_map/project/pallas_call | solution.py:215
  22.0 0.0 collective-permute-done.4
  22.2 3.0 %collective-permute-start.5 = (bf16[4,2,4,288]{3,2,1,0:T(4,128)(2,1)S(1)}, bf16[4,2,4,288]{3,2,1,0:T(4,128)(2,1)S(1)}, u32[]{:S(2)}, u32[]{:S(2)}) collective-permute-start(bf16[4,2,4,288]{3,2,1,0:T(4,128)(2,1)S(1)} %pad_maximum_fusion.1), channel_id=1, source_target_pairs={{0,8},{2,10},{4,12},{6,14},{8,0},{10,2},{12,4},{14,6},{1,9},{3,11}... | collective-permute-start | bytes 55304 | tf_op jit(solution)/shard_map/ppermute | solution.py:75
  25.2 1.8 %collective-permute-done.5.far_ref = bf16[4,2,4,288]{3,2,1,0:T(4,128)(2,1)S(1)} collective-permute-done((bf16[4,2,4,288]{3,2,1,0:T(4,128)(2,1)S(1)}, bf16[4,2,4,288]{3,2,1,0:T(4,128)(2,1)S(1)}, u32[]{:S(2)}, u32[]{:S(2)}) %collective-permute-start.5) | collective-permute-done | bytes 18464 | tf_op jit(solution)/shard_map/ppermute | solution.py:75
  27.0 2.7 %collective-permute-start.6 = (bf16[2,2,4,288]{3,2,1,0:T(4,128)(2,1)S(1)}, bf16[2,2,4,288]{3,2,1,0:T(4,128)(2,1)S(1)}, u32[]{:S(2)}, u32[]{:S(2)}) collective-permute-start(bf16[2,2,4,288]{3,2,1,0:T(4,128)(2,1)S(1)} %get-tuple-element.11), channel_id=1, source_target_pairs={{0,6},{2,4},{4,2},{6,0},{8,14},{10,12},{12,10},{14,8},{1,7},{3,5},... | collective-permute-start | bytes 27656 | tf_op jit(solution)/shard_map/ppermute | solution.py:75
  29.7 0.8 %collective-permute-start.8 = (bf16[2,2,4,288]{3,2,1,0:T(4,128)(2,1)S(1)}, bf16[2,2,4,288]{3,2,1,0:T(4,128)(2,1)S(1)}, u32[]{:S(2)}, u32[]{:S(2)}) collective-permute-start(bf16[2,2,4,288]{3,2,1,0:T(4,128)(2,1)S(1)} %get-tuple-element.13), channel_id=1, source_target_pairs={{0,2},{2,0},{4,6},{6,4},{8,10},{10,8},{12,14},{14,12},{1,3},{3,1},... | collective-permute-start | bytes 27656 | tf_op jit(solution)/shard_map/ppermute | solution.py:75
  30.6 1.1 %collective-permute-done.6.refs_0_ = bf16[2,2,4,288]{3,2,1,0:T(4,128)(2,1)S(1)} collective-permute-done((bf16[2,2,4,288]{3,2,1,0:T(4,128)(2,1)S(1)}, bf16[2,2,4,288]{3,2,1,0:T(4,128)(2,1)S(1)}, u32[]{:S(2)}, u32[]{:S(2)}) %collective-permute-start.6) | collective-permute-done | bytes 9248 | tf_op jit(solution)/shard_map/ppermute | solution.py:75
  31.7 1.7 %collective-permute-done.7.refs_1_ = bf16[2,2,4,288]{3,2,1,0:T(4,128)(2,1)S(1)} collective-permute-done((bf16[2,2,4,288]{3,2,1,0:T(4,128)(2,1)S(1)}, bf16[2,2,4,288]{3,2,1,0:T(4,128)(2,1)S(1)}, u32[]{:S(2)}, u32[]{:S(2)}) %collective-permute-start.7) | collective-permute-done | bytes 9248 | tf_op jit(solution)/shard_map/ppermute | solution.py:75
  33.4 1.5 %attend.1.mine_ref = bf16[4,4096]{1,0:T(4,128)(2,1)S(1)} custom-call(s32[4]{0:T(128)S(1)} %copy-done.3, bf16[2,2,4,288]{3,2,1,0:T(4,128)(2,1)S(1)} %collective-permute-done.6.refs_0_, bf16[2,2,4,288]{3,2,1,0:T(4,128)(2,1)S(1)} %collective-permute-done.7.refs_1_, bf16[2,2,4,288]{3,2,1,0:T(4,128)(2,1)S(1)} %collective-permute-done.8.refs_2_, ...), custom_call_target="tpu_custom_call" | custom-call | tf_op jit(solution)/shard_map/attend/pallas_call | solution.py:242
  35.0 2.9 %collective-permute-start.9 = (bf16[4,4096]{1,0:T(4,128)(2,1)S(1)}, bf16[4,4096]{1,0:T(4,128)(2,1)S(1)}, u32[]{:S(2)}, u32[]{:S(2)}) collective-permute-start(bf16[4,4096]{1,0:T(4,128)(2,1)S(1)} %attend.1.mine_ref), channel_id=1, source_target_pairs={{0,8},{2,10},{4,12},{6,14},{8,0},{10,2},{12,4},{14,6},{1,9},{3,11}... | collective-permute-start | bytes 98312 | tf_op jit(solution)/shard_map/ppermute | solution.py:75
  37.9 2.0 %collective-permute-done.9.theirs_ref = bf16[4,4096]{1,0:T(4,128)(2,1)S(1)} collective-permute-done((bf16[4,4096]{1,0:T(4,128)(2,1)S(1)}, bf16[4,4096]{1,0:T(4,128)(2,1)S(1)}, u32[]{:S(2)}, u32[]{:S(2)}) %collective-permute-start.9) | collective-permute-done | bytes 32800 | tf_op jit(solution)/shard_map/ppermute | solution.py:75
  39.9 2.1 %collective-permute-start.12 = (bf16[8,4096]{1,0:T(8,128)(2,1)S(1)}, bf16[8,4096]{1,0:T(8,128)(2,1)S(1)}, u32[]{:S(2)}, u32[]{:S(2)}) collective-permute-start(bf16[8,4096]{1,0:T(8,128)(2,1)S(1)} %pair.3.refs_0_), channel_id=1, source_target_pairs={{0,6},{2,4},{4,2},{6,0},{8,14},{10,12},{12,10},{14,8},{1,7},{3,5},... | collective-permute-start | bytes 196616 | tf_op jit(solution)/shard_map/ppermute | solution.py:75
  42.0 0.3 collective-permute-start.11
  42.2 1.2 %collective-permute-start.10 = (bf16[8,4096]{1,0:T(8,128)(2,1)S(1)}, bf16[8,4096]{1,0:T(8,128)(2,1)S(1)}, u32[]{:S(2)}, u32[]{:S(2)}) collective-permute-start(bf16[8,4096]{1,0:T(8,128)(2,1)S(1)} %pair.3.refs_0_), channel_id=1, source_target_pairs={{0,2},{2,0},{4,6},{6,4},{8,10},{10,8},{12,14},{14,12},{1,3},{3,1},... | collective-permute-start | bytes 196616 | tf_op jit(solution)/shard_map/ppermute | solution.py:75
  43.4 1.7 %collective-permute-done.12.refs_3_ = bf16[8,4096]{1,0:T(8,128)(2,1)S(1)} collective-permute-done((bf16[8,4096]{1,0:T(8,128)(2,1)S(1)}, bf16[8,4096]{1,0:T(8,128)(2,1)S(1)}, u32[]{:S(2)}, u32[]{:S(2)}) %collective-permute-start.12) | collective-permute-done | bytes 65568 | tf_op jit(solution)/shard_map/ppermute | solution.py:75
  45.1 1.1 %collective-permute-done.11.refs_2_ = bf16[8,4096]{1,0:T(8,128)(2,1)S(1)} collective-permute-done((bf16[8,4096]{1,0:T(8,128)(2,1)S(1)}, bf16[8,4096]{1,0:T(8,128)(2,1)S(1)}, u32[]{:S(2)}, u32[]{:S(2)}) %collective-permute-start.11) | collective-permute-done | bytes 65568 | tf_op jit(solution)/shard_map/ppermute | solution.py:75
  46.2 0.3 collective-permute-done.10.refs_1_
  46.5 5.1 %output.1 = (bf16[16,2048]{1,0:T(8,128)(2,1)S(1)}, bf16[16,2048]{1,0:T(8,128)(2,1)S(1)}) custom-call(bf16[8,4096]{1,0:T(8,128)(2,1)S(1)} %pair.3.refs_0_, bf16[8,4096]{1,0:T(8,128)(2,1)S(1)} %collective-permute-done.10.refs_1_, bf16[8,4096]{1,0:T(8,128)(2,1)S(1)} %collective-permute-done.11.refs_2_, bf16[8,4096]{1,0:T(8,128)(2,1)S(1)} %collective-permute-done.12.refs_3_, ...), custom_call_target="tpu_custom_call" | custom-call | tf_op jit(solution)/shard_map/output/pallas_call | solution.py:259
  51.7 0.0 collective-permute-start.13
  51.7 1.2 %collective-permute-done.13 = bf16[16,2048]{1,0:T(8,128)(2,1)S(1)} collective-permute-done((bf16[16,2048]{1,0:T(8,128)(2,1)S(1)}, bf16[16,2048]{1,0:T(8,128)(2,1)S(1)}, u32[]{:S(2)}, u32[]{:S(2)}) %collective-permute-start.13) | collective-permute-done | bytes 65568 | tf_op jit(solution)/shard_map/ppermute | solution.py:71
  53.0 0.6 %add_convert_fusion = bf16[16,2048]{1,0:T(8,128)(2,1)} fusion(bf16[16,2048]{1,0:T(8,128)(2,1)S(1)} %collective-permute-done.13, bf16[16,2048]{1,0:T(8,128)(2,1)S(1)} %get-tuple-element.15), kind=kLoop, calls=%fused_computation | loop fusion | flops 131072 | bytes 196608 | tf_op jit(solution)/shard_map/convert_element_type | solution.py:267
  (33 shorter events, 0.3 us)
Async XLA Ops:
  0.0 16.2 %copy-start = (bf16[4,288,8192]{2,1,0:T(8,128)(2,1)S(1)}, bf16[4,288,8192]{2,1,0:T(8,128)(2,1)}, u32[]{:S(2)}) copy-start(bf16[4,288,8192]{2,1,0:T(8,128)(2,1)} %refs_4_.5) | copy-start | bytes 56623108
  0.0 7.9 %collective-permute-start = (bf16[4,8192]{1,0:T(4,128)(2,1)}, bf16[4,8192]{1,0:T(4,128)(2,1)S(1)}, u32[]{:S(2)}, u32[]{:S(2)}) collective-permute-start(bf16[4,8192]{1,0:T(4,128)(2,1)} %mine_ref.1), channel_id=1, source_target_pairs={{0,8},{2,10},{4,12},{6,14},{8,0},{10,2},{12,4},{14,6},{1,9},{3,11}... | collective-permute-start | bytes 196616 | tf_op jit(solution)/shard_map/ppermute | solution.py:75
  4.0 1.6 %copy-start.4 = (bf16[4,8192]{1,0:T(4,128)(2,1)S(1)}, bf16[4,8192]{1,0:T(4,128)(2,1)}, u32[]{:S(2)}) copy-start(bf16[4,8192]{1,0:T(4,128)(2,1)} %mine_ref.1) | copy-start | bytes 196612
  7.9 25.5 %copy-start.1 = (bf16[4,2,512,128]{3,2,1,0:T(8,128)(2,1)S(1)}, bf16[4,2,512,128]{3,2,1,0:T(8,128)(2,1)}, u32[]{:S(2)}) copy-start(bf16[4,2,512,128]{3,2,1,0:T(8,128)(2,1)} %refs_4_.6) | copy-start | bytes 3145732
  8.0 25.5 %copy-start.2 = (bf16[4,2,512,128]{3,2,1,0:T(8,128)(2,1)S(1)}, bf16[4,2,512,128]{3,2,1,0:T(8,128)(2,1)}, u32[]{:S(2)}) copy-start(bf16[4,2,512,128]{3,2,1,0:T(8,128)(2,1)} %refs_5_.1) | copy-start | bytes 3145732
  8.0 25.5 %copy-start.3 = (s32[4]{0:T(128)S(1)}, s32[4]{0:T(128)}, u32[]{:S(2)}) copy-start(s32[4]{0:T(128)} %lengths_ref.1) | copy-start | bytes 52
  8.0 38.5 %slice-start = ((s8[16777216]{0:T(1024)(128)(4,1)}), s8[4194304]{0:T(1024)(128)(4,1)S(1)}, s32[]{:S(2)}) async-start(s8[16777216]{0:T(1024)(128)(4,1)} %bitcast.17), calls=%async_computation | async-start | bytes 8388608
  8.0 38.5 %slice-start.1 = ((s8[16777216]{0:T(1024)(128)(4,1)}), s8[4194304]{0:T(1024)(128)(4,1)S(1)}, s32[]{:S(2)}) async-start(s8[16777216]{0:T(1024)(128)(4,1)} %bitcast.17), calls=%async_computation.1 | async-start | bytes 8388608
  8.0 6.3 %collective-permute-start.3 = (bf16[8,8192]{1,0:T(8,128)(2,1)S(1)}, bf16[8,8192]{1,0:T(8,128)(2,1)S(1)}, u32[]{:S(2)}, u32[]{:S(2)}) collective-permute-start(bf16[8,8192]{1,0:T(8,128)(2,1)S(1)} %pair.2.refs_0_), channel_id=1, source_target_pairs={{0,6},{2,4},{4,2},{6,0},{8,14},{10,12},{12,10},{14,8},{1,7},{3,5},... | collective-permute-start | bytes 393224 | tf_op jit(solution)/shard_map/ppermute | solution.py:75
  9.7 6.1 %collective-permute-start.2 = (bf16[8,8192]{1,0:T(8,128)(2,1)S(1)}, bf16[8,8192]{1,0:T(8,128)(2,1)S(1)}, u32[]{:S(2)}, u32[]{:S(2)}) collective-permute-start(bf16[8,8192]{1,0:T(8,128)(2,1)S(1)} %pair.2.refs_0_), channel_id=1, source_target_pairs={{0,4},{2,6},{4,0},{6,2},{8,12},{10,14},{12,8},{14,10},{1,5},{3,7},... | collective-permute-start | bytes 393224 | tf_op jit(solution)/shard_map/ppermute | solution.py:75
  11.2 5.0 %collective-permute-start.1 = (bf16[8,8192]{1,0:T(8,128)(2,1)S(1)}, bf16[8,8192]{1,0:T(8,128)(2,1)S(1)}, u32[]{:S(2)}, u32[]{:S(2)}) collective-permute-start(bf16[8,8192]{1,0:T(8,128)(2,1)S(1)} %pair.2.refs_0_), channel_id=1, source_target_pairs={{0,2},{2,0},{4,6},{6,4},{8,10},{10,8},{12,14},{14,12},{1,3},{3,1},... | collective-permute-start | bytes 393224 | tf_op jit(solution)/shard_map/ppermute | solution.py:75
  19.0 27.5 %slice-start.2 = ((s8[16777216]{0:T(1024)(128)(4,1)}), s8[4194304]{0:T(1024)(128)(4,1)S(1)}, s32[]{:S(2)}) async-start(s8[16777216]{0:T(1024)(128)(4,1)} %bitcast.17), calls=%async_computation.2 | async-start | bytes 8388608
  19.1 27.5 %slice-start.3 = ((s8[16777216]{0:T(1024)(128)(4,1)}), s8[4194304]{0:T(1024)(128)(4,1)S(1)}, s32[]{:S(2)}) async-start(s8[16777216]{0:T(1024)(128)(4,1)} %bitcast.17), calls=%async_computation.3 | async-start | bytes 8388608
  19.1 2.9 %collective-permute-start.4 = (bf16[2,32,288]{2,1,0:T(8,128)(2,1)S(1)}, bf16[2,32,288]{2,1,0:T(8,128)(2,1)S(1)}, u32[]{:S(2)}, u32[]{:S(2)}) collective-permute-start(bf16[2,32,288]{2,1,0:T(8,128)(2,1)S(1)} %project.3), channel_id=1, source_target_pairs={{0,1},{1,0},{2,3},{3,2},{4,5},{5,4},{6,7},{7,6},{8,9},{9,8},{10,11... | collective-permute-start | bytes 110600 | tf_op jit(solution)/shard_map/ppermute | solution.py:71
  22.2 4.8 %collective-permute-start.5 = (bf16[4,2,4,288]{3,2,1,0:T(4,128)(2,1)S(1)}, bf16[4,2,4,288]{3,2,1,0:T(4,128)(2,1)S(1)}, u32[]{:S(2)}, u32[]{:S(2)}) collective-permute-start(bf16[4,2,4,288]{3,2,1,0:T(4,128)(2,1)S(1)} %pad_maximum_fusion.1), channel_id=1, source_target_pairs={{0,8},{2,10},{4,12},{6,14},{8,0},{10,2},{12,4},{14,6},{1,9},{3,11}... | collective-permute-start | bytes 55304 | tf_op jit(solution)/shard_map/ppermute | solution.py:75
  27.0 4.7 %collective-permute-start.6 = (bf16[2,2,4,288]{3,2,1,0:T(4,128)(2,1)S(1)}, bf16[2,2,4,288]{3,2,1,0:T(4,128)(2,1)S(1)}, u32[]{:S(2)}, u32[]{:S(2)}) collective-permute-start(bf16[2,2,4,288]{3,2,1,0:T(4,128)(2,1)S(1)} %get-tuple-element.11), channel_id=1, source_target_pairs={{0,6},{2,4},{4,2},{6,0},{8,14},{10,12},{12,10},{14,8},{1,7},{3,5},... | collective-permute-start | bytes 27656 | tf_op jit(solution)/shard_map/ppermute | solution.py:75
  29.7 3.7 %collective-permute-start.7 = (bf16[2,2,4,288]{3,2,1,0:T(4,128)(2,1)S(1)}, bf16[2,2,4,288]{3,2,1,0:T(4,128)(2,1)S(1)}, u32[]{:S(2)}, u32[]{:S(2)}) collective-permute-start(bf16[2,2,4,288]{3,2,1,0:T(4,128)(2,1)S(1)} %get-tuple-element.12), channel_id=1, source_target_pairs={{0,4},{2,6},{4,0},{6,2},{8,12},{10,14},{12,8},{14,10},{1,5},{3,7},... | collective-permute-start | bytes 27656 | tf_op jit(solution)/shard_map/ppermute | solution.py:75
  29.7 3.7 %collective-permute-start.8 = (bf16[2,2,4,288]{3,2,1,0:T(4,128)(2,1)S(1)}, bf16[2,2,4,288]{3,2,1,0:T(4,128)(2,1)S(1)}, u32[]{:S(2)}, u32[]{:S(2)}) collective-permute-start(bf16[2,2,4,288]{3,2,1,0:T(4,128)(2,1)S(1)} %get-tuple-element.13), channel_id=1, source_target_pairs={{0,2},{2,0},{4,6},{6,4},{8,10},{10,8},{12,14},{14,12},{1,3},{3,1},... | collective-permute-start | bytes 27656 | tf_op jit(solution)/shard_map/ppermute | solution.py:75
  35.0 4.9 %collective-permute-start.9 = (bf16[4,4096]{1,0:T(4,128)(2,1)S(1)}, bf16[4,4096]{1,0:T(4,128)(2,1)S(1)}, u32[]{:S(2)}, u32[]{:S(2)}) collective-permute-start(bf16[4,4096]{1,0:T(4,128)(2,1)S(1)} %attend.1.mine_ref), channel_id=1, source_target_pairs={{0,8},{2,10},{4,12},{6,14},{8,0},{10,2},{12,4},{14,6},{1,9},{3,11}... | collective-permute-start | bytes 98312 | tf_op jit(solution)/shard_map/ppermute | solution.py:75
  39.9 5.2 %collective-permute-start.12 = (bf16[8,4096]{1,0:T(8,128)(2,1)S(1)}, bf16[8,4096]{1,0:T(8,128)(2,1)S(1)}, u32[]{:S(2)}, u32[]{:S(2)}) collective-permute-start(bf16[8,4096]{1,0:T(8,128)(2,1)S(1)} %pair.3.refs_0_), channel_id=1, source_target_pairs={{0,6},{2,4},{4,2},{6,0},{8,14},{10,12},{12,10},{14,8},{1,7},{3,5},... | collective-permute-start | bytes 196616 | tf_op jit(solution)/shard_map/ppermute | solution.py:75
  42.0 4.3 %collective-permute-start.11 = (bf16[8,4096]{1,0:T(8,128)(2,1)S(1)}, bf16[8,4096]{1,0:T(8,128)(2,1)S(1)}, u32[]{:S(2)}, u32[]{:S(2)}) collective-permute-start(bf16[8,4096]{1,0:T(8,128)(2,1)S(1)} %pair.3.refs_0_), channel_id=1, source_target_pairs={{0,4},{2,6},{4,0},{6,2},{8,12},{10,14},{12,8},{14,10},{1,5},{3,7},... | collective-permute-start | bytes 196616 | tf_op jit(solution)/shard_map/ppermute | solution.py:75
  42.2 4.3 %collective-permute-start.10 = (bf16[8,4096]{1,0:T(8,128)(2,1)S(1)}, bf16[8,4096]{1,0:T(8,128)(2,1)S(1)}, u32[]{:S(2)}, u32[]{:S(2)}) collective-permute-start(bf16[8,4096]{1,0:T(8,128)(2,1)S(1)} %pair.3.refs_0_), channel_id=1, source_target_pairs={{0,2},{2,0},{4,6},{6,4},{8,10},{10,8},{12,14},{14,12},{1,3},{3,1},... | collective-permute-start | bytes 196616 | tf_op jit(solution)/shard_map/ppermute | solution.py:75
  51.7 1.3 %collective-permute-start.13 = (bf16[16,2048]{1,0:T(8,128)(2,1)S(1)}, bf16[16,2048]{1,0:T(8,128)(2,1)S(1)}, u32[]{:S(2)}, u32[]{:S(2)}) collective-permute-start(bf16[16,2048]{1,0:T(8,128)(2,1)S(1)} %get-tuple-element.16), channel_id=1, source_target_pairs={{0,1},{1,0},{2,3},{3,2},{4,5},{5,4},{6,7},{7,6},{8,9},{9,8},{10,11... | collective-permute-start | bytes 196616 | tf_op jit(solution)/shard_map/ppermute | solution.py:71

commit v4 on v3

--- a/solution.py
+++ b/solution.py
@@ -107,6 +107,18 @@
     return [pair] + [hop(pair, chips, mask) for mask in range(1, chips // 2)]
 
 
+def gather_early(block, staged, chips):
+    half = chips // 2
+    far = hop(block, chips, half)
+    masks = range(half - 1, 0, -1)
+    near = {mask: hop(block, chips, mask) for mask in masks}
+    beyond = {mask: hop(far, chips, mask) for mask in masks}
+    pieces = [staged, far]
+    for mask in range(1, half):
+        pieces += [near[mask], beyond[mask]]
+    return pieces
+
+
 def project_kernel(*refs, swapped):
     *x_refs, w_ref, out_ref = refs
     heads = out_ref.shape[0]
@@ -114,8 +126,8 @@
     core = lax.axis_index("gx")
     first = heads * ((1 - core) if swapped else core)
     for head in range(heads):
-        value = lax.dot_general(x, w_ref[first + head], NT, preferred_element_type=jnp.float32)
-        out_ref[head] = value.astype(jnp.bfloat16)
+        value = lax.dot_general(w_ref[first + head], x, NT, preferred_element_type=jnp.float32)
+        out_ref[head] = value.T.astype(jnp.bfloat16)
 
 
 def merge_kernel(near_ref, far_ref, *out_refs):
@@ -185,10 +197,13 @@
     source = (mask % half) * (2 * rows) + (mask // half) * rows + within % rows
     order = jnp.where(column == source, 1.0, 0.0).astype(jnp.bfloat16)
     x = jnp.dot(order, x, preferred_element_type=jnp.float32).astype(jnp.bfloat16)
-    value = lax.dot_general(x, w_ref[...], NT, preferred_element_type=jnp.float32)
-    value = value.astype(jnp.bfloat16)
-    keep_ref[...] = value[: half * rows]
-    send_ref[...] = value[half * rows :]
+    cols = w_ref.shape[0]
+    width = min(cols, 256)
+    for at in range(0, cols, width):
+        value = lax.dot_general(w_ref[at : at + width], x, NT, preferred_element_type=jnp.float32)
+        value = value.T.astype(jnp.bfloat16)
+        keep_ref[:, at : at + width] = value[: half * rows]
+        send_ref[:, at : at + width] = value[half * rows :]
 
 
 def in_vmem(count):
@@ -209,13 +224,13 @@
     qkv_weight, out_weight = hold(qkv_weight), hold(out_weight)
     key_cache, value_cache = hold(key_cache), hold(value_cache)
 
-    pieces = [hold(piece) for piece in gather_rows(stage(activations), hop(activations, chips, half), chips)]
+    pieces = [hold(piece) for piece in gather_early(activations, stage(activations), chips)]
 
     def project(swapped):
         return pl.pallas_call(
             functools.partial(project_kernel, swapped=swapped),
             out_shape=jax.ShapeDtypeStruct((kv_local, rows, part), jnp.bfloat16),
-            in_specs=in_vmem(half + 1),
+            in_specs=in_vmem(chips + 1),
             out_specs=in_vmem(1)[0],
             compiler_params=limits,
             cost_estimate=pl.CostEstimate(

time: 53.7 us -> 51.9 us (0.966)
  waiting for transfers between devices: 17.9 us -> 15.4 us
  starting transfers between devices: 20.7 us -> 22.9 us
  Pallas kernels: 12.4 us -> 11.5 us
  local copies, waits for them, and re-layouts: 1.75 us -> 0.98 us
    ppermute x12 -> x15, waiting for transfers between devices: 16.6 us -> 14.2 us  [hop(): return lax.ppermute(x, 'gy', [(chip, chip ^ mask) for chip in range(chips)])]
    ppermute x12 -> x15, starting transfers between devices: 20.6 us -> 22.8 us  [hop(): return lax.ppermute(x, 'gy', [(chip, chip ^ mask) for chip in range(chips)])]
    unnamed x18, local copies, waits for them, and re-layouts: 1.64 us -> 0.88 us
  transfers between devices with their start and end apart: 14 -> 17, of which waited for: 12 -> 13; matrix products, arithmetic and copies ran while one was open for 0% -> 0% of each run, Pallas kernels for 5% -> 5%
where the time goes in v4:
time: 51.9 us; the launch traced here: 51.7 us
  starting transfers between devices  22.9 us (44%)
  waiting for transfers between devices  15.4 us (30%)
  Pallas kernels  11.5 us (22%)
  local copies, waits for them, and re-layouts  0.98 us (2%)
  other arithmetic  0.72 us (1%)
    ppermute x15, starting transfers between devices, hop(): return lax.ppermute(x, 'gy', [(chip, chip ^ mask) for chip in range(chips)])  22.8 us
    ppermute x15, waiting for transfers between devices, hop(): return lax.ppermute(x, 'gy', [(chip, chip ^ mask) for chip in range(chips)])  14.2 us
    pallas_call x2, Pallas kernels, project(): pl.pallas_call(functools.partial(project_kernel, swapped=swapped), out_sh...  5.28 us
    pallas_call x1, Pallas kernels, local(): pl.pallas_call(functools.partial(output_kernel, rows=seqs), out_shape=(pi...  4.64 us
    pallas_call x1, Pallas kernels, local(): pl.pallas_call(attend_kernel, out_shape=jax.ShapeDtypeStruct((seqs, feats...  1.52 us
    ppermute x2, waiting for transfers between devices, swap(): return lax.ppermute(x, 'gx', [(0, 1), (1, 0)])  1.24 us
  transfers between devices with their start and end apart: 17, of which 13 were waited for; matrix products, arithmetic and copies ran while one was open for 0% of the time, Pallas kernels for 5%

profile of v4, /device:TPU:0, one launch (start us, length us, event | category | flops | bytes accessed | tf_op | source)
XLA Modules:
  0.0 51.7 jit_solution(4821924311702727471)
XLA Ops:
  0.0 4.0 %collective-permute-start = (bf16[4,8192]{1,0:T(4,128)(2,1)}, bf16[4,8192]{1,0:T(4,128)(2,1)S(1)}, u32[]{:S(2)}, u32[]{:S(2)}) collective-permute-start(bf16[4,8192]{1,0:T(4,128)(2,1)} %mine_ref.1), channel_id=1, source_target_pairs={{0,8},{2,10},{4,12},{6,14},{8,0},{10,2},{12,4},{14,6},{1,9},{3,11}... | collective-permute-start | bytes 196616 | tf_op jit(solution)/shard_map/ppermute | solution.py:75
  4.0 1.5 %collective-permute-start.1 = (bf16[4,8192]{1,0:T(4,128)(2,1)}, bf16[4,8192]{1,0:T(4,128)(2,1)S(1)}, u32[]{:S(2)}, u32[]{:S(2)}) collective-permute-start(bf16[4,8192]{1,0:T(4,128)(2,1)} %mine_ref.1), channel_id=1, source_target_pairs={{0,2},{2,0},{4,6},{6,4},{8,10},{10,8},{12,14},{14,12},{1,3},{3,1},... | collective-permute-start | bytes 196616 | tf_op jit(solution)/shard_map/ppermute | solution.py:75
  5.5 1.5 %collective-permute-start.5 = (bf16[4,8192]{1,0:T(4,128)(2,1)}, bf16[4,8192]{1,0:T(4,128)(2,1)S(1)}, u32[]{:S(2)}, u32[]{:S(2)}) collective-permute-start(bf16[4,8192]{1,0:T(4,128)(2,1)} %mine_ref.1), channel_id=1, source_target_pairs={{0,6},{2,4},{4,2},{6,0},{8,14},{10,12},{12,10},{14,8},{1,7},{3,5},... | collective-permute-start | bytes 196616 | tf_op jit(solution)/shard_map/ppermute | solution.py:75
  7.1 0.4 collective-permute-start.3
  7.5 2.5 %collective-permute-start.6 = (bf16[4,8192]{1,0:T(4,128)(2,1)S(1)}, bf16[4,8192]{1,0:T(4,128)(2,1)S(1)}, u32[]{:S(2)}, u32[]{:S(2)}) collective-permute-start(bf16[4,8192]{1,0:T(4,128)(2,1)S(1)} %collective-permute-done.refs_1_), channel_id=1, source_target_pairs={{0,6},{2,4},{4,2},{6,0},{8,14},{10,12},{12,10},{14,8},{1,7},{3,5},... | collective-permute-start | bytes 196616 | tf_op jit(solution)/shard_map/ppermute | solution.py:75
  10.0 0.8 %collective-permute-start.4 = (bf16[4,8192]{1,0:T(4,128)(2,1)S(1)}, bf16[4,8192]{1,0:T(4,128)(2,1)S(1)}, u32[]{:S(2)}, u32[]{:S(2)}) collective-permute-start(bf16[4,8192]{1,0:T(4,128)(2,1)S(1)} %collective-permute-done.refs_1_), channel_id=1, source_target_pairs={{0,4},{2,6},{4,0},{6,2},{8,12},{10,14},{12,8},{14,10},{1,5},{3,7},... | collective-permute-start | bytes 196616 | tf_op jit(solution)/shard_map/ppermute | solution.py:75
  11.0 0.8 %copy-done.4 = bf16[4,8192]{1,0:T(4,128)(2,1)S(1)} copy-done((bf16[4,8192]{1,0:T(4,128)(2,1)S(1)}, bf16[4,8192]{1,0:T(4,128)(2,1)}, u32[]{:S(2)}) %copy-start.4) | copy-done | bytes 65560
  11.9 0.2 collective-permute-done.3.refs_4_
  12.1 1.9 %collective-permute-done.6.refs_7_ = bf16[4,8192]{1,0:T(4,128)(2,1)S(1)} collective-permute-done((bf16[4,8192]{1,0:T(4,128)(2,1)S(1)}, bf16[4,8192]{1,0:T(4,128)(2,1)S(1)}, u32[]{:S(2)}, u32[]{:S(2)}) %collective-permute-start.6) | collective-permute-done | bytes 65568 | tf_op jit(solution)/shard_map/ppermute | solution.py:75
  14.0 0.3 collective-permute-done.4.refs_5_
  14.3 0.8 %collective-permute-done.2.refs_3_ = bf16[4,8192]{1,0:T(4,128)(2,1)S(1)} collective-permute-done((bf16[4,8192]{1,0:T(4,128)(2,1)S(1)}, bf16[4,8192]{1,0:T(4,128)(2,1)S(1)}, u32[]{:S(2)}, u32[]{:S(2)}) %collective-permute-start.2) | collective-permute-done | bytes 65568 | tf_op jit(solution)/shard_map/ppermute | solution.py:75
  15.1 2.6 %project.3 = bf16[2,32,288]{2,1,0:T(8,128)(2,1)S(1)} custom-call(bf16[4,8192]{1,0:T(4,128)(2,1)S(1)} %stage.1.refs_0_, bf16[4,8192]{1,0:T(4,128)(2,1)S(1)} %collective-permute-done.refs_1_, bf16[4,8192]{1,0:T(4,128)(2,1)S(1)} %collective-permute-done.1.refs_2_, bf16[4,8192]{1,0:T(4,128)(2,1)S(1)} %collective-permute-done.2.refs_3_, ...), custom_call_target="tpu_custom_call" | custom-call | flops 2415919104 | bytes 1048576 | tf_op jit(solution)/shard_map/project/pallas_call | solution.py:230
  17.9 2.6 %project.2 = bf16[2,32,288]{2,1,0:T(8,128)(2,1)S(1)} custom-call(bf16[4,8192]{1,0:T(4,128)(2,1)S(1)} %stage.1.refs_0_, bf16[4,8192]{1,0:T(4,128)(2,1)S(1)} %collective-permute-done.refs_1_, bf16[4,8192]{1,0:T(4,128)(2,1)S(1)} %collective-permute-done.1.refs_2_, bf16[4,8192]{1,0:T(4,128)(2,1)S(1)} %collective-permute-done.2.refs_3_, ...), custom_call_target="tpu_custom_call" | custom-call | flops 2415919104 | bytes 1048576 | tf_op jit(solution)/shard_map/project/pallas_call | solution.py:230
  20.7 2.1 %collective-permute-start.8 = (bf16[4,2,4,288]{3,2,1,0:T(4,128)(2,1)S(1)}, bf16[4,2,4,288]{3,2,1,0:T(4,128)(2,1)S(1)}, u32[]{:S(2)}, u32[]{:S(2)}) collective-permute-start(bf16[4,2,4,288]{3,2,1,0:T(4,128)(2,1)S(1)} %pad_maximum_fusion.1), channel_id=1, source_target_pairs={{0,8},{2,10},{4,12},{6,14},{8,0},{10,2},{12,4},{14,6},{1,9},{3,11}... | collective-permute-start | bytes 55304 | tf_op jit(solution)/shard_map/ppermute | solution.py:75
  22.9 2.6 %collective-permute-done.8.far_ref = bf16[4,2,4,288]{3,2,1,0:T(4,128)(2,1)S(1)} collective-permute-done((bf16[4,2,4,288]{3,2,1,0:T(4,128)(2,1)S(1)}, bf16[4,2,4,288]{3,2,1,0:T(4,128)(2,1)S(1)}, u32[]{:S(2)}, u32[]{:S(2)}) %collective-permute-start.8) | collective-permute-done | bytes 18464 | tf_op jit(solution)/shard_map/ppermute | solution.py:75
  25.5 1.2 %collective-permute-start.9 = (bf16[2,2,4,288]{3,2,1,0:T(4,128)(2,1)S(1)}, bf16[2,2,4,288]{3,2,1,0:T(4,128)(2,1)S(1)}, u32[]{:S(2)}, u32[]{:S(2)}) collective-permute-start(bf16[2,2,4,288]{3,2,1,0:T(4,128)(2,1)S(1)} %get-tuple-element.11), channel_id=1, source_target_pairs={{0,6},{2,4},{4,2},{6,0},{8,14},{10,12},{12,10},{14,8},{1,7},{3,5},... | collective-permute-start | bytes 27656 | tf_op jit(solution)/shard_map/ppermute | solution.py:75
  26.8 0.4 collective-permute-start.10
  27.2 1.9 %collective-permute-start.11 = (bf16[2,2,4,288]{3,2,1,0:T(4,128)(2,1)S(1)}, bf16[2,2,4,288]{3,2,1,0:T(4,128)(2,1)S(1)}, u32[]{:S(2)}, u32[]{:S(2)}) collective-permute-start(bf16[2,2,4,288]{3,2,1,0:T(4,128)(2,1)S(1)} %get-tuple-element.13), channel_id=1, source_target_pairs={{0,2},{2,0},{4,6},{6,4},{8,10},{10,8},{12,14},{14,12},{1,3},{3,1},... | collective-permute-start | bytes 27656 | tf_op jit(solution)/shard_map/ppermute | solution.py:75
  29.1 1.1 %collective-permute-done.9.refs_0_ = bf16[2,2,4,288]{3,2,1,0:T(4,128)(2,1)S(1)} collective-permute-done((bf16[2,2,4,288]{3,2,1,0:T(4,128)(2,1)S(1)}, bf16[2,2,4,288]{3,2,1,0:T(4,128)(2,1)S(1)}, u32[]{:S(2)}, u32[]{:S(2)}) %collective-permute-start.9) | collective-permute-done | bytes 9248 | tf_op jit(solution)/shard_map/ppermute | solution.py:75
  30.2 0.3 collective-permute-done.10.refs_1_
  30.5 0.4 collective-permute-done.11.refs_2_
  30.9 1.5 %attend.1.mine_ref = bf16[4,4096]{1,0:T(4,128)(2,1)S(1)} custom-call(s32[4]{0:T(128)S(1)} %copy-done.3, bf16[2,2,4,288]{3,2,1,0:T(4,128)(2,1)S(1)} %collective-permute-done.9.refs_0_, bf16[2,2,4,288]{3,2,1,0:T(4,128)(2,1)S(1)} %collective-permute-done.10.refs_1_, bf16[2,2,4,288]{3,2,1,0:T(4,128)(2,1)S(1)} %collective-permute-done.11.refs_2_, ...), custom_call_target="tpu_custom_call" | custom-call | tf_op jit(solution)/shard_map/attend/pallas_call | solution.py:257
  32.4 2.6 %collective-permute-start.12 = (bf16[4,4096]{1,0:T(4,128)(2,1)S(1)}, bf16[4,4096]{1,0:T(4,128)(2,1)S(1)}, u32[]{:S(2)}, u32[]{:S(2)}) collective-permute-start(bf16[4,4096]{1,0:T(4,128)(2,1)S(1)} %attend.1.mine_ref), channel_id=1, source_target_pairs={{0,8},{2,10},{4,12},{6,14},{8,0},{10,2},{12,4},{14,6},{1,9},{3,11}... | collective-permute-start | bytes 98312 | tf_op jit(solution)/shard_map/ppermute | solution.py:75
  35.0 2.3 %collective-permute-done.12.theirs_ref = bf16[4,4096]{1,0:T(4,128)(2,1)S(1)} collective-permute-done((bf16[4,4096]{1,0:T(4,128)(2,1)S(1)}, bf16[4,4096]{1,0:T(4,128)(2,1)S(1)}, u32[]{:S(2)}, u32[]{:S(2)}) %collective-permute-start.12) | collective-permute-done | bytes 32800 | tf_op jit(solution)/shard_map/ppermute | solution.py:75
  37.4 2.6 %collective-permute-start.15 = (bf16[8,4096]{1,0:T(8,128)(2,1)S(1)}, bf16[8,4096]{1,0:T(8,128)(2,1)S(1)}, u32[]{:S(2)}, u32[]{:S(2)}) collective-permute-start(bf16[8,4096]{1,0:T(8,128)(2,1)S(1)} %pair.1.refs_0_), channel_id=1, source_target_pairs={{0,6},{2,4},{4,2},{6,0},{8,14},{10,12},{12,10},{14,8},{1,7},{3,5},... | collective-permute-start | bytes 196616 | tf_op jit(solution)/shard_map/ppermute | solution.py:75
  39.9 0.9 %collective-permute-start.14 = (bf16[8,4096]{1,0:T(8,128)(2,1)S(1)}, bf16[8,4096]{1,0:T(8,128)(2,1)S(1)}, u32[]{:S(2)}, u32[]{:S(2)}) collective-permute-start(bf16[8,4096]{1,0:T(8,128)(2,1)S(1)} %pair.1.refs_0_), channel_id=1, source_target_pairs={{0,4},{2,6},{4,0},{6,2},{8,12},{10,14},{12,8},{14,10},{1,5},{3,7},... | collective-permute-start | bytes 196616 | tf_op jit(solution)/shard_map/ppermute | solution.py:75
  40.9 1.7 %collective-permute-done.15.refs_3_ = bf16[8,4096]{1,0:T(8,128)(2,1)S(1)} collective-permute-done((bf16[8,4096]{1,0:T(8,128)(2,1)S(1)}, bf16[8,4096]{1,0:T(8,128)(2,1)S(1)}, u32[]{:S(2)}, u32[]{:S(2)}) %collective-permute-start.15) | collective-permute-done | bytes 65568 | tf_op jit(solution)/shard_map/ppermute | solution.py:75
  42.6 1.6 %collective-permute-done.14.refs_2_ = bf16[8,4096]{1,0:T(8,128)(2,1)S(1)} collective-permute-done((bf16[8,4096]{1,0:T(8,128)(2,1)S(1)}, bf16[8,4096]{1,0:T(8,128)(2,1)S(1)}, u32[]{:S(2)}, u32[]{:S(2)}) %collective-permute-start.14) | collective-permute-done | bytes 65568 | tf_op jit(solution)/shard_map/ppermute | solution.py:75
  44.2 0.9 %collective-permute-done.13.refs_1_ = bf16[8,4096]{1,0:T(8,128)(2,1)S(1)} collective-permute-done((bf16[8,4096]{1,0:T(8,128)(2,1)S(1)}, bf16[8,4096]{1,0:T(8,128)(2,1)S(1)}, u32[]{:S(2)}, u32[]{:S(2)}) %collective-permute-start.13) | collective-permute-done | bytes 65568 | tf_op jit(solution)/shard_map/ppermute | solution.py:75
  45.1 4.6 %output.1 = (bf16[16,2048]{1,0:T(8,128)(2,1)S(1)}, bf16[16,2048]{1,0:T(8,128)(2,1)S(1)}) custom-call(bf16[8,4096]{1,0:T(8,128)(2,1)S(1)} %pair.1.refs_0_, bf16[8,4096]{1,0:T(8,128)(2,1)S(1)} %collective-permute-done.13.refs_1_, bf16[8,4096]{1,0:T(8,128)(2,1)S(1)} %collective-permute-done.14.refs_2_, bf16[8,4096]{1,0:T(8,128)(2,1)S(1)} %collective-permute-done.15.refs_3_, ...), custom_call_target="tpu_custom_call" | custom-call | tf_op jit(solution)/shard_map/output/pallas_call | solution.py:274
  49.8 1.2 %collective-permute-done.16 = bf16[16,2048]{1,0:T(8,128)(2,1)S(1)} collective-permute-done((bf16[16,2048]{1,0:T(8,128)(2,1)S(1)}, bf16[16,2048]{1,0:T(8,128)(2,1)S(1)}, u32[]{:S(2)}, u32[]{:S(2)}) %collective-permute-start.16) | collective-permute-done | bytes 65568 | tf_op jit(solution)/shard_map/ppermute | solution.py:71
  51.1 0.6 %add_convert_fusion = bf16[16,2048]{1,0:T(8,128)(2,1)} fusion(bf16[16,2048]{1,0:T(8,128)(2,1)S(1)} %collective-permute-done.16, bf16[16,2048]{1,0:T(8,128)(2,1)S(1)} %get-tuple-element.15), kind=kLoop, calls=%fused_computation | loop fusion | flops 131072 | bytes 196608 | tf_op jit(solution)/shard_map/convert_element_type | solution.py:282
  (38 shorter events, 0.6 us)
Async XLA Ops:
  0.0 15.1 %copy-start = (bf16[4,288,8192]{2,1,0:T(8,128)(2,1)S(1)}, bf16[4,288,8192]{2,1,0:T(8,128)(2,1)}, u32[]{:S(2)}) copy-start(bf16[4,288,8192]{2,1,0:T(8,128)(2,1)} %refs_8_.3) | copy-start | bytes 56623108
  0.0 7.5 %collective-permute-start = (bf16[4,8192]{1,0:T(4,128)(2,1)}, bf16[4,8192]{1,0:T(4,128)(2,1)S(1)}, u32[]{:S(2)}, u32[]{:S(2)}) collective-permute-start(bf16[4,8192]{1,0:T(4,128)(2,1)} %mine_ref.1), channel_id=1, source_target_pairs={{0,8},{2,10},{4,12},{6,14},{8,0},{10,2},{12,4},{14,6},{1,9},{3,11}... | collective-permute-start | bytes 196616 | tf_op jit(solution)/shard_map/ppermute | solution.py:75
  4.0 6.8 %collective-permute-start.1 = (bf16[4,8192]{1,0:T(4,128)(2,1)}, bf16[4,8192]{1,0:T(4,128)(2,1)S(1)}, u32[]{:S(2)}, u32[]{:S(2)}) collective-permute-start(bf16[4,8192]{1,0:T(4,128)(2,1)} %mine_ref.1), channel_id=1, source_target_pairs={{0,2},{2,0},{4,6},{6,4},{8,10},{10,8},{12,14},{14,12},{1,3},{3,1},... | collective-permute-start | bytes 196616 | tf_op jit(solution)/shard_map/ppermute | solution.py:75
  5.5 6.4 %collective-permute-start.5 = (bf16[4,8192]{1,0:T(4,128)(2,1)}, bf16[4,8192]{1,0:T(4,128)(2,1)S(1)}, u32[]{:S(2)}, u32[]{:S(2)}) collective-permute-start(bf16[4,8192]{1,0:T(4,128)(2,1)} %mine_ref.1), channel_id=1, source_target_pairs={{0,6},{2,4},{4,2},{6,0},{8,14},{10,12},{12,10},{14,8},{1,7},{3,5},... | collective-permute-start | bytes 196616 | tf_op jit(solution)/shard_map/ppermute | solution.py:75
  7.1 5.0 %collective-permute-start.3 = (bf16[4,8192]{1,0:T(4,128)(2,1)}, bf16[4,8192]{1,0:T(4,128)(2,1)S(1)}, u32[]{:S(2)}, u32[]{:S(2)}) collective-permute-start(bf16[4,8192]{1,0:T(4,128)(2,1)} %mine_ref.1), channel_id=1, source_target_pairs={{0,4},{2,6},{4,0},{6,2},{8,12},{10,14},{12,8},{14,10},{1,5},{3,7},... | collective-permute-start | bytes 196616 | tf_op jit(solution)/shard_map/ppermute | solution.py:75
  7.5 6.5 %collective-permute-start.6 = (bf16[4,8192]{1,0:T(4,128)(2,1)S(1)}, bf16[4,8192]{1,0:T(4,128)(2,1)S(1)}, u32[]{:S(2)}, u32[]{:S(2)}) collective-permute-start(bf16[4,8192]{1,0:T(4,128)(2,1)S(1)} %collective-permute-done.refs_1_), channel_id=1, source_target_pairs={{0,6},{2,4},{4,2},{6,0},{8,14},{10,12},{12,10},{14,8},{1,7},{3,5},... | collective-permute-start | bytes 196616 | tf_op jit(solution)/shard_map/ppermute | solution.py:75
  10.0 4.3 %collective-permute-start.4 = (bf16[4,8192]{1,0:T(4,128)(2,1)S(1)}, bf16[4,8192]{1,0:T(4,128)(2,1)S(1)}, u32[]{:S(2)}, u32[]{:S(2)}) collective-permute-start(bf16[4,8192]{1,0:T(4,128)(2,1)S(1)} %collective-permute-done.refs_1_), channel_id=1, source_target_pairs={{0,4},{2,6},{4,0},{6,2},{8,12},{10,14},{12,8},{14,10},{1,5},{3,7},... | collective-permute-start | bytes 196616 | tf_op jit(solution)/shard_map/ppermute | solution.py:75
  10.9 4.3 %collective-permute-start.2 = (bf16[4,8192]{1,0:T(4,128)(2,1)S(1)}, bf16[4,8192]{1,0:T(4,128)(2,1)S(1)}, u32[]{:S(2)}, u32[]{:S(2)}) collective-permute-start(bf16[4,8192]{1,0:T(4,128)(2,1)S(1)} %collective-permute-done.refs_1_), channel_id=1, source_target_pairs={{0,2},{2,0},{4,6},{6,4},{8,10},{10,8},{12,14},{14,12},{1,3},{3,1},... | collective-permute-start | bytes 196616 | tf_op jit(solution)/shard_map/ppermute | solution.py:75
  11.0 0.8 %copy-start.4 = (bf16[4,8192]{1,0:T(4,128)(2,1)S(1)}, bf16[4,8192]{1,0:T(4,128)(2,1)}, u32[]{:S(2)}) copy-start(bf16[4,8192]{1,0:T(4,128)(2,1)} %mine_ref.1) | copy-start | bytes 196612
  11.9 19.0 %copy-start.1 = (bf16[4,2,512,128]{3,2,1,0:T(8,128)(2,1)S(1)}, bf16[4,2,512,128]{3,2,1,0:T(8,128)(2,1)}, u32[]{:S(2)}) copy-start(bf16[4,2,512,128]{3,2,1,0:T(8,128)(2,1)} %refs_4_.2) | copy-start | bytes 3145732
  11.9 19.0 %copy-start.2 = (bf16[4,2,512,128]{3,2,1,0:T(8,128)(2,1)S(1)}, bf16[4,2,512,128]{3,2,1,0:T(8,128)(2,1)}, u32[]{:S(2)}) copy-start(bf16[4,2,512,128]{3,2,1,0:T(8,128)(2,1)} %refs_5_.1) | copy-start | bytes 3145732
  11.9 19.0 %copy-start.3 = (s32[4]{0:T(128)S(1)}, s32[4]{0:T(128)}, u32[]{:S(2)}) copy-start(s32[4]{0:T(128)} %lengths_ref.1) | copy-start | bytes 52
  11.9 33.2 %slice-start = ((s8[16777216]{0:T(1024)(128)(4,1)}), s8[4194304]{0:T(1024)(128)(4,1)S(1)}, s32[]{:S(2)}) async-start(s8[16777216]{0:T(1024)(128)(4,1)} %bitcast.17), calls=%async_computation | async-start | bytes 8388608
  11.9 33.2 %slice-start.1 = ((s8[16777216]{0:T(1024)(128)(4,1)}), s8[4194304]{0:T(1024)(128)(4,1)S(1)}, s32[]{:S(2)}) async-start(s8[16777216]{0:T(1024)(128)(4,1)} %bitcast.17), calls=%async_computation.1 | async-start | bytes 8388608
  17.8 27.3 %slice-start.2 = ((s8[16777216]{0:T(1024)(128)(4,1)}), s8[4194304]{0:T(1024)(128)(4,1)S(1)}, s32[]{:S(2)}) async-start(s8[16777216]{0:T(1024)(128)(4,1)} %bitcast.17), calls=%async_computation.2 | async-start | bytes 8388608
  17.8 27.3 %slice-start.3 = ((s8[16777216]{0:T(1024)(128)(4,1)}), s8[4194304]{0:T(1024)(128)(4,1)S(1)}, s32[]{:S(2)}) async-start(s8[16777216]{0:T(1024)(128)(4,1)} %bitcast.17), calls=%async_computation.3 | async-start | bytes 8388608
  17.8 2.7 %collective-permute-start.7 = (bf16[2,32,288]{2,1,0:T(8,128)(2,1)S(1)}, bf16[2,32,288]{2,1,0:T(8,128)(2,1)S(1)}, u32[]{:S(2)}, u32[]{:S(2)}) collective-permute-start(bf16[2,32,288]{2,1,0:T(8,128)(2,1)S(1)} %project.3), channel_id=1, source_target_pairs={{0,1},{1,0},{2,3},{3,2},{4,5},{5,4},{6,7},{7,6},{8,9},{9,8},{10,11... | collective-permute-start | bytes 110600 | tf_op jit(solution)/shard_map/ppermute | solution.py:71
  20.7 4.8 %collective-permute-start.8 = (bf16[4,2,4,288]{3,2,1,0:T(4,128)(2,1)S(1)}, bf16[4,2,4,288]{3,2,1,0:T(4,128)(2,1)S(1)}, u32[]{:S(2)}, u32[]{:S(2)}) collective-permute-start(bf16[4,2,4,288]{3,2,1,0:T(4,128)(2,1)S(1)} %pad_maximum_fusion.1), channel_id=1, source_target_pairs={{0,8},{2,10},{4,12},{6,14},{8,0},{10,2},{12,4},{14,6},{1,9},{3,11}... | collective-permute-start | bytes 55304 | tf_op jit(solution)/shard_map/ppermute | solution.py:75
  25.5 4.7 %collective-permute-start.9 = (bf16[2,2,4,288]{3,2,1,0:T(4,128)(2,1)S(1)}, bf16[2,2,4,288]{3,2,1,0:T(4,128)(2,1)S(1)}, u32[]{:S(2)}, u32[]{:S(2)}) collective-permute-start(bf16[2,2,4,288]{3,2,1,0:T(4,128)(2,1)S(1)} %get-tuple-element.11), channel_id=1, source_target_pairs={{0,6},{2,4},{4,2},{6,0},{8,14},{10,12},{12,10},{14,8},{1,7},{3,5},... | collective-permute-start | bytes 27656 | tf_op jit(solution)/shard_map/ppermute | solution.py:75
  26.8 3.7 %collective-permute-start.10 = (bf16[2,2,4,288]{3,2,1,0:T(4,128)(2,1)S(1)}, bf16[2,2,4,288]{3,2,1,0:T(4,128)(2,1)S(1)}, u32[]{:S(2)}, u32[]{:S(2)}) collective-permute-start(bf16[2,2,4,288]{3,2,1,0:T(4,128)(2,1)S(1)} %get-tuple-element.12), channel_id=1, source_target_pairs={{0,4},{2,6},{4,0},{6,2},{8,12},{10,14},{12,8},{14,10},{1,5},{3,7},... | collective-permute-start | bytes 27656 | tf_op jit(solution)/shard_map/ppermute | solution.py:75
  27.2 3.7 %collective-permute-start.11 = (bf16[2,2,4,288]{3,2,1,0:T(4,128)(2,1)S(1)}, bf16[2,2,4,288]{3,2,1,0:T(4,128)(2,1)S(1)}, u32[]{:S(2)}, u32[]{:S(2)}) collective-permute-start(bf16[2,2,4,288]{3,2,1,0:T(4,128)(2,1)S(1)} %get-tuple-element.13), channel_id=1, source_target_pairs={{0,2},{2,0},{4,6},{6,4},{8,10},{10,8},{12,14},{14,12},{1,3},{3,1},... | collective-permute-start | bytes 27656 | tf_op jit(solution)/shard_map/ppermute | solution.py:75
  32.4 4.9 %collective-permute-start.12 = (bf16[4,4096]{1,0:T(4,128)(2,1)S(1)}, bf16[4,4096]{1,0:T(4,128)(2,1)S(1)}, u32[]{:S(2)}, u32[]{:S(2)}) collective-permute-start(bf16[4,4096]{1,0:T(4,128)(2,1)S(1)} %attend.1.mine_ref), channel_id=1, source_target_pairs={{0,8},{2,10},{4,12},{6,14},{8,0},{10,2},{12,4},{14,6},{1,9},{3,11}... | collective-permute-start | bytes 98312 | tf_op jit(solution)/shard_map/ppermute | solution.py:75
  37.4 5.2 %collective-permute-start.15 = (bf16[8,4096]{1,0:T(8,128)(2,1)S(1)}, bf16[8,4096]{1,0:T(8,128)(2,1)S(1)}, u32[]{:S(2)}, u32[]{:S(2)}) collective-permute-start(bf16[8,4096]{1,0:T(8,128)(2,1)S(1)} %pair.1.refs_0_), channel_id=1, source_target_pairs={{0,6},{2,4},{4,2},{6,0},{8,14},{10,12},{12,10},{14,8},{1,7},{3,5},... | collective-permute-start | bytes 196616 | tf_op jit(solution)/shard_map/ppermute | solution.py:75
  39.9 4.3 %collective-permute-start.14 = (bf16[8,4096]{1,0:T(8,128)(2,1)S(1)}, bf16[8,4096]{1,0:T(8,128)(2,1)S(1)}, u32[]{:S(2)}, u32[]{:S(2)}) collective-permute-start(bf16[8,4096]{1,0:T(8,128)(2,1)S(1)} %pair.1.refs_0_), channel_id=1, source_target_pairs={{0,4},{2,6},{4,0},{6,2},{8,12},{10,14},{12,8},{14,10},{1,5},{3,7},... | collective-permute-start | bytes 196616 | tf_op jit(solution)/shard_map/ppermute | solution.py:75
  40.8 4.3 %collective-permute-start.13 = (bf16[8,4096]{1,0:T(8,128)(2,1)S(1)}, bf16[8,4096]{1,0:T(8,128)(2,1)S(1)}, u32[]{:S(2)}, u32[]{:S(2)}) collective-permute-start(bf16[8,4096]{1,0:T(8,128)(2,1)S(1)} %pair.1.refs_0_), channel_id=1, source_target_pairs={{0,2},{2,0},{4,6},{6,4},{8,10},{10,8},{12,14},{14,12},{1,3},{3,1},... | collective-permute-start | bytes 196616 | tf_op jit(solution)/shard_map/ppermute | solution.py:75
  49.8 1.3 %collective-permute-start.16 = (bf16[16,2048]{1,0:T(8,128)(2,1)S(1)}, bf16[16,2048]{1,0:T(8,128)(2,1)S(1)}, u32[]{:S(2)}, u32[]{:S(2)}) collective-permute-start(bf16[16,2048]{1,0:T(8,128)(2,1)S(1)} %get-tuple-element.16), channel_id=1, source_target_pairs={{0,1},{1,0},{2,3},{3,2},{4,5},{5,4},{6,7},{7,6},{8,9},{9,8},{10,11... | collective-permute-start | bytes 196616 | tf_op jit(solution)/shard_map/ppermute | solution.py:71

commit v5 on v4

--- a/solution.py
+++ b/solution.py
@@ -72,7 +72,8 @@
 
 
 def hop(x, chips, mask):
-    return lax.ppermute(x, "gy", [(chip, chip ^ mask) for chip in range(chips)])
+    pairs = [(2 * g + c, 2 * (g ^ mask) + 1 - c) for g in range(chips) for c in range(2)]
+    return lax.ppermute(x, ("gy", "gx"), pairs)
 
 
 def stage_kernel(mine_ref, out_ref):
@@ -95,7 +96,9 @@
     )(block)
 
 
-def gather_rows(block, far, chips):
+def gather_rows(block, chips):
+    half = chips // 2
+    far = hop(block, chips, half)
     pair = pl.pallas_call(
         pair_kernel,
         out_shape=jax.ShapeDtypeStruct((2 * block.shape[0], block.shape[1]), block.dtype),
@@ -103,17 +106,18 @@
         out_specs=in_vmem(1)[0],
         compiler_params=pltpu.CompilerParams(vmem_limit_bytes=2 * MIB),
         name="pair",
-    )(hold(block), hold(far))
-    return [pair] + [hop(pair, chips, mask) for mask in range(1, chips // 2)]
+    )(hold(swap(block)), hold(far))
+    return [block, swap(far)] + [hop(pair, chips, mask) for mask in range(1, half)]
 
 
 def gather_early(block, staged, chips):
     half = chips // 2
     far = hop(block, chips, half)
+    other = swap(block)
     masks = range(half - 1, 0, -1)
-    near = {mask: hop(block, chips, mask) for mask in masks}
+    near = {mask: hop(other, chips, mask) for mask in masks}
     beyond = {mask: hop(far, chips, mask) for mask in masks}
-    pieces = [staged, far]
+    pieces = [staged, swap(far)]
     for mask in range(1, half):
         pieces += [near[mask], beyond[mask]]
     return pieces
@@ -130,20 +134,24 @@
         out_ref[head] = value.T.astype(jnp.bfloat16)
 
 
-def merge_kernel(near_ref, far_ref, *out_refs):
-    for mask, out_ref in enumerate(reversed(out_refs)):
+def merge_kernel(near_ref, far_ref, back_ref, *out_refs):
+    back_ref[...] = far_ref[0]
+    for at, out_ref in enumerate(out_refs):
+        mask = len(out_refs) - at
         out_ref[0] = near_ref[mask]
         out_ref[1] = far_ref[mask]
 
 
-def attend_kernel(lengths_ref, *refs):
+def attend_kernel(lengths_ref, near_ref, back_ref, *refs):
     *got_refs, key_ref, value_ref, out_ref, got, wide, tall, flat = refs
-    half = len(got_refs)
+    half = len(got_refs) + 1
     seqs, heads, slots = key_ref.shape[0], key_ref.shape[1], key_ref.shape[2]
     part = got.shape[4]
     chip = lax.axis_index("gy")
-    for mask, got_ref in enumerate(reversed(got_refs)):
-        got[mask] = got_ref[...]
+    got[0, 0] = near_ref[0]
+    got[0, 1] = back_ref[...]
+    for at, got_ref in enumerate(got_refs):
+        got[half - 1 - at] = got_ref[...]
     for other in range(2 * half):
         mask = chip ^ other
         piece = got[mask & (half - 1), mask // half]
@@ -188,7 +196,7 @@
     *x_refs, w_ref, keep_ref, send_ref = refs
     x = jnp.concatenate([x_ref[...] for x_ref in x_refs], axis=0)
     total = x.shape[0]
-    half = len(x_refs)
+    half = total // (2 * rows)
     chip, core = lax.axis_index("gy"), lax.axis_index("gx")
     row = lax.broadcasted_iota(jnp.int32, (total, total), 0)
     column = lax.broadcasted_iota(jnp.int32, (total, total), 1)
@@ -244,20 +252,23 @@
     joined = joined.reshape(kv_local, half, 2, seqs, part)
     near = jnp.stack([joined[:, mask, 0] for mask in range(half)])
     far = hop(jnp.stack([joined[:, mask, 1] for mask in range(half)]), chips, half)
-    *far_first, mine = pl.pallas_call(
+    piece = jax.ShapeDtypeStruct((kv_local, seqs, part), jnp.bfloat16)
+    pair = jax.ShapeDtypeStruct((2, kv_local, seqs, part), jnp.bfloat16)
+    back, *pairs = pl.pallas_call(
         merge_kernel,
-        out_shape=(jax.ShapeDtypeStruct((2, kv_local, seqs, part), jnp.bfloat16),) * half,
+        out_shape=(piece,) + (pair,) * (half - 1),
         in_specs=in_vmem(2),
         out_specs=tuple(in_vmem(half)),
         compiler_params=pltpu.CompilerParams(vmem_limit_bytes=2 * MIB),
         name="merge",
-    )(hold(near), hold(far))
-    got = [hop(piece, chips, half - 1 - at) for at, piece in enumerate(far_first)] + [mine]
+    )(hold(swap(near)), hold(far))
+    got = [hop(pair, chips, half - 1 - at) for at, pair in enumerate(pairs)]
+    got = [near, swap(back)] + got
 
     attended = pl.pallas_call(
         attend_kernel,
         out_shape=jax.ShapeDtypeStruct((seqs, feats), jnp.bfloat16),
-        in_specs=[pl.BlockSpec(memory_space=pltpu.SMEM)] + in_vmem(half + 2),
+        in_specs=[pl.BlockSpec(memory_space=pltpu.SMEM)] + in_vmem(half + 3),
         out_specs=in_vmem(1)[0],
         scratch_shapes=[
             pltpu.VMEM((half, 2, kv_local, seqs, part), jnp.bfloat16),
@@ -269,12 +280,12 @@
         name="attend",
     )(lengths, *[hold(piece) for piece in got], key_cache, value_cache)
 
-    pieces = [hold(piece) for piece in gather_rows(attended, hop(attended, chips, half), chips)]
+    pieces = [hold(piece) for piece in gather_rows(attended, chips)]
     piece = jax.ShapeDtypeStruct((rows // 2, out_cols), jnp.bfloat16)
     keep, send = pl.pallas_call(
         functools.partial(output_kernel, rows=seqs),
         out_shape=(piece, piece),
-        in_specs=in_vmem(half + 1),
+        in_specs=in_vmem(half + 2),
         out_specs=tuple(in_vmem(2)),
         compiler_params=limits,
         name="output",

time: 51.9 us -> 50.3 us (0.969)
  waiting for transfers between devices: 15.4 us -> 13 us
  starting transfers between devices: 22.9 us -> 23.7 us
    ppermute x15, waiting for transfers between devices: 14.2 us -> 9.83 us  [hop(): return lax.ppermute(x, ('gy', 'gx'), pairs)]
    ppermute x2 -> x8, starting transfers between devices: 0.12 us -> 2.18 us  [swap(): return lax.ppermute(x, 'gx', [(0, 1), (1, 0)])]
    ppermute x2 -> x8, waiting for transfers between devices: 1.24 us -> 3.2 us  [swap(): return lax.ppermute(x, 'gx', [(0, 1), (1, 0)])]
    ppermute x15, starting transfers between devices: 22.8 us -> 21.6 us  [hop(): return lax.ppermute(x, ('gy', 'gx'), pairs)]
  transfers between devices with their start and end apart: 17 -> 23, of which waited for: 13 -> 12; matrix products, arithmetic and copies ran while one was open for 0% -> 0% of each run, Pallas kernels for 5% -> 5%
where the time goes in v5:
time: 50.3 us; the launch traced here: 50.2 us
  starting transfers between devices  23.7 us (47%)
  waiting for transfers between devices  13 us (26%)
  Pallas kernels  11.5 us (23%)
  local copies, waits for them, and re-layouts  0.99 us (2%)
  other arithmetic  0.72 us (1%)
    ppermute x15, starting transfers between devices, hop(): return lax.ppermute(x, ('gy', 'gx'), pairs)  21.6 us
    ppermute x15, waiting for transfers between devices, hop(): return lax.ppermute(x, ('gy', 'gx'), pairs)  9.83 us
    pallas_call x2, Pallas kernels, project(): pl.pallas_call(functools.partial(project_kernel, swapped=swapped), out_sh...  5.28 us
    pallas_call x1, Pallas kernels, local(): pl.pallas_call(functools.partial(output_kernel, rows=seqs), out_shape=(pi...  4.65 us
    ppermute x8, waiting for transfers between devices, swap(): return lax.ppermute(x, 'gx', [(0, 1), (1, 0)])  3.2 us
    ppermute x8, starting transfers between devices, swap(): return lax.ppermute(x, 'gx', [(0, 1), (1, 0)])  2.18 us
    pallas_call x1, Pallas kernels, local(): pl.pallas_call(attend_kernel, out_shape=jax.ShapeDtypeStruct((seqs, feats...  1.52 us
  transfers between devices with their start and end apart: 23, of which 12 were waited for; matrix products, arithmetic and copies ran while one was open for 0% of the time, Pallas kernels for 5%

profile of v5, /device:TPU:0, one launch (start us, length us, event | category | flops | bytes accessed | tf_op | source)
XLA Modules:
  0.0 50.2 jit_solution(17186665735156623436)
XLA Ops:
  0.0 0.5 collective-permute-start.2
  0.5 3.7 %collective-permute-start = (bf16[4,8192]{1,0:T(4,128)(2,1)}, bf16[4,8192]{1,0:T(4,128)(2,1)S(1)}, u32[]{:S(2)}, u32[]{:S(2)}) collective-permute-start(bf16[4,8192]{1,0:T(4,128)(2,1)} %mine_ref.1), channel_id=1, source_target_pairs={{0,9},{1,8},{2,11},{3,10},{4,13},{5,12},{6,15},{7,14},{8,1},{9,0},... | collective-permute-start | bytes 196616 | tf_op jit(solution)/shard_map/ppermute | solution.py:76
  4.2 2.2 %collective-permute-start.7 = (bf16[4,8192]{1,0:T(4,128)(2,1)S(1)}, bf16[4,8192]{1,0:T(4,128)(2,1)S(1)}, u32[]{:S(2)}, u32[]{:S(2)}) collective-permute-start(bf16[4,8192]{1,0:T(4,128)(2,1)S(1)} %collective-permute-done.2), channel_id=1, source_target_pairs={{0,7},{1,6},{2,5},{3,4},{4,3},{5,2},{6,1},{7,0},{8,15},{9,14},{10,... | collective-permute-start | bytes 196616 | tf_op jit(solution)/shard_map/ppermute | solution.py:76
  6.3 0.5 collective-permute-start.5
  7.0 1.2 %collective-permute-done = bf16[4,8192]{1,0:T(4,128)(2,1)S(1)} collective-permute-done((bf16[4,8192]{1,0:T(4,128)(2,1)}, bf16[4,8192]{1,0:T(4,128)(2,1)S(1)}, u32[]{:S(2)}, u32[]{:S(2)}) %collective-permute-start) | collective-permute-done | bytes 65568 | tf_op jit(solution)/shard_map/ppermute | solution.py:76
  8.3 1.6 %collective-permute-start.8 = (bf16[4,8192]{1,0:T(4,128)(2,1)S(1)}, bf16[4,8192]{1,0:T(4,128)(2,1)S(1)}, u32[]{:S(2)}, u32[]{:S(2)}) collective-permute-start(bf16[4,8192]{1,0:T(4,128)(2,1)S(1)} %collective-permute-done), channel_id=1, source_target_pairs={{0,7},{1,6},{2,5},{3,4},{4,3},{5,2},{6,1},{7,0},{8,15},{9,14},{10,... | collective-permute-start | bytes 196616 | tf_op jit(solution)/shard_map/ppermute | solution.py:76
  9.8 1.5 %collective-permute-start.4 = (bf16[4,8192]{1,0:T(4,128)(2,1)S(1)}, bf16[4,8192]{1,0:T(4,128)(2,1)S(1)}, u32[]{:S(2)}, u32[]{:S(2)}) collective-permute-start(bf16[4,8192]{1,0:T(4,128)(2,1)S(1)} %collective-permute-done), channel_id=1, source_target_pairs={{0,3},{1,2},{2,1},{3,0},{4,7},{5,6},{6,5},{7,4},{8,11},{9,10},{10,... | collective-permute-start | bytes 196616 | tf_op jit(solution)/shard_map/ppermute | solution.py:76
  11.4 0.2 collective-permute-start.1
  11.6 0.8 %copy-done.4 = bf16[4,8192]{1,0:T(4,128)(2,1)S(1)} copy-done((bf16[4,8192]{1,0:T(4,128)(2,1)S(1)}, bf16[4,8192]{1,0:T(4,128)(2,1)}, u32[]{:S(2)}) %copy-start.4) | copy-done | bytes 65560
  12.5 0.7 %collective-permute-done.8.refs_7_ = bf16[4,8192]{1,0:T(4,128)(2,1)S(1)} collective-permute-done((bf16[4,8192]{1,0:T(4,128)(2,1)S(1)}, bf16[4,8192]{1,0:T(4,128)(2,1)S(1)}, u32[]{:S(2)}, u32[]{:S(2)}) %collective-permute-start.8) | collective-permute-done | bytes 65568 | tf_op jit(solution)/shard_map/ppermute | solution.py:76
  13.2 1.0 %collective-permute-done.6.refs_5_ = bf16[4,8192]{1,0:T(4,128)(2,1)S(1)} collective-permute-done((bf16[4,8192]{1,0:T(4,128)(2,1)S(1)}, bf16[4,8192]{1,0:T(4,128)(2,1)S(1)}, u32[]{:S(2)}, u32[]{:S(2)}) %collective-permute-start.6) | collective-permute-done | bytes 65568 | tf_op jit(solution)/shard_map/ppermute | solution.py:76
  14.3 2.6 %project.3 = bf16[2,32,288]{2,1,0:T(8,128)(2,1)S(1)} custom-call(bf16[4,8192]{1,0:T(4,128)(2,1)S(1)} %stage.1.refs_0_, bf16[4,8192]{1,0:T(4,128)(2,1)S(1)} %collective-permute-done.1.refs_1_, bf16[4,8192]{1,0:T(4,128)(2,1)S(1)} %collective-permute-done.3.refs_2_, bf16[4,8192]{1,0:T(4,128)(2,1)S(1)} %collective-permute-done.4.refs_3_, ...), custom_call_target="tpu_custom_call" | custom-call | flops 2415919104 | bytes 1048576 | tf_op jit(solution)/shard_map/project/pallas_call | solution.py:238
  16.9 0.7 %collective-permute-start.9 = (bf16[2,32,288]{2,1,0:T(8,128)(2,1)S(1)}, bf16[2,32,288]{2,1,0:T(8,128)(2,1)S(1)}, u32[]{:S(2)}, u32[]{:S(2)}) collective-permute-start(bf16[2,32,288]{2,1,0:T(8,128)(2,1)S(1)} %project.3), channel_id=1, source_target_pairs={{0,1},{1,0},{2,3},{3,2},{4,5},{5,4},{6,7},{7,6},{8,9},{9,8},{10,11... | collective-permute-start | bytes 110600 | tf_op jit(solution)/shard_map/ppermute | solution.py:71
  17.7 2.6 %project.2 = bf16[2,32,288]{2,1,0:T(8,128)(2,1)S(1)} custom-call(bf16[4,8192]{1,0:T(4,128)(2,1)S(1)} %stage.1.refs_0_, bf16[4,8192]{1,0:T(4,128)(2,1)S(1)} %collective-permute-done.1.refs_1_, bf16[4,8192]{1,0:T(4,128)(2,1)S(1)} %collective-permute-done.3.refs_2_, bf16[4,8192]{1,0:T(4,128)(2,1)S(1)} %collective-permute-done.4.refs_3_, ...), custom_call_target="tpu_custom_call" | custom-call | flops 2415919104 | bytes 1048576 | tf_op jit(solution)/shard_map/project/pallas_call | solution.py:238
  20.6 2.7 %collective-permute-start.11 = (bf16[4,2,4,288]{3,2,1,0:T(4,128)(2,1)S(1)}, bf16[4,2,4,288]{3,2,1,0:T(4,128)(2,1)S(1)}, u32[]{:S(2)}, u32[]{:S(2)}) collective-permute-start(bf16[4,2,4,288]{3,2,1,0:T(4,128)(2,1)S(1)} %pad_maximum_fusion.1), channel_id=1, source_target_pairs={{0,9},{1,8},{2,11},{3,10},{4,13},{5,12},{6,15},{7,14},{8,1},{9,0},... | collective-permute-start | bytes 55304 | tf_op jit(solution)/shard_map/ppermute | solution.py:76
  23.3 1.5 %collective-permute-done.11.far_ref = bf16[4,2,4,288]{3,2,1,0:T(4,128)(2,1)S(1)} collective-permute-done((bf16[4,2,4,288]{3,2,1,0:T(4,128)(2,1)S(1)}, bf16[4,2,4,288]{3,2,1,0:T(4,128)(2,1)S(1)}, u32[]{:S(2)}, u32[]{:S(2)}) %collective-permute-start.11) | collective-permute-done | bytes 18464 | tf_op jit(solution)/shard_map/ppermute | solution.py:76
  24.9 2.9 %collective-permute-start.13 = (bf16[2,2,4,288]{3,2,1,0:T(4,128)(2,1)S(1)}, bf16[2,2,4,288]{3,2,1,0:T(4,128)(2,1)S(1)}, u32[]{:S(2)}, u32[]{:S(2)}) collective-permute-start(bf16[2,2,4,288]{3,2,1,0:T(4,128)(2,1)S(1)} %get-tuple-element.12), channel_id=1, source_target_pairs={{0,7},{1,6},{2,5},{3,4},{4,3},{5,2},{6,1},{7,0},{8,15},{9,14},{10,... | collective-permute-start | bytes 27656 | tf_op jit(solution)/shard_map/ppermute | solution.py:76
  27.7 0.5 collective-permute-start.15
  28.5 0.9 %collective-permute-done.12.back_ref = bf16[2,4,288]{2,1,0:T(4,128)(2,1)S(1)} collective-permute-done((bf16[2,4,288]{2,1,0:T(4,128)(2,1)S(1)}, bf16[2,4,288]{2,1,0:T(4,128)(2,1)S(1)}, u32[]{:S(2)}, u32[]{:S(2)}) %collective-permute-start.12) | collective-permute-done | bytes 4640 | tf_op jit(solution)/shard_map/ppermute | solution.py:71
  29.4 1.5 %collective-permute-done.14.refs_1_ = bf16[2,2,4,288]{3,2,1,0:T(4,128)(2,1)S(1)} collective-permute-done((bf16[2,2,4,288]{3,2,1,0:T(4,128)(2,1)S(1)}, bf16[2,2,4,288]{3,2,1,0:T(4,128)(2,1)S(1)}, u32[]{:S(2)}, u32[]{:S(2)}) %collective-permute-start.14) | collective-permute-done | bytes 9248 | tf_op jit(solution)/shard_map/ppermute | solution.py:76
  30.9 1.5 %attend.1.refs_0_ = bf16[4,4096]{1,0:T(4,128)(2,1)S(1)} custom-call(s32[4]{0:T(128)S(1)} %copy-done.3, bf16[4,2,4,288]{3,2,1,0:T(4,128)(2,1)S(1)} %pad_maximum_fusion.near_ref, bf16[2,4,288]{2,1,0:T(4,128)(2,1)S(1)} %collective-permute-done.12.back_ref, bf16[2,2,4,288]{3,2,1,0:T(4,128)(2,1)S(1)} %collective-permute-done.13.refs_0_, ...), custom_call_target="tpu_custom_call" | custom-call | tf_op jit(solution)/shard_map/attend/pallas_call | solution.py:268
  32.6 2.6 %collective-permute-start.16 = (bf16[4,4096]{1,0:T(4,128)(2,1)S(1)}, bf16[4,4096]{1,0:T(4,128)(2,1)S(1)}, u32[]{:S(2)}, u32[]{:S(2)}) collective-permute-start(bf16[4,4096]{1,0:T(4,128)(2,1)S(1)} %attend.1.refs_0_), channel_id=1, source_target_pairs={{0,9},{1,8},{2,11},{3,10},{4,13},{5,12},{6,15},{7,14},{8,1},{9,0},... | collective-permute-start | bytes 98312 | tf_op jit(solution)/shard_map/ppermute | solution.py:76
  35.2 1.7 %collective-permute-done.16.theirs_ref = bf16[4,4096]{1,0:T(4,128)(2,1)S(1)} collective-permute-done((bf16[4,4096]{1,0:T(4,128)(2,1)S(1)}, bf16[4,4096]{1,0:T(4,128)(2,1)S(1)}, u32[]{:S(2)}, u32[]{:S(2)}) %collective-permute-start.16) | collective-permute-done | bytes 32800 | tf_op jit(solution)/shard_map/ppermute | solution.py:76
  36.9 1.9 %collective-permute-start.21 = (bf16[8,4096]{1,0:T(8,128)(2,1)S(1)}, bf16[8,4096]{1,0:T(8,128)(2,1)S(1)}, u32[]{:S(2)}, u32[]{:S(2)}) collective-permute-start(bf16[8,4096]{1,0:T(8,128)(2,1)S(1)} %pair.1), channel_id=1, source_target_pairs={{0,7},{1,6},{2,5},{3,4},{4,3},{5,2},{6,1},{7,0},{8,15},{9,14},{10,... | collective-permute-start | bytes 196616 | tf_op jit(solution)/shard_map/ppermute | solution.py:76
  38.8 1.4 %collective-permute-start.19 = (bf16[8,4096]{1,0:T(8,128)(2,1)S(1)}, bf16[8,4096]{1,0:T(8,128)(2,1)S(1)}, u32[]{:S(2)}, u32[]{:S(2)}) collective-permute-start(bf16[8,4096]{1,0:T(8,128)(2,1)S(1)} %pair.1), channel_id=1, source_target_pairs={{0,3},{1,2},{2,1},{3,0},{4,7},{5,6},{6,5},{7,4},{8,11},{9,10},{10,... | collective-permute-start | bytes 196616 | tf_op jit(solution)/shard_map/ppermute | solution.py:76
  40.3 1.1 %collective-permute-done.17.refs_1_ = bf16[4,4096]{1,0:T(4,128)(2,1)S(1)} collective-permute-done((bf16[4,4096]{1,0:T(4,128)(2,1)S(1)}, bf16[4,4096]{1,0:T(4,128)(2,1)S(1)}, u32[]{:S(2)}, u32[]{:S(2)}) %collective-permute-start.17) | collective-permute-done | bytes 32800 | tf_op jit(solution)/shard_map/ppermute | solution.py:71
  41.4 0.4 collective-permute-done.21.refs_4_
  41.8 0.9 %collective-permute-done.20.refs_3_ = bf16[8,4096]{1,0:T(8,128)(2,1)S(1)} collective-permute-done((bf16[8,4096]{1,0:T(8,128)(2,1)S(1)}, bf16[8,4096]{1,0:T(8,128)(2,1)S(1)}, u32[]{:S(2)}, u32[]{:S(2)}) %collective-permute-start.20) | collective-permute-done | bytes 65568 | tf_op jit(solution)/shard_map/ppermute | solution.py:76
  42.7 0.8 %collective-permute-done.19.refs_2_ = bf16[8,4096]{1,0:T(8,128)(2,1)S(1)} collective-permute-done((bf16[8,4096]{1,0:T(8,128)(2,1)S(1)}, bf16[8,4096]{1,0:T(8,128)(2,1)S(1)}, u32[]{:S(2)}, u32[]{:S(2)}) %collective-permute-start.19) | collective-permute-done | bytes 65568 | tf_op jit(solution)/shard_map/ppermute | solution.py:76
  43.6 4.7 %output.1 = (bf16[16,2048]{1,0:T(8,128)(2,1)S(1)}, bf16[16,2048]{1,0:T(8,128)(2,1)S(1)}) custom-call(bf16[4,4096]{1,0:T(4,128)(2,1)S(1)} %attend.1.refs_0_, bf16[4,4096]{1,0:T(4,128)(2,1)S(1)} %collective-permute-done.17.refs_1_, bf16[8,4096]{1,0:T(8,128)(2,1)S(1)} %collective-permute-done.19.refs_2_, bf16[8,4096]{1,0:T(8,128)(2,1)S(1)} %collective-permute-done.20.refs_3_, ...), custom_call_target="tpu_custom_call" | custom-call | tf_op jit(solution)/shard_map/output/pallas_call | solution.py:285
  48.4 1.1 %collective-permute-done.22 = bf16[16,2048]{1,0:T(8,128)(2,1)S(1)} collective-permute-done((bf16[16,2048]{1,0:T(8,128)(2,1)S(1)}, bf16[16,2048]{1,0:T(8,128)(2,1)S(1)}, u32[]{:S(2)}, u32[]{:S(2)}) %collective-permute-start.22) | collective-permute-done | bytes 65568 | tf_op jit(solution)/shard_map/ppermute | solution.py:71
  49.5 0.6 %add_convert_fusion = bf16[16,2048]{1,0:T(8,128)(2,1)} fusion(bf16[16,2048]{1,0:T(8,128)(2,1)S(1)} %collective-permute-done.22, bf16[16,2048]{1,0:T(8,128)(2,1)S(1)} %get-tuple-element.15), kind=kLoop, calls=%fused_computation | loop fusion | flops 131072 | bytes 196608 | tf_op jit(solution)/shard_map/convert_element_type | solution.py:293
  (50 shorter events, 1.4 us)
Async XLA Ops:
  0.0 14.3 %copy-start = (bf16[4,288,8192]{2,1,0:T(8,128)(2,1)S(1)}, bf16[4,288,8192]{2,1,0:T(8,128)(2,1)}, u32[]{:S(2)}) copy-start(bf16[4,288,8192]{2,1,0:T(8,128)(2,1)} %refs_8_.3) | copy-start | bytes 56623108
  0.0 4.2 %collective-permute-start.2 = (bf16[4,8192]{1,0:T(4,128)(2,1)}, bf16[4,8192]{1,0:T(4,128)(2,1)S(1)}, u32[]{:S(2)}, u32[]{:S(2)}) collective-permute-start(bf16[4,8192]{1,0:T(4,128)(2,1)} %mine_ref.1), channel_id=1, source_target_pairs={{0,1},{1,0},{2,3},{3,2},{4,5},{5,4},{6,7},{7,6},{8,9},{9,8},{10,11... | collective-permute-start | bytes 196616 | tf_op jit(solution)/shard_map/ppermute | solution.py:71
  0.5 7.8 %collective-permute-start = (bf16[4,8192]{1,0:T(4,128)(2,1)}, bf16[4,8192]{1,0:T(4,128)(2,1)S(1)}, u32[]{:S(2)}, u32[]{:S(2)}) collective-permute-start(bf16[4,8192]{1,0:T(4,128)(2,1)} %mine_ref.1), channel_id=1, source_target_pairs={{0,9},{1,8},{2,11},{3,10},{4,13},{5,12},{6,15},{7,14},{8,1},{9,0},... | collective-permute-start | bytes 196616 | tf_op jit(solution)/shard_map/ppermute | solution.py:76
  4.2 5.7 %collective-permute-start.7 = (bf16[4,8192]{1,0:T(4,128)(2,1)S(1)}, bf16[4,8192]{1,0:T(4,128)(2,1)S(1)}, u32[]{:S(2)}, u32[]{:S(2)}) collective-permute-start(bf16[4,8192]{1,0:T(4,128)(2,1)S(1)} %collective-permute-done.2), channel_id=1, source_target_pairs={{0,7},{1,6},{2,5},{3,4},{4,3},{5,2},{6,1},{7,0},{8,15},{9,14},{10,... | collective-permute-start | bytes 196616 | tf_op jit(solution)/shard_map/ppermute | solution.py:76
  6.3 5.0 %collective-permute-start.5 = (bf16[4,8192]{1,0:T(4,128)(2,1)S(1)}, bf16[4,8192]{1,0:T(4,128)(2,1)S(1)}, u32[]{:S(2)}, u32[]{:S(2)}) collective-permute-start(bf16[4,8192]{1,0:T(4,128)(2,1)S(1)} %collective-permute-done.2), channel_id=1, source_target_pairs={{0,5},{1,4},{2,7},{3,6},{4,1},{5,0},{6,3},{7,2},{8,13},{9,12},{10,... | collective-permute-start | bytes 196616 | tf_op jit(solution)/shard_map/ppermute | solution.py:76
  6.8 5.7 %collective-permute-start.3 = (bf16[4,8192]{1,0:T(4,128)(2,1)S(1)}, bf16[4,8192]{1,0:T(4,128)(2,1)S(1)}, u32[]{:S(2)}, u32[]{:S(2)}) collective-permute-start(bf16[4,8192]{1,0:T(4,128)(2,1)S(1)} %collective-permute-done.2), channel_id=1, source_target_pairs={{0,3},{1,2},{2,1},{3,0},{4,7},{5,6},{6,5},{7,4},{8,11},{9,10},{10,... | collective-permute-start | bytes 196616 | tf_op jit(solution)/shard_map/ppermute | solution.py:76
  8.3 5.0 %collective-permute-start.8 = (bf16[4,8192]{1,0:T(4,128)(2,1)S(1)}, bf16[4,8192]{1,0:T(4,128)(2,1)S(1)}, u32[]{:S(2)}, u32[]{:S(2)}) collective-permute-start(bf16[4,8192]{1,0:T(4,128)(2,1)S(1)} %collective-permute-done), channel_id=1, source_target_pairs={{0,7},{1,6},{2,5},{3,4},{4,3},{5,2},{6,1},{7,0},{8,15},{9,14},{10,... | collective-permute-start | bytes 196616 | tf_op jit(solution)/shard_map/ppermute | solution.py:76
  9.8 4.4 %collective-permute-start.6 = (bf16[4,8192]{1,0:T(4,128)(2,1)S(1)}, bf16[4,8192]{1,0:T(4,128)(2,1)S(1)}, u32[]{:S(2)}, u32[]{:S(2)}) collective-permute-start(bf16[4,8192]{1,0:T(4,128)(2,1)S(1)} %collective-permute-done), channel_id=1, source_target_pairs={{0,5},{1,4},{2,7},{3,6},{4,1},{5,0},{6,3},{7,2},{8,13},{9,12},{10,... | collective-permute-start | bytes 196616 | tf_op jit(solution)/shard_map/ppermute | solution.py:76
  9.8 4.4 %collective-permute-start.4 = (bf16[4,8192]{1,0:T(4,128)(2,1)S(1)}, bf16[4,8192]{1,0:T(4,128)(2,1)S(1)}, u32[]{:S(2)}, u32[]{:S(2)}) collective-permute-start(bf16[4,8192]{1,0:T(4,128)(2,1)S(1)} %collective-permute-done), channel_id=1, source_target_pairs={{0,3},{1,2},{2,1},{3,0},{4,7},{5,6},{6,5},{7,4},{8,11},{9,10},{10,... | collective-permute-start | bytes 196616 | tf_op jit(solution)/shard_map/ppermute | solution.py:76
  11.4 2.9 %collective-permute-start.1 = (bf16[4,8192]{1,0:T(4,128)(2,1)S(1)}, bf16[4,8192]{1,0:T(4,128)(2,1)S(1)}, u32[]{:S(2)}, u32[]{:S(2)}) collective-permute-start(bf16[4,8192]{1,0:T(4,128)(2,1)S(1)} %collective-permute-done), channel_id=1, source_target_pairs={{0,1},{1,0},{2,3},{3,2},{4,5},{5,4},{6,7},{7,6},{8,9},{9,8},{10,11... | collective-permute-start | bytes 196616 | tf_op jit(solution)/shard_map/ppermute | solution.py:71
  11.6 0.8 %copy-start.4 = (bf16[4,8192]{1,0:T(4,128)(2,1)S(1)}, bf16[4,8192]{1,0:T(4,128)(2,1)}, u32[]{:S(2)}) copy-start(bf16[4,8192]{1,0:T(4,128)(2,1)} %mine_ref.1) | copy-start | bytes 196612
  12.5 18.4 %copy-start.1 = (bf16[4,2,512,128]{3,2,1,0:T(8,128)(2,1)S(1)}, bf16[4,2,512,128]{3,2,1,0:T(8,128)(2,1)}, u32[]{:S(2)}) copy-start(bf16[4,2,512,128]{3,2,1,0:T(8,128)(2,1)} %refs_3_.1) | copy-start | bytes 3145732
  12.5 18.4 %copy-start.2 = (bf16[4,2,512,128]{3,2,1,0:T(8,128)(2,1)S(1)}, bf16[4,2,512,128]{3,2,1,0:T(8,128)(2,1)}, u32[]{:S(2)}) copy-start(bf16[4,2,512,128]{3,2,1,0:T(8,128)(2,1)} %refs_4_.1) | copy-start | bytes 3145732
  12.5 18.4 %copy-start.3 = (s32[4]{0:T(128)S(1)}, s32[4]{0:T(128)}, u32[]{:S(2)}) copy-start(s32[4]{0:T(128)} %lengths_ref.1) | copy-start | bytes 52
  12.5 31.1 %slice-start = ((s8[16777216]{0:T(1024)(128)(4,1)}), s8[4194304]{0:T(1024)(128)(4,1)S(1)}, s32[]{:S(2)}) async-start(s8[16777216]{0:T(1024)(128)(4,1)} %bitcast.17), calls=%async_computation | async-start | bytes 8388608
  12.5 31.1 %slice-start.1 = ((s8[16777216]{0:T(1024)(128)(4,1)}), s8[4194304]{0:T(1024)(128)(4,1)S(1)}, s32[]{:S(2)}) async-start(s8[16777216]{0:T(1024)(128)(4,1)} %bitcast.17), calls=%async_computation.1 | async-start | bytes 8388608
  16.9 26.6 %slice-start.2 = ((s8[16777216]{0:T(1024)(128)(4,1)}), s8[4194304]{0:T(1024)(128)(4,1)S(1)}, s32[]{:S(2)}) async-start(s8[16777216]{0:T(1024)(128)(4,1)} %bitcast.17), calls=%async_computation.2 | async-start | bytes 8388608
  16.9 26.6 %slice-start.3 = ((s8[16777216]{0:T(1024)(128)(4,1)}), s8[4194304]{0:T(1024)(128)(4,1)S(1)}, s32[]{:S(2)}) async-start(s8[16777216]{0:T(1024)(128)(4,1)} %bitcast.17), calls=%async_computation.3 | async-start | bytes 8388608
  16.9 3.4 %collective-permute-start.9 = (bf16[2,32,288]{2,1,0:T(8,128)(2,1)S(1)}, bf16[2,32,288]{2,1,0:T(8,128)(2,1)S(1)}, u32[]{:S(2)}, u32[]{:S(2)}) collective-permute-start(bf16[2,32,288]{2,1,0:T(8,128)(2,1)S(1)} %project.3), channel_id=1, source_target_pairs={{0,1},{1,0},{2,3},{3,2},{4,5},{5,4},{6,7},{7,6},{8,9},{9,8},{10,11... | collective-permute-start | bytes 110600 | tf_op jit(solution)/shard_map/ppermute | solution.py:71
  20.5 2.8 %collective-permute-start.10 = (bf16[4,2,4,288]{3,2,1,0:T(4,128)(2,1)S(1)}, bf16[4,2,4,288]{3,2,1,0:T(4,128)(2,1)S(1)}, u32[]{:S(2)}, u32[]{:S(2)}) collective-permute-start(bf16[4,2,4,288]{3,2,1,0:T(4,128)(2,1)S(1)} %pad_maximum_fusion.near_ref), channel_id=1, source_target_pairs={{0,1},{1,0},{2,3},{3,2},{4,5},{5,4},{6,7},{7,6},{8,9},{9,8},{10,11... | collective-permute-start | bytes 55304 | tf_op jit(solution)/shard_map/ppermute | solution.py:71
  20.6 4.2 %collective-permute-start.11 = (bf16[4,2,4,288]{3,2,1,0:T(4,128)(2,1)S(1)}, bf16[4,2,4,288]{3,2,1,0:T(4,128)(2,1)S(1)}, u32[]{:S(2)}, u32[]{:S(2)}) collective-permute-start(bf16[4,2,4,288]{3,2,1,0:T(4,128)(2,1)S(1)} %pad_maximum_fusion.1), channel_id=1, source_target_pairs={{0,9},{1,8},{2,11},{3,10},{4,13},{5,12},{6,15},{7,14},{8,1},{9,0},... | collective-permute-start | bytes 55304 | tf_op jit(solution)/shard_map/ppermute | solution.py:76
  24.9 4.5 %collective-permute-start.13 = (bf16[2,2,4,288]{3,2,1,0:T(4,128)(2,1)S(1)}, bf16[2,2,4,288]{3,2,1,0:T(4,128)(2,1)S(1)}, u32[]{:S(2)}, u32[]{:S(2)}) collective-permute-start(bf16[2,2,4,288]{3,2,1,0:T(4,128)(2,1)S(1)} %get-tuple-element.12), channel_id=1, source_target_pairs={{0,7},{1,6},{2,5},{3,4},{4,3},{5,2},{6,1},{7,0},{8,15},{9,14},{10,... | collective-permute-start | bytes 27656 | tf_op jit(solution)/shard_map/ppermute | solution.py:76
  27.7 3.1 %collective-permute-start.14 = (bf16[2,2,4,288]{3,2,1,0:T(4,128)(2,1)S(1)}, bf16[2,2,4,288]{3,2,1,0:T(4,128)(2,1)S(1)}, u32[]{:S(2)}, u32[]{:S(2)}) collective-permute-start(bf16[2,2,4,288]{3,2,1,0:T(4,128)(2,1)S(1)} %get-tuple-element.13), channel_id=1, source_target_pairs={{0,5},{1,4},{2,7},{3,6},{4,1},{5,0},{6,3},{7,2},{8,13},{9,12},{10,... | collective-permute-start | bytes 27656 | tf_op jit(solution)/shard_map/ppermute | solution.py:76
  27.7 3.1 %collective-permute-start.15 = (bf16[2,2,4,288]{3,2,1,0:T(4,128)(2,1)S(1)}, bf16[2,2,4,288]{3,2,1,0:T(4,128)(2,1)S(1)}, u32[]{:S(2)}, u32[]{:S(2)}) collective-permute-start(bf16[2,2,4,288]{3,2,1,0:T(4,128)(2,1)S(1)} %get-tuple-element.14), channel_id=1, source_target_pairs={{0,3},{1,2},{2,1},{3,0},{4,7},{5,6},{6,5},{7,4},{8,11},{9,10},{10,... | collective-permute-start | bytes 27656 | tf_op jit(solution)/shard_map/ppermute | solution.py:76
  28.2 1.2 %collective-permute-start.12 = (bf16[2,4,288]{2,1,0:T(4,128)(2,1)S(1)}, bf16[2,4,288]{2,1,0:T(4,128)(2,1)S(1)}, u32[]{:S(2)}, u32[]{:S(2)}) collective-permute-start(bf16[2,4,288]{2,1,0:T(4,128)(2,1)S(1)} %get-tuple-element.11), channel_id=1, source_target_pairs={{0,1},{1,0},{2,3},{3,2},{4,5},{5,4},{6,7},{7,6},{8,9},{9,8},{10,11... | collective-permute-start | bytes 13832 | tf_op jit(solution)/shard_map/ppermute | solution.py:71
  32.4 2.8 %collective-permute-start.18 = (bf16[4,4096]{1,0:T(4,128)(2,1)S(1)}, bf16[4,4096]{1,0:T(4,128)(2,1)S(1)}, u32[]{:S(2)}, u32[]{:S(2)}) collective-permute-start(bf16[4,4096]{1,0:T(4,128)(2,1)S(1)} %attend.1.refs_0_), channel_id=1, source_target_pairs={{0,1},{1,0},{2,3},{3,2},{4,5},{5,4},{6,7},{7,6},{8,9},{9,8},{10,11... | collective-permute-start | bytes 98312 | tf_op jit(solution)/shard_map/ppermute | solution.py:71
  32.6 4.3 %collective-permute-start.16 = (bf16[4,4096]{1,0:T(4,128)(2,1)S(1)}, bf16[4,4096]{1,0:T(4,128)(2,1)S(1)}, u32[]{:S(2)}, u32[]{:S(2)}) collective-permute-start(bf16[4,4096]{1,0:T(4,128)(2,1)S(1)} %attend.1.refs_0_), channel_id=1, source_target_pairs={{0,9},{1,8},{2,11},{3,10},{4,13},{5,12},{6,15},{7,14},{8,1},{9,0},... | collective-permute-start | bytes 98312 | tf_op jit(solution)/shard_map/ppermute | solution.py:76
  36.9 4.9 %collective-permute-start.21 = (bf16[8,4096]{1,0:T(8,128)(2,1)S(1)}, bf16[8,4096]{1,0:T(8,128)(2,1)S(1)}, u32[]{:S(2)}, u32[]{:S(2)}) collective-permute-start(bf16[8,4096]{1,0:T(8,128)(2,1)S(1)} %pair.1), channel_id=1, source_target_pairs={{0,7},{1,6},{2,5},{3,4},{4,3},{5,2},{6,1},{7,0},{8,15},{9,14},{10,... | collective-permute-start | bytes 196616 | tf_op jit(solution)/shard_map/ppermute | solution.py:76
  38.8 3.9 %collective-permute-start.20 = (bf16[8,4096]{1,0:T(8,128)(2,1)S(1)}, bf16[8,4096]{1,0:T(8,128)(2,1)S(1)}, u32[]{:S(2)}, u32[]{:S(2)}) collective-permute-start(bf16[8,4096]{1,0:T(8,128)(2,1)S(1)} %pair.1), channel_id=1, source_target_pairs={{0,5},{1,4},{2,7},{3,6},{4,1},{5,0},{6,3},{7,2},{8,13},{9,12},{10,... | collective-permute-start | bytes 196616 | tf_op jit(solution)/shard_map/ppermute | solution.py:76
  38.8 4.7 %collective-permute-start.19 = (bf16[8,4096]{1,0:T(8,128)(2,1)S(1)}, bf16[8,4096]{1,0:T(8,128)(2,1)S(1)}, u32[]{:S(2)}, u32[]{:S(2)}) collective-permute-start(bf16[8,4096]{1,0:T(8,128)(2,1)S(1)} %pair.1), channel_id=1, source_target_pairs={{0,3},{1,2},{2,1},{3,0},{4,7},{5,6},{6,5},{7,4},{8,11},{9,10},{10,... | collective-permute-start | bytes 196616 | tf_op jit(solution)/shard_map/ppermute | solution.py:76
  40.2 1.2 %collective-permute-start.17 = (bf16[4,4096]{1,0:T(4,128)(2,1)S(1)}, bf16[4,4096]{1,0:T(4,128)(2,1)S(1)}, u32[]{:S(2)}, u32[]{:S(2)}) collective-permute-start(bf16[4,4096]{1,0:T(4,128)(2,1)S(1)} %collective-permute-done.16.theirs_ref), channel_id=1, source_target_pairs={{0,1},{1,0},{2,3},{3,2},{4,5},{5,4},{6,7},{7,6},{8,9},{9,8},{10,11... | collective-permute-start | bytes 98312 | tf_op jit(solution)/shard_map/ppermute | solution.py:71
  48.2 1.3 %collective-permute-start.22 = (bf16[16,2048]{1,0:T(8,128)(2,1)S(1)}, bf16[16,2048]{1,0:T(8,128)(2,1)S(1)}, u32[]{:S(2)}, u32[]{:S(2)}) collective-permute-start(bf16[16,2048]{1,0:T(8,128)(2,1)S(1)} %get-tuple-element.16), channel_id=1, source_target_pairs={{0,1},{1,0},{2,3},{3,2},{4,5},{5,4},{6,7},{7,6},{8,9},{9,8},{10,11... | collective-permute-start | bytes 196616 | tf_op jit(solution)/shard_map/ppermute | solution.py:71

commit v6 on v5

--- a/solution.py
+++ b/solution.py
@@ -132,6 +132,15 @@
     for head in range(heads):
         value = lax.dot_general(w_ref[first + head], x, NT, preferred_element_type=jnp.float32)
         out_ref[head] = value.T.astype(jnp.bfloat16)
+
+
+def sum_kernel(keep_ref, arrived_ref, near_ref, far_ref):
+    half, _, seqs, _ = near_ref.shape
+    total = keep_ref[...].astype(jnp.float32) + arrived_ref[...].astype(jnp.float32)
+    for mask in range(half):
+        at = 2 * seqs * mask
+        near_ref[mask] = total[:, at : at + seqs].astype(jnp.bfloat16)
+        far_ref[mask] = total[:, at + seqs : at + 2 * seqs].astype(jnp.bfloat16)
 
 
 def merge_kernel(near_ref, far_ref, back_ref, *out_refs):
@@ -248,10 +257,16 @@
         )(*pieces, qkv_weight)
 
     arrived = swap(project(True))
-    joined = (project(False).astype(jnp.float32) + arrived.astype(jnp.float32)).astype(jnp.bfloat16)
-    joined = joined.reshape(kv_local, half, 2, seqs, part)
-    near = jnp.stack([joined[:, mask, 0] for mask in range(half)])
-    far = hop(jnp.stack([joined[:, mask, 1] for mask in range(half)]), chips, half)
+    stack = jax.ShapeDtypeStruct((half, kv_local, seqs, part), jnp.bfloat16)
+    near, far = pl.pallas_call(
+        sum_kernel,
+        out_shape=(stack, stack),
+        in_specs=in_vmem(2),
+        out_specs=tuple(in_vmem(2)),
+        compiler_params=pltpu.CompilerParams(vmem_limit_bytes=2 * MIB),
+        name="sum",
+    )(hold(project(False)), hold(arrived))
+    far = hop(far, chips, half)
     piece = jax.ShapeDtypeStruct((kv_local, seqs, part), jnp.bfloat16)
     pair = jax.ShapeDtypeStruct((2, kv_local, seqs, part), jnp.bfloat16)
     back, *pairs = pl.pallas_call(

time: 50.3 us -> 50 us (level)
    ppermute x8, starting transfers between devices: 2.18 us -> 2.75 us  [swap(): return lax.ppermute(x, 'gx', [(0, 1), (1, 0)])]
    ppermute x15, starting transfers between devices: 21.6 us -> 21 us  [hop(): return lax.ppermute(x, ('gy', 'gx'), pairs)]
  transfers between devices with their start and end apart: 23 -> 23, of which waited for: 12 -> 13; matrix products, arithmetic and copies ran while one was open for 0% -> 0% of each run, Pallas kernels for 5% -> 5%
where the time goes in v6:
time: 50 us; the launch traced here: 49.8 us
  starting transfers between devices  23.8 us (48%)
  waiting for transfers between devices  12.9 us (26%)
  Pallas kernels  11.5 us (23%)
  local copies, waits for them, and re-layouts  0.88 us (2%)
  other arithmetic  0.65 us (1%)
    ppermute x15, starting transfers between devices, hop(): return lax.ppermute(x, ('gy', 'gx'), pairs)  21 us
    ppermute x15, waiting for transfers between devices, hop(): return lax.ppermute(x, ('gy', 'gx'), pairs)  9.83 us
    pallas_call x2, Pallas kernels, project(): pl.pallas_call(functools.partial(project_kernel, swapped=swapped), out_sh...  5.28 us
    pallas_call x1, Pallas kernels, local(): pl.pallas_call(functools.partial(output_kernel, rows=seqs), out_shape=(pi...  4.66 us
    ppermute x8, waiting for transfers between devices, swap(): return lax.ppermute(x, 'gx', [(0, 1), (1, 0)])  3.06 us
    ppermute x8, starting transfers between devices, swap(): return lax.ppermute(x, 'gx', [(0, 1), (1, 0)])  2.75 us
    pallas_call x1, Pallas kernels, local(): pl.pallas_call(attend_kernel, out_shape=jax.ShapeDtypeStruct((seqs, feats...  1.51 us
  transfers between devices with their start and end apart: 23, of which 13 were waited for; matrix products, arithmetic and copies ran while one was open for 0% of the time, Pallas kernels for 5%

profile of v6, /device:TPU:0, one launch (start us, length us, event | category | flops | bytes accessed | tf_op | source)
XLA Modules:
  0.0 49.8 jit_solution(11073900903379692215)
XLA Ops:
  0.0 0.5 collective-permute-start.2
  0.5 3.7 %collective-permute-start = (bf16[4,8192]{1,0:T(4,128)(2,1)}, bf16[4,8192]{1,0:T(4,128)(2,1)S(1)}, u32[]{:S(2)}, u32[]{:S(2)}) collective-permute-start(bf16[4,8192]{1,0:T(4,128)(2,1)} %mine_ref.1), channel_id=1, source_target_pairs={{0,9},{1,8},{2,11},{3,10},{4,13},{5,12},{6,15},{7,14},{8,1},{9,0},... | collective-permute-start | bytes 196616 | tf_op jit(solution)/shard_map/ppermute | solution.py:76
  4.2 2.2 %collective-permute-start.7 = (bf16[4,8192]{1,0:T(4,128)(2,1)S(1)}, bf16[4,8192]{1,0:T(4,128)(2,1)S(1)}, u32[]{:S(2)}, u32[]{:S(2)}) collective-permute-start(bf16[4,8192]{1,0:T(4,128)(2,1)S(1)} %collective-permute-done.2), channel_id=1, source_target_pairs={{0,7},{1,6},{2,5},{3,4},{4,3},{5,2},{6,1},{7,0},{8,15},{9,14},{10,... | collective-permute-start | bytes 196616 | tf_op jit(solution)/shard_map/ppermute | solution.py:76
  6.3 0.5 %collective-permute-start.5 = (bf16[4,8192]{1,0:T(4,128)(2,1)S(1)}, bf16[4,8192]{1,0:T(4,128)(2,1)S(1)}, u32[]{:S(2)}, u32[]{:S(2)}) collective-permute-start(bf16[4,8192]{1,0:T(4,128)(2,1)S(1)} %collective-permute-done.2), channel_id=1, source_target_pairs={{0,5},{1,4},{2,7},{3,6},{4,1},{5,0},{6,3},{7,2},{8,13},{9,12},{10,... | collective-permute-start | bytes 196616 | tf_op jit(solution)/shard_map/ppermute | solution.py:76
  7.0 1.2 %collective-permute-done = bf16[4,8192]{1,0:T(4,128)(2,1)S(1)} collective-permute-done((bf16[4,8192]{1,0:T(4,128)(2,1)}, bf16[4,8192]{1,0:T(4,128)(2,1)S(1)}, u32[]{:S(2)}, u32[]{:S(2)}) %collective-permute-start) | collective-permute-done | bytes 65568 | tf_op jit(solution)/shard_map/ppermute | solution.py:76
  8.3 1.6 %collective-permute-start.8 = (bf16[4,8192]{1,0:T(4,128)(2,1)S(1)}, bf16[4,8192]{1,0:T(4,128)(2,1)S(1)}, u32[]{:S(2)}, u32[]{:S(2)}) collective-permute-start(bf16[4,8192]{1,0:T(4,128)(2,1)S(1)} %collective-permute-done), channel_id=1, source_target_pairs={{0,7},{1,6},{2,5},{3,4},{4,3},{5,2},{6,1},{7,0},{8,15},{9,14},{10,... | collective-permute-start | bytes 196616 | tf_op jit(solution)/shard_map/ppermute | solution.py:76
  9.8 1.5 %collective-permute-start.4 = (bf16[4,8192]{1,0:T(4,128)(2,1)S(1)}, bf16[4,8192]{1,0:T(4,128)(2,1)S(1)}, u32[]{:S(2)}, u32[]{:S(2)}) collective-permute-start(bf16[4,8192]{1,0:T(4,128)(2,1)S(1)} %collective-permute-done), channel_id=1, source_target_pairs={{0,3},{1,2},{2,1},{3,0},{4,7},{5,6},{6,5},{7,4},{8,11},{9,10},{10,... | collective-permute-start | bytes 196616 | tf_op jit(solution)/shard_map/ppermute | solution.py:76
  11.6 0.8 %copy-done.4 = bf16[4,8192]{1,0:T(4,128)(2,1)S(1)} copy-done((bf16[4,8192]{1,0:T(4,128)(2,1)S(1)}, bf16[4,8192]{1,0:T(4,128)(2,1)}, u32[]{:S(2)}) %copy-start.4) | copy-done | bytes 65560
  12.5 0.7 %collective-permute-done.8.refs_7_ = bf16[4,8192]{1,0:T(4,128)(2,1)S(1)} collective-permute-done((bf16[4,8192]{1,0:T(4,128)(2,1)S(1)}, bf16[4,8192]{1,0:T(4,128)(2,1)S(1)}, u32[]{:S(2)}, u32[]{:S(2)}) %collective-permute-start.8) | collective-permute-done | bytes 65568 | tf_op jit(solution)/shard_map/ppermute | solution.py:76
  13.2 1.0 %collective-permute-done.6.refs_5_ = bf16[4,8192]{1,0:T(4,128)(2,1)S(1)} collective-permute-done((bf16[4,8192]{1,0:T(4,128)(2,1)S(1)}, bf16[4,8192]{1,0:T(4,128)(2,1)S(1)}, u32[]{:S(2)}, u32[]{:S(2)}) %collective-permute-start.6) | collective-permute-done | bytes 65568 | tf_op jit(solution)/shard_map/ppermute | solution.py:76
  14.3 2.6 %project.3 = bf16[2,32,288]{2,1,0:T(8,128)(2,1)S(1)} custom-call(bf16[4,8192]{1,0:T(4,128)(2,1)S(1)} %stage.1.refs_0_, bf16[4,8192]{1,0:T(4,128)(2,1)S(1)} %collective-permute-done.1.refs_1_, bf16[4,8192]{1,0:T(4,128)(2,1)S(1)} %collective-permute-done.3.refs_2_, bf16[4,8192]{1,0:T(4,128)(2,1)S(1)} %collective-permute-done.4.refs_3_, ...), custom_call_target="tpu_custom_call" | custom-call | flops 2415919104 | bytes 1048576 | tf_op jit(solution)/shard_map/project/pallas_call | solution.py:247
  16.9 0.7 %collective-permute-start.9 = (bf16[2,32,288]{2,1,0:T(8,128)(2,1)S(1)}, bf16[2,32,288]{2,1,0:T(8,128)(2,1)S(1)}, u32[]{:S(2)}, u32[]{:S(2)}) collective-permute-start(bf16[2,32,288]{2,1,0:T(8,128)(2,1)S(1)} %project.3), channel_id=1, source_target_pairs={{0,1},{1,0},{2,3},{3,2},{4,5},{5,4},{6,7},{7,6},{8,9},{9,8},{10,11... | collective-permute-start | bytes 110600 | tf_op jit(solution)/shard_map/ppermute | solution.py:71
  17.7 2.6 %project.2.keep_ref = bf16[2,32,288]{2,1,0:T(8,128)(2,1)S(1)} custom-call(bf16[4,8192]{1,0:T(4,128)(2,1)S(1)} %stage.1.refs_0_, bf16[4,8192]{1,0:T(4,128)(2,1)S(1)} %collective-permute-done.1.refs_1_, bf16[4,8192]{1,0:T(4,128)(2,1)S(1)} %collective-permute-done.3.refs_2_, bf16[4,8192]{1,0:T(4,128)(2,1)S(1)} %collective-permute-done.4.refs_3_, ...), custom_call_target="tpu_custom_call" | custom-call | flops 2415919104 | bytes 1048576 | tf_op jit(solution)/shard_map/project/pallas_call | solution.py:247
  20.3 2.4 %collective-permute-start.11 = (bf16[4,2,4,288]{3,2,1,0:T(4,128)(2,1)S(1)}, bf16[4,2,4,288]{3,2,1,0:T(4,128)(2,1)S(1)}, u32[]{:S(2)}, u32[]{:S(2)}) collective-permute-start(bf16[4,2,4,288]{3,2,1,0:T(4,128)(2,1)S(1)} %get-tuple-element.14), channel_id=1, source_target_pairs={{0,9},{1,8},{2,11},{3,10},{4,13},{5,12},{6,15},{7,14},{8,1},{9,0},... | collective-permute-start | bytes 55304 | tf_op jit(solution)/shard_map/ppermute | solution.py:76
  23.0 1.6 %collective-permute-done.11.far_ref = bf16[4,2,4,288]{3,2,1,0:T(4,128)(2,1)S(1)} collective-permute-done((bf16[4,2,4,288]{3,2,1,0:T(4,128)(2,1)S(1)}, bf16[4,2,4,288]{3,2,1,0:T(4,128)(2,1)S(1)}, u32[]{:S(2)}, u32[]{:S(2)}) %collective-permute-start.11) | collective-permute-done | bytes 18464 | tf_op jit(solution)/shard_map/ppermute | solution.py:76
  24.6 2.4 %collective-permute-start.13 = (bf16[2,2,4,288]{3,2,1,0:T(4,128)(2,1)S(1)}, bf16[2,2,4,288]{3,2,1,0:T(4,128)(2,1)S(1)}, u32[]{:S(2)}, u32[]{:S(2)}) collective-permute-start(bf16[2,2,4,288]{3,2,1,0:T(4,128)(2,1)S(1)} %get-tuple-element.16), channel_id=1, source_target_pairs={{0,7},{1,6},{2,5},{3,4},{4,3},{5,2},{6,1},{7,0},{8,15},{9,14},{10,... | collective-permute-start | bytes 27656 | tf_op jit(solution)/shard_map/ppermute | solution.py:76
  27.1 0.6 %collective-permute-start.15 = (bf16[2,2,4,288]{3,2,1,0:T(4,128)(2,1)S(1)}, bf16[2,2,4,288]{3,2,1,0:T(4,128)(2,1)S(1)}, u32[]{:S(2)}, u32[]{:S(2)}) collective-permute-start(bf16[2,2,4,288]{3,2,1,0:T(4,128)(2,1)S(1)} %get-tuple-element.18), channel_id=1, source_target_pairs={{0,3},{1,2},{2,1},{3,0},{4,7},{5,6},{6,5},{7,4},{8,11},{9,10},{10,... | collective-permute-start | bytes 27656 | tf_op jit(solution)/shard_map/ppermute | solution.py:76
  28.0 0.9 %collective-permute-done.12.back_ref = bf16[2,4,288]{2,1,0:T(4,128)(2,1)S(1)} collective-permute-done((bf16[2,4,288]{2,1,0:T(4,128)(2,1)S(1)}, bf16[2,4,288]{2,1,0:T(4,128)(2,1)S(1)}, u32[]{:S(2)}, u32[]{:S(2)}) %collective-permute-start.12) | collective-permute-done | bytes 4640 | tf_op jit(solution)/shard_map/ppermute | solution.py:71
  28.9 1.3 %collective-permute-done.14.refs_1_ = bf16[2,2,4,288]{3,2,1,0:T(4,128)(2,1)S(1)} collective-permute-done((bf16[2,2,4,288]{3,2,1,0:T(4,128)(2,1)S(1)}, bf16[2,2,4,288]{3,2,1,0:T(4,128)(2,1)S(1)}, u32[]{:S(2)}, u32[]{:S(2)}) %collective-permute-start.14) | collective-permute-done | bytes 9248 | tf_op jit(solution)/shard_map/ppermute | solution.py:76
  30.3 1.5 %attend.1.refs_0_ = bf16[4,4096]{1,0:T(4,128)(2,1)S(1)} custom-call(s32[4]{0:T(128)S(1)} %copy-done.3, bf16[4,2,4,288]{3,2,1,0:T(4,128)(2,1)S(1)} %get-tuple-element.13.near_ref, bf16[2,4,288]{2,1,0:T(4,128)(2,1)S(1)} %collective-permute-done.12.back_ref, bf16[2,2,4,288]{3,2,1,0:T(4,128)(2,1)S(1)} %collective-permute-done.13.refs_0_, ...), custom_call_target="tpu_custom_call" | custom-call | tf_op jit(solution)/shard_map/attend/pallas_call | solution.py:283
  31.8 0.4 collective-permute-start.18
  32.2 2.6 %collective-permute-start.16 = (bf16[4,4096]{1,0:T(4,128)(2,1)S(1)}, bf16[4,4096]{1,0:T(4,128)(2,1)S(1)}, u32[]{:S(2)}, u32[]{:S(2)}) collective-permute-start(bf16[4,4096]{1,0:T(4,128)(2,1)S(1)} %attend.1.refs_0_), channel_id=1, source_target_pairs={{0,9},{1,8},{2,11},{3,10},{4,13},{5,12},{6,15},{7,14},{8,1},{9,0},... | collective-permute-start | bytes 98312 | tf_op jit(solution)/shard_map/ppermute | solution.py:76
  34.9 1.6 %collective-permute-done.16.theirs_ref = bf16[4,4096]{1,0:T(4,128)(2,1)S(1)} collective-permute-done((bf16[4,4096]{1,0:T(4,128)(2,1)S(1)}, bf16[4,4096]{1,0:T(4,128)(2,1)S(1)}, u32[]{:S(2)}, u32[]{:S(2)}) %collective-permute-start.16) | collective-permute-done | bytes 32800 | tf_op jit(solution)/shard_map/ppermute | solution.py:76
  36.5 1.8 %collective-permute-start.21 = (bf16[8,4096]{1,0:T(8,128)(2,1)S(1)}, bf16[8,4096]{1,0:T(8,128)(2,1)S(1)}, u32[]{:S(2)}, u32[]{:S(2)}) collective-permute-start(bf16[8,4096]{1,0:T(8,128)(2,1)S(1)} %pair.1), channel_id=1, source_target_pairs={{0,7},{1,6},{2,5},{3,4},{4,3},{5,2},{6,1},{7,0},{8,15},{9,14},{10,... | collective-permute-start | bytes 196616 | tf_op jit(solution)/shard_map/ppermute | solution.py:76
  38.4 1.4 %collective-permute-start.19 = (bf16[8,4096]{1,0:T(8,128)(2,1)S(1)}, bf16[8,4096]{1,0:T(8,128)(2,1)S(1)}, u32[]{:S(2)}, u32[]{:S(2)}) collective-permute-start(bf16[8,4096]{1,0:T(8,128)(2,1)S(1)} %pair.1), channel_id=1, source_target_pairs={{0,3},{1,2},{2,1},{3,0},{4,7},{5,6},{6,5},{7,4},{8,11},{9,10},{10,... | collective-permute-start | bytes 196616 | tf_op jit(solution)/shard_map/ppermute | solution.py:76
  39.9 1.0 %collective-permute-done.17.refs_1_ = bf16[4,4096]{1,0:T(4,128)(2,1)S(1)} collective-permute-done((bf16[4,4096]{1,0:T(4,128)(2,1)S(1)}, bf16[4,4096]{1,0:T(4,128)(2,1)S(1)}, u32[]{:S(2)}, u32[]{:S(2)}) %collective-permute-start.17) | collective-permute-done | bytes 32800 | tf_op jit(solution)/shard_map/ppermute | solution.py:71
  41.0 0.6 %collective-permute-done.21.refs_4_ = bf16[8,4096]{1,0:T(8,128)(2,1)S(1)} collective-permute-done((bf16[8,4096]{1,0:T(8,128)(2,1)S(1)}, bf16[8,4096]{1,0:T(8,128)(2,1)S(1)}, u32[]{:S(2)}, u32[]{:S(2)}) %collective-permute-start.21) | collective-permute-done | bytes 65568 | tf_op jit(solution)/shard_map/ppermute | solution.py:76
  41.5 0.7 %collective-permute-done.20.refs_3_ = bf16[8,4096]{1,0:T(8,128)(2,1)S(1)} collective-permute-done((bf16[8,4096]{1,0:T(8,128)(2,1)S(1)}, bf16[8,4096]{1,0:T(8,128)(2,1)S(1)}, u32[]{:S(2)}, u32[]{:S(2)}) %collective-permute-start.20) | collective-permute-done | bytes 65568 | tf_op jit(solution)/shard_map/ppermute | solution.py:76
  42.2 1.0 %collective-permute-done.19.refs_2_ = bf16[8,4096]{1,0:T(8,128)(2,1)S(1)} collective-permute-done((bf16[8,4096]{1,0:T(8,128)(2,1)S(1)}, bf16[8,4096]{1,0:T(8,128)(2,1)S(1)}, u32[]{:S(2)}, u32[]{:S(2)}) %collective-permute-start.19) | collective-permute-done | bytes 65568 | tf_op jit(solution)/shard_map/ppermute | solution.py:76
  43.2 4.7 %output.1 = (bf16[16,2048]{1,0:T(8,128)(2,1)S(1)}, bf16[16,2048]{1,0:T(8,128)(2,1)S(1)}) custom-call(bf16[4,4096]{1,0:T(4,128)(2,1)S(1)} %attend.1.refs_0_, bf16[4,4096]{1,0:T(4,128)(2,1)S(1)} %collective-permute-done.17.refs_1_, bf16[8,4096]{1,0:T(8,128)(2,1)S(1)} %collective-permute-done.19.refs_2_, bf16[8,4096]{1,0:T(8,128)(2,1)S(1)} %collective-permute-done.20.refs_3_, ...), custom_call_target="tpu_custom_call" | custom-call | tf_op jit(solution)/shard_map/output/pallas_call | solution.py:300
  48.1 1.1 %collective-permute-done.22 = bf16[16,2048]{1,0:T(8,128)(2,1)S(1)} collective-permute-done((bf16[16,2048]{1,0:T(8,128)(2,1)S(1)}, bf16[16,2048]{1,0:T(8,128)(2,1)S(1)}, u32[]{:S(2)}, u32[]{:S(2)}) %collective-permute-start.22) | collective-permute-done | bytes 65568 | tf_op jit(solution)/shard_map/ppermute | solution.py:71
  49.2 0.6 %add_convert_fusion = bf16[16,2048]{1,0:T(8,128)(2,1)} fusion(bf16[16,2048]{1,0:T(8,128)(2,1)S(1)} %collective-permute-done.22, bf16[16,2048]{1,0:T(8,128)(2,1)S(1)} %get-tuple-element.19), kind=kLoop, calls=%fused_computation | loop fusion | flops 131072 | bytes 196608 | tf_op jit(solution)/shard_map/convert_element_type | solution.py:308
  (42 shorter events, 1.8 us)
Async XLA Ops:
  0.0 14.3 %copy-start = (bf16[4,288,8192]{2,1,0:T(8,128)(2,1)S(1)}, bf16[4,288,8192]{2,1,0:T(8,128)(2,1)}, u32[]{:S(2)}) copy-start(bf16[4,288,8192]{2,1,0:T(8,128)(2,1)} %refs_8_.3) | copy-start | bytes 56623108
  0.0 4.2 %collective-permute-start.2 = (bf16[4,8192]{1,0:T(4,128)(2,1)}, bf16[4,8192]{1,0:T(4,128)(2,1)S(1)}, u32[]{:S(2)}, u32[]{:S(2)}) collective-permute-start(bf16[4,8192]{1,0:T(4,128)(2,1)} %mine_ref.1), channel_id=1, source_target_pairs={{0,1},{1,0},{2,3},{3,2},{4,5},{5,4},{6,7},{7,6},{8,9},{9,8},{10,11... | collective-permute-start | bytes 196616 | tf_op jit(solution)/shard_map/ppermute | solution.py:71
  0.5 7.8 %collective-permute-start = (bf16[4,8192]{1,0:T(4,128)(2,1)}, bf16[4,8192]{1,0:T(4,128)(2,1)S(1)}, u32[]{:S(2)}, u32[]{:S(2)}) collective-permute-start(bf16[4,8192]{1,0:T(4,128)(2,1)} %mine_ref.1), channel_id=1, source_target_pairs={{0,9},{1,8},{2,11},{3,10},{4,13},{5,12},{6,15},{7,14},{8,1},{9,0},... | collective-permute-start | bytes 196616 | tf_op jit(solution)/shard_map/ppermute | solution.py:76
  4.2 5.7 %collective-permute-start.7 = (bf16[4,8192]{1,0:T(4,128)(2,1)S(1)}, bf16[4,8192]{1,0:T(4,128)(2,1)S(1)}, u32[]{:S(2)}, u32[]{:S(2)}) collective-permute-start(bf16[4,8192]{1,0:T(4,128)(2,1)S(1)} %collective-permute-done.2), channel_id=1, source_target_pairs={{0,7},{1,6},{2,5},{3,4},{4,3},{5,2},{6,1},{7,0},{8,15},{9,14},{10,... | collective-permute-start | bytes 196616 | tf_op jit(solution)/shard_map/ppermute | solution.py:76
  6.3 5.0 %collective-permute-start.5 = (bf16[4,8192]{1,0:T(4,128)(2,1)S(1)}, bf16[4,8192]{1,0:T(4,128)(2,1)S(1)}, u32[]{:S(2)}, u32[]{:S(2)}) collective-permute-start(bf16[4,8192]{1,0:T(4,128)(2,1)S(1)} %collective-permute-done.2), channel_id=1, source_target_pairs={{0,5},{1,4},{2,7},{3,6},{4,1},{5,0},{6,3},{7,2},{8,13},{9,12},{10,... | collective-permute-start | bytes 196616 | tf_op jit(solution)/shard_map/ppermute | solution.py:76
  6.8 5.7 %collective-permute-start.3 = (bf16[4,8192]{1,0:T(4,128)(2,1)S(1)}, bf16[4,8192]{1,0:T(4,128)(2,1)S(1)}, u32[]{:S(2)}, u32[]{:S(2)}) collective-permute-start(bf16[4,8192]{1,0:T(4,128)(2,1)S(1)} %collective-permute-done.2), channel_id=1, source_target_pairs={{0,3},{1,2},{2,1},{3,0},{4,7},{5,6},{6,5},{7,4},{8,11},{9,10},{10,... | collective-permute-start | bytes 196616 | tf_op jit(solution)/shard_map/ppermute | solution.py:76
  8.3 5.0 %collective-permute-start.8 = (bf16[4,8192]{1,0:T(4,128)(2,1)S(1)}, bf16[4,8192]{1,0:T(4,128)(2,1)S(1)}, u32[]{:S(2)}, u32[]{:S(2)}) collective-permute-start(bf16[4,8192]{1,0:T(4,128)(2,1)S(1)} %collective-permute-done), channel_id=1, source_target_pairs={{0,7},{1,6},{2,5},{3,4},{4,3},{5,2},{6,1},{7,0},{8,15},{9,14},{10,... | collective-permute-start | bytes 196616 | tf_op jit(solution)/shard_map/ppermute | solution.py:76
  9.8 4.4 %collective-permute-start.6 = (bf16[4,8192]{1,0:T(4,128)(2,1)S(1)}, bf16[4,8192]{1,0:T(4,128)(2,1)S(1)}, u32[]{:S(2)}, u32[]{:S(2)}) collective-permute-start(bf16[4,8192]{1,0:T(4,128)(2,1)S(1)} %collective-permute-done), channel_id=1, source_target_pairs={{0,5},{1,4},{2,7},{3,6},{4,1},{5,0},{6,3},{7,2},{8,13},{9,12},{10,... | collective-permute-start | bytes 196616 | tf_op jit(solution)/shard_map/ppermute | solution.py:76
  9.8 4.4 %collective-permute-start.4 = (bf16[4,8192]{1,0:T(4,128)(2,1)S(1)}, bf16[4,8192]{1,0:T(4,128)(2,1)S(1)}, u32[]{:S(2)}, u32[]{:S(2)}) collective-permute-start(bf16[4,8192]{1,0:T(4,128)(2,1)S(1)} %collective-permute-done), channel_id=1, source_target_pairs={{0,3},{1,2},{2,1},{3,0},{4,7},{5,6},{6,5},{7,4},{8,11},{9,10},{10,... | collective-permute-start | bytes 196616 | tf_op jit(solution)/shard_map/ppermute | solution.py:76
  11.4 2.9 %collective-permute-start.1 = (bf16[4,8192]{1,0:T(4,128)(2,1)S(1)}, bf16[4,8192]{1,0:T(4,128)(2,1)S(1)}, u32[]{:S(2)}, u32[]{:S(2)}) collective-permute-start(bf16[4,8192]{1,0:T(4,128)(2,1)S(1)} %collective-permute-done), channel_id=1, source_target_pairs={{0,1},{1,0},{2,3},{3,2},{4,5},{5,4},{6,7},{7,6},{8,9},{9,8},{10,11... | collective-permute-start | bytes 196616 | tf_op jit(solution)/shard_map/ppermute | solution.py:71
  11.6 0.8 %copy-start.4 = (bf16[4,8192]{1,0:T(4,128)(2,1)S(1)}, bf16[4,8192]{1,0:T(4,128)(2,1)}, u32[]{:S(2)}) copy-start(bf16[4,8192]{1,0:T(4,128)(2,1)} %mine_ref.1) | copy-start | bytes 196612
  12.5 17.8 %copy-start.1 = (bf16[4,2,512,128]{3,2,1,0:T(8,128)(2,1)S(1)}, bf16[4,2,512,128]{3,2,1,0:T(8,128)(2,1)}, u32[]{:S(2)}) copy-start(bf16[4,2,512,128]{3,2,1,0:T(8,128)(2,1)} %refs_3_.1) | copy-start | bytes 3145732
  12.5 17.8 %copy-start.2 = (bf16[4,2,512,128]{3,2,1,0:T(8,128)(2,1)S(1)}, bf16[4,2,512,128]{3,2,1,0:T(8,128)(2,1)}, u32[]{:S(2)}) copy-start(bf16[4,2,512,128]{3,2,1,0:T(8,128)(2,1)} %refs_4_.1) | copy-start | bytes 3145732
  12.5 17.8 %copy-start.3 = (s32[4]{0:T(128)S(1)}, s32[4]{0:T(128)}, u32[]{:S(2)}) copy-start(s32[4]{0:T(128)} %lengths_ref.1) | copy-start | bytes 52
  12.5 30.7 %slice-start = ((s8[16777216]{0:T(1024)(128)(4,1)}), s8[4194304]{0:T(1024)(128)(4,1)S(1)}, s32[]{:S(2)}) async-start(s8[16777216]{0:T(1024)(128)(4,1)} %bitcast), calls=%async_computation | async-start | bytes 8388608
  12.5 30.7 %slice-start.1 = ((s8[16777216]{0:T(1024)(128)(4,1)}), s8[4194304]{0:T(1024)(128)(4,1)S(1)}, s32[]{:S(2)}) async-start(s8[16777216]{0:T(1024)(128)(4,1)} %bitcast), calls=%async_computation.1 | async-start | bytes 8388608
  16.9 26.3 %slice-start.2 = ((s8[16777216]{0:T(1024)(128)(4,1)}), s8[4194304]{0:T(1024)(128)(4,1)S(1)}, s32[]{:S(2)}) async-start(s8[16777216]{0:T(1024)(128)(4,1)} %bitcast), calls=%async_computation.2 | async-start | bytes 8388608
  16.9 26.3 %slice-start.3 = ((s8[16777216]{0:T(1024)(128)(4,1)}), s8[4194304]{0:T(1024)(128)(4,1)S(1)}, s32[]{:S(2)}) async-start(s8[16777216]{0:T(1024)(128)(4,1)} %bitcast), calls=%async_computation.3 | async-start | bytes 8388608
  16.9 3.4 %collective-permute-start.9 = (bf16[2,32,288]{2,1,0:T(8,128)(2,1)S(1)}, bf16[2,32,288]{2,1,0:T(8,128)(2,1)S(1)}, u32[]{:S(2)}, u32[]{:S(2)}) collective-permute-start(bf16[2,32,288]{2,1,0:T(8,128)(2,1)S(1)} %project.3), channel_id=1, source_target_pairs={{0,1},{1,0},{2,3},{3,2},{4,5},{5,4},{6,7},{7,6},{8,9},{9,8},{10,11... | collective-permute-start | bytes 110600 | tf_op jit(solution)/shard_map/ppermute | solution.py:71
  20.3 4.3 %collective-permute-start.11 = (bf16[4,2,4,288]{3,2,1,0:T(4,128)(2,1)S(1)}, bf16[4,2,4,288]{3,2,1,0:T(4,128)(2,1)S(1)}, u32[]{:S(2)}, u32[]{:S(2)}) collective-permute-start(bf16[4,2,4,288]{3,2,1,0:T(4,128)(2,1)S(1)} %get-tuple-element.14), channel_id=1, source_target_pairs={{0,9},{1,8},{2,11},{3,10},{4,13},{5,12},{6,15},{7,14},{8,1},{9,0},... | collective-permute-start | bytes 55304 | tf_op jit(solution)/shard_map/ppermute | solution.py:76
  22.7 1.9 %collective-permute-start.10 = (bf16[4,2,4,288]{3,2,1,0:T(4,128)(2,1)S(1)}, bf16[4,2,4,288]{3,2,1,0:T(4,128)(2,1)S(1)}, u32[]{:S(2)}, u32[]{:S(2)}) collective-permute-start(bf16[4,2,4,288]{3,2,1,0:T(4,128)(2,1)S(1)} %get-tuple-element.13.near_ref), channel_id=1, source_target_pairs={{0,1},{1,0},{2,3},{3,2},{4,5},{5,4},{6,7},{7,6},{8,9},{9,8},{10,11... | collective-permute-start | bytes 55304 | tf_op jit(solution)/shard_map/ppermute | solution.py:71
  24.6 4.3 %collective-permute-start.13 = (bf16[2,2,4,288]{3,2,1,0:T(4,128)(2,1)S(1)}, bf16[2,2,4,288]{3,2,1,0:T(4,128)(2,1)S(1)}, u32[]{:S(2)}, u32[]{:S(2)}) collective-permute-start(bf16[2,2,4,288]{3,2,1,0:T(4,128)(2,1)S(1)} %get-tuple-element.16), channel_id=1, source_target_pairs={{0,7},{1,6},{2,5},{3,4},{4,3},{5,2},{6,1},{7,0},{8,15},{9,14},{10,... | collective-permute-start | bytes 27656 | tf_op jit(solution)/shard_map/ppermute | solution.py:76
  27.0 3.1 %collective-permute-start.14 = (bf16[2,2,4,288]{3,2,1,0:T(4,128)(2,1)S(1)}, bf16[2,2,4,288]{3,2,1,0:T(4,128)(2,1)S(1)}, u32[]{:S(2)}, u32[]{:S(2)}) collective-permute-start(bf16[2,2,4,288]{3,2,1,0:T(4,128)(2,1)S(1)} %get-tuple-element.17), channel_id=1, source_target_pairs={{0,5},{1,4},{2,7},{3,6},{4,1},{5,0},{6,3},{7,2},{8,13},{9,12},{10,... | collective-permute-start | bytes 27656 | tf_op jit(solution)/shard_map/ppermute | solution.py:76
  27.1 3.1 %collective-permute-start.15 = (bf16[2,2,4,288]{3,2,1,0:T(4,128)(2,1)S(1)}, bf16[2,2,4,288]{3,2,1,0:T(4,128)(2,1)S(1)}, u32[]{:S(2)}, u32[]{:S(2)}) collective-permute-start(bf16[2,2,4,288]{3,2,1,0:T(4,128)(2,1)S(1)} %get-tuple-element.18), channel_id=1, source_target_pairs={{0,3},{1,2},{2,1},{3,0},{4,7},{5,6},{6,5},{7,4},{8,11},{9,10},{10,... | collective-permute-start | bytes 27656 | tf_op jit(solution)/shard_map/ppermute | solution.py:76
  27.7 1.2 %collective-permute-start.12 = (bf16[2,4,288]{2,1,0:T(4,128)(2,1)S(1)}, bf16[2,4,288]{2,1,0:T(4,128)(2,1)S(1)}, u32[]{:S(2)}, u32[]{:S(2)}) collective-permute-start(bf16[2,4,288]{2,1,0:T(4,128)(2,1)S(1)} %get-tuple-element.15), channel_id=1, source_target_pairs={{0,1},{1,0},{2,3},{3,2},{4,5},{5,4},{6,7},{7,6},{8,9},{9,8},{10,11... | collective-permute-start | bytes 13832 | tf_op jit(solution)/shard_map/ppermute | solution.py:71
  31.8 3.1 %collective-permute-start.18 = (bf16[4,4096]{1,0:T(4,128)(2,1)S(1)}, bf16[4,4096]{1,0:T(4,128)(2,1)S(1)}, u32[]{:S(2)}, u32[]{:S(2)}) collective-permute-start(bf16[4,4096]{1,0:T(4,128)(2,1)S(1)} %attend.1.refs_0_), channel_id=1, source_target_pairs={{0,1},{1,0},{2,3},{3,2},{4,5},{5,4},{6,7},{7,6},{8,9},{9,8},{10,11... | collective-permute-start | bytes 98312 | tf_op jit(solution)/shard_map/ppermute | solution.py:71
  32.2 4.3 %collective-permute-start.16 = (bf16[4,4096]{1,0:T(4,128)(2,1)S(1)}, bf16[4,4096]{1,0:T(4,128)(2,1)S(1)}, u32[]{:S(2)}, u32[]{:S(2)}) collective-permute-start(bf16[4,4096]{1,0:T(4,128)(2,1)S(1)} %attend.1.refs_0_), channel_id=1, source_target_pairs={{0,9},{1,8},{2,11},{3,10},{4,13},{5,12},{6,15},{7,14},{8,1},{9,0},... | collective-permute-start | bytes 98312 | tf_op jit(solution)/shard_map/ppermute | solution.py:76
  36.5 5.0 %collective-permute-start.21 = (bf16[8,4096]{1,0:T(8,128)(2,1)S(1)}, bf16[8,4096]{1,0:T(8,128)(2,1)S(1)}, u32[]{:S(2)}, u32[]{:S(2)}) collective-permute-start(bf16[8,4096]{1,0:T(8,128)(2,1)S(1)} %pair.1), channel_id=1, source_target_pairs={{0,7},{1,6},{2,5},{3,4},{4,3},{5,2},{6,1},{7,0},{8,15},{9,14},{10,... | collective-permute-start | bytes 196616 | tf_op jit(solution)/shard_map/ppermute | solution.py:76
  38.3 3.9 %collective-permute-start.20 = (bf16[8,4096]{1,0:T(8,128)(2,1)S(1)}, bf16[8,4096]{1,0:T(8,128)(2,1)S(1)}, u32[]{:S(2)}, u32[]{:S(2)}) collective-permute-start(bf16[8,4096]{1,0:T(8,128)(2,1)S(1)} %pair.1), channel_id=1, source_target_pairs={{0,5},{1,4},{2,7},{3,6},{4,1},{5,0},{6,3},{7,2},{8,13},{9,12},{10,... | collective-permute-start | bytes 196616 | tf_op jit(solution)/shard_map/ppermute | solution.py:76
  38.4 4.8 %collective-permute-start.19 = (bf16[8,4096]{1,0:T(8,128)(2,1)S(1)}, bf16[8,4096]{1,0:T(8,128)(2,1)S(1)}, u32[]{:S(2)}, u32[]{:S(2)}) collective-permute-start(bf16[8,4096]{1,0:T(8,128)(2,1)S(1)} %pair.1), channel_id=1, source_target_pairs={{0,3},{1,2},{2,1},{3,0},{4,7},{5,6},{6,5},{7,4},{8,11},{9,10},{10,... | collective-permute-start | bytes 196616 | tf_op jit(solution)/shard_map/ppermute | solution.py:76
  39.7 1.2 %collective-permute-start.17 = (bf16[4,4096]{1,0:T(4,128)(2,1)S(1)}, bf16[4,4096]{1,0:T(4,128)(2,1)S(1)}, u32[]{:S(2)}, u32[]{:S(2)}) collective-permute-start(bf16[4,4096]{1,0:T(4,128)(2,1)S(1)} %collective-permute-done.16.theirs_ref), channel_id=1, source_target_pairs={{0,1},{1,0},{2,3},{3,2},{4,5},{5,4},{6,7},{7,6},{8,9},{9,8},{10,11... | collective-permute-start | bytes 98312 | tf_op jit(solution)/shard_map/ppermute | solution.py:71
  47.9 1.3 %collective-permute-start.22 = (bf16[16,2048]{1,0:T(8,128)(2,1)S(1)}, bf16[16,2048]{1,0:T(8,128)(2,1)S(1)}, u32[]{:S(2)}, u32[]{:S(2)}) collective-permute-start(bf16[16,2048]{1,0:T(8,128)(2,1)S(1)} %get-tuple-element.20), channel_id=1, source_target_pairs={{0,1},{1,0},{2,3},{3,2},{4,5},{5,4},{6,7},{7,6},{8,9},{9,8},{10,11... | collective-permute-start | bytes 196616 | tf_op jit(solution)/shard_map/ppermute | solution.py:71

commit v7 on v6

--- a/solution.py
+++ b/solution.py
@@ -201,19 +201,24 @@
     out_ref[...] = flat[...].astype(jnp.bfloat16)
 
 
-def output_kernel(*refs, rows):
-    *x_refs, w_ref, keep_ref, send_ref = refs
-    x = jnp.concatenate([x_ref[...] for x_ref in x_refs], axis=0)
-    total = x.shape[0]
-    half = total // (2 * rows)
+def output_kernel(*refs):
+    own_ref, back_ref, *pair_refs, w_ref, keep_ref, send_ref, placed = refs
+    chips, rows = placed.shape[0], placed.shape[1]
+    half = chips // 2
     chip, core = lax.axis_index("gy"), lax.axis_index("gx")
-    row = lax.broadcasted_iota(jnp.int32, (total, total), 0)
-    column = lax.broadcasted_iota(jnp.int32, (total, total), 1)
-    side, within = row // (half * rows), row % (half * rows)
-    mask = chip ^ ((core ^ side) * half + within // rows)
-    source = (mask % half) * (2 * rows) + (mask // half) * rows + within % rows
-    order = jnp.where(column == source, 1.0, 0.0).astype(jnp.bfloat16)
-    x = jnp.dot(order, x, preferred_element_type=jnp.float32).astype(jnp.bfloat16)
+
+    def place(mask, block):
+        source = chip ^ mask
+        side = core ^ (source // half)
+        placed[side * half + source % half] = block.astype(jnp.float32)
+
+    place(0, own_ref[...])
+    place(half, back_ref[...])
+    for at, pair_ref in enumerate(pair_refs):
+        pair = pair_ref[...].astype(jnp.float32)
+        place(at + 1, pair[:rows])
+        place(at + 1 + half, pair[rows:])
+    x = jnp.concatenate([placed[at] for at in range(chips)], axis=0).astype(jnp.bfloat16)
     cols = w_ref.shape[0]
     width = min(cols, 256)
     for at in range(0, cols, width):
@@ -298,10 +303,11 @@
     pieces = [hold(piece) for piece in gather_rows(attended, chips)]
     piece = jax.ShapeDtypeStruct((rows // 2, out_cols), jnp.bfloat16)
     keep, send = pl.pallas_call(
-        functools.partial(output_kernel, rows=seqs),
+        output_kernel,
         out_shape=(piece, piece),
         in_specs=in_vmem(half + 2),
         out_specs=tuple(in_vmem(2)),
+        scratch_shapes=[pltpu.VMEM((chips, seqs, feats), jnp.float32)],
         compiler_params=limits,
         name="output",
     )(*pieces, out_weight)

time: 50 us -> 49.9 us (level)
  no operation moved by 1% of the time
where the time goes in v7:
time: 49.9 us; the launch traced here: 49.7 us
  starting transfers between devices  23.8 us (48%)
  waiting for transfers between devices  12.9 us (26%)
  Pallas kernels  11.4 us (23%)
  local copies, waits for them, and re-layouts  0.88 us (2%)
  other arithmetic  0.65 us (1%)
    ppermute x15, starting transfers between devices, hop(): return lax.ppermute(x, ('gy', 'gx'), pairs)  21 us
    ppermute x15, waiting for transfers between devices, hop(): return lax.ppermute(x, ('gy', 'gx'), pairs)  9.83 us
    pallas_call x2, Pallas kernels, project(): pl.pallas_call(functools.partial(project_kernel, swapped=swapped), out_sh...  5.28 us
    pallas_call x1, Pallas kernels, local(): pl.pallas_call(output_kernel, out_shape=(piece, piece), in_specs=in_vmem(...  4.56 us
    ppermute x8, waiting for transfers between devices, swap(): return lax.ppermute(x, 'gx', [(0, 1), (1, 0)])  3.06 us
    ppermute x8, starting transfers between devices, swap(): return lax.ppermute(x, 'gx', [(0, 1), (1, 0)])  2.75 us
    pallas_call x1, Pallas kernels, local(): pl.pallas_call(attend_kernel, out_shape=jax.ShapeDtypeStruct((seqs, feats...  1.51 us
  transfers between devices with their start and end apart: 23, of which 13 were waited for; matrix products, arithmetic and copies ran while one was open for 0% of the time, Pallas kernels for 5%

profile of v7, /device:TPU:0, one launch (start us, length us, event | category | flops | bytes accessed | tf_op | source)
XLA Modules:
  0.0 49.7 jit_solution(6797217794440043175)
XLA Ops:
  0.0 0.5 collective-permute-start.2
  0.5 3.7 %collective-permute-start = (bf16[4,8192]{1,0:T(4,128)(2,1)}, bf16[4,8192]{1,0:T(4,128)(2,1)S(1)}, u32[]{:S(2)}, u32[]{:S(2)}) collective-permute-start(bf16[4,8192]{1,0:T(4,128)(2,1)} %mine_ref.1), channel_id=1, source_target_pairs={{0,9},{1,8},{2,11},{3,10},{4,13},{5,12},{6,15},{7,14},{8,1},{9,0},... | collective-permute-start | bytes 196616 | tf_op jit(solution)/shard_map/ppermute | solution.py:76
  4.2 2.2 %collective-permute-start.7 = (bf16[4,8192]{1,0:T(4,128)(2,1)S(1)}, bf16[4,8192]{1,0:T(4,128)(2,1)S(1)}, u32[]{:S(2)}, u32[]{:S(2)}) collective-permute-start(bf16[4,8192]{1,0:T(4,128)(2,1)S(1)} %collective-permute-done.2), channel_id=1, source_target_pairs={{0,7},{1,6},{2,5},{3,4},{4,3},{5,2},{6,1},{7,0},{8,15},{9,14},{10,... | collective-permute-start | bytes 196616 | tf_op jit(solution)/shard_map/ppermute | solution.py:76
  6.3 0.5 %collective-permute-start.5 = (bf16[4,8192]{1,0:T(4,128)(2,1)S(1)}, bf16[4,8192]{1,0:T(4,128)(2,1)S(1)}, u32[]{:S(2)}, u32[]{:S(2)}) collective-permute-start(bf16[4,8192]{1,0:T(4,128)(2,1)S(1)} %collective-permute-done.2), channel_id=1, source_target_pairs={{0,5},{1,4},{2,7},{3,6},{4,1},{5,0},{6,3},{7,2},{8,13},{9,12},{10,... | collective-permute-start | bytes 196616 | tf_op jit(solution)/shard_map/ppermute | solution.py:76
  7.0 1.2 %collective-permute-done = bf16[4,8192]{1,0:T(4,128)(2,1)S(1)} collective-permute-done((bf16[4,8192]{1,0:T(4,128)(2,1)}, bf16[4,8192]{1,0:T(4,128)(2,1)S(1)}, u32[]{:S(2)}, u32[]{:S(2)}) %collective-permute-start) | collective-permute-done | bytes 65568 | tf_op jit(solution)/shard_map/ppermute | solution.py:76
  8.3 1.6 %collective-permute-start.8 = (bf16[4,8192]{1,0:T(4,128)(2,1)S(1)}, bf16[4,8192]{1,0:T(4,128)(2,1)S(1)}, u32[]{:S(2)}, u32[]{:S(2)}) collective-permute-start(bf16[4,8192]{1,0:T(4,128)(2,1)S(1)} %collective-permute-done), channel_id=1, source_target_pairs={{0,7},{1,6},{2,5},{3,4},{4,3},{5,2},{6,1},{7,0},{8,15},{9,14},{10,... | collective-permute-start | bytes 196616 | tf_op jit(solution)/shard_map/ppermute | solution.py:76
  9.8 1.5 %collective-permute-start.4 = (bf16[4,8192]{1,0:T(4,128)(2,1)S(1)}, bf16[4,8192]{1,0:T(4,128)(2,1)S(1)}, u32[]{:S(2)}, u32[]{:S(2)}) collective-permute-start(bf16[4,8192]{1,0:T(4,128)(2,1)S(1)} %collective-permute-done), channel_id=1, source_target_pairs={{0,3},{1,2},{2,1},{3,0},{4,7},{5,6},{6,5},{7,4},{8,11},{9,10},{10,... | collective-permute-start | bytes 196616 | tf_op jit(solution)/shard_map/ppermute | solution.py:76
  11.6 0.8 %copy-done.4 = bf16[4,8192]{1,0:T(4,128)(2,1)S(1)} copy-done((bf16[4,8192]{1,0:T(4,128)(2,1)S(1)}, bf16[4,8192]{1,0:T(4,128)(2,1)}, u32[]{:S(2)}) %copy-start.4) | copy-done | bytes 65560
  12.5 0.7 %collective-permute-done.8.refs_7_ = bf16[4,8192]{1,0:T(4,128)(2,1)S(1)} collective-permute-done((bf16[4,8192]{1,0:T(4,128)(2,1)S(1)}, bf16[4,8192]{1,0:T(4,128)(2,1)S(1)}, u32[]{:S(2)}, u32[]{:S(2)}) %collective-permute-start.8) | collective-permute-done | bytes 65568 | tf_op jit(solution)/shard_map/ppermute | solution.py:76
  13.2 1.0 %collective-permute-done.6.refs_5_ = bf16[4,8192]{1,0:T(4,128)(2,1)S(1)} collective-permute-done((bf16[4,8192]{1,0:T(4,128)(2,1)S(1)}, bf16[4,8192]{1,0:T(4,128)(2,1)S(1)}, u32[]{:S(2)}, u32[]{:S(2)}) %collective-permute-start.6) | collective-permute-done | bytes 65568 | tf_op jit(solution)/shard_map/ppermute | solution.py:76
  14.3 2.6 %project.3 = bf16[2,32,288]{2,1,0:T(8,128)(2,1)S(1)} custom-call(bf16[4,8192]{1,0:T(4,128)(2,1)S(1)} %stage.1.refs_0_, bf16[4,8192]{1,0:T(4,128)(2,1)S(1)} %collective-permute-done.1.refs_1_, bf16[4,8192]{1,0:T(4,128)(2,1)S(1)} %collective-permute-done.3.refs_2_, bf16[4,8192]{1,0:T(4,128)(2,1)S(1)} %collective-permute-done.4.refs_3_, ...), custom_call_target="tpu_custom_call" | custom-call | flops 2415919104 | bytes 1048576 | tf_op jit(solution)/shard_map/project/pallas_call | solution.py:252
  16.9 0.7 %collective-permute-start.9 = (bf16[2,32,288]{2,1,0:T(8,128)(2,1)S(1)}, bf16[2,32,288]{2,1,0:T(8,128)(2,1)S(1)}, u32[]{:S(2)}, u32[]{:S(2)}) collective-permute-start(bf16[2,32,288]{2,1,0:T(8,128)(2,1)S(1)} %project.3), channel_id=1, source_target_pairs={{0,1},{1,0},{2,3},{3,2},{4,5},{5,4},{6,7},{7,6},{8,9},{9,8},{10,11... | collective-permute-start | bytes 110600 | tf_op jit(solution)/shard_map/ppermute | solution.py:71
  17.7 2.6 %project.2.keep_ref = bf16[2,32,288]{2,1,0:T(8,128)(2,1)S(1)} custom-call(bf16[4,8192]{1,0:T(4,128)(2,1)S(1)} %stage.1.refs_0_, bf16[4,8192]{1,0:T(4,128)(2,1)S(1)} %collective-permute-done.1.refs_1_, bf16[4,8192]{1,0:T(4,128)(2,1)S(1)} %collective-permute-done.3.refs_2_, bf16[4,8192]{1,0:T(4,128)(2,1)S(1)} %collective-permute-done.4.refs_3_, ...), custom_call_target="tpu_custom_call" | custom-call | flops 2415919104 | bytes 1048576 | tf_op jit(solution)/shard_map/project/pallas_call | solution.py:252
  20.3 2.4 %collective-permute-start.11 = (bf16[4,2,4,288]{3,2,1,0:T(4,128)(2,1)S(1)}, bf16[4,2,4,288]{3,2,1,0:T(4,128)(2,1)S(1)}, u32[]{:S(2)}, u32[]{:S(2)}) collective-permute-start(bf16[4,2,4,288]{3,2,1,0:T(4,128)(2,1)S(1)} %get-tuple-element.14), channel_id=1, source_target_pairs={{0,9},{1,8},{2,11},{3,10},{4,13},{5,12},{6,15},{7,14},{8,1},{9,0},... | collective-permute-start | bytes 55304 | tf_op jit(solution)/shard_map/ppermute | solution.py:76
  23.0 1.6 %collective-permute-done.11.far_ref = bf16[4,2,4,288]{3,2,1,0:T(4,128)(2,1)S(1)} collective-permute-done((bf16[4,2,4,288]{3,2,1,0:T(4,128)(2,1)S(1)}, bf16[4,2,4,288]{3,2,1,0:T(4,128)(2,1)S(1)}, u32[]{:S(2)}, u32[]{:S(2)}) %collective-permute-start.11) | collective-permute-done | bytes 18464 | tf_op jit(solution)/shard_map/ppermute | solution.py:76
  24.6 2.4 %collective-permute-start.13 = (bf16[2,2,4,288]{3,2,1,0:T(4,128)(2,1)S(1)}, bf16[2,2,4,288]{3,2,1,0:T(4,128)(2,1)S(1)}, u32[]{:S(2)}, u32[]{:S(2)}) collective-permute-start(bf16[2,2,4,288]{3,2,1,0:T(4,128)(2,1)S(1)} %get-tuple-element.16), channel_id=1, source_target_pairs={{0,7},{1,6},{2,5},{3,4},{4,3},{5,2},{6,1},{7,0},{8,15},{9,14},{10,... | collective-permute-start | bytes 27656 | tf_op jit(solution)/shard_map/ppermute | solution.py:76
  27.1 0.6 %collective-permute-start.15 = (bf16[2,2,4,288]{3,2,1,0:T(4,128)(2,1)S(1)}, bf16[2,2,4,288]{3,2,1,0:T(4,128)(2,1)S(1)}, u32[]{:S(2)}, u32[]{:S(2)}) collective-permute-start(bf16[2,2,4,288]{3,2,1,0:T(4,128)(2,1)S(1)} %get-tuple-element.18), channel_id=1, source_target_pairs={{0,3},{1,2},{2,1},{3,0},{4,7},{5,6},{6,5},{7,4},{8,11},{9,10},{10,... | collective-permute-start | bytes 27656 | tf_op jit(solution)/shard_map/ppermute | solution.py:76
  28.0 0.9 %collective-permute-done.12.back_ref = bf16[2,4,288]{2,1,0:T(4,128)(2,1)S(1)} collective-permute-done((bf16[2,4,288]{2,1,0:T(4,128)(2,1)S(1)}, bf16[2,4,288]{2,1,0:T(4,128)(2,1)S(1)}, u32[]{:S(2)}, u32[]{:S(2)}) %collective-permute-start.12) | collective-permute-done | bytes 4640 | tf_op jit(solution)/shard_map/ppermute | solution.py:71
  28.9 1.3 %collective-permute-done.14.refs_1_ = bf16[2,2,4,288]{3,2,1,0:T(4,128)(2,1)S(1)} collective-permute-done((bf16[2,2,4,288]{3,2,1,0:T(4,128)(2,1)S(1)}, bf16[2,2,4,288]{3,2,1,0:T(4,128)(2,1)S(1)}, u32[]{:S(2)}, u32[]{:S(2)}) %collective-permute-start.14) | collective-permute-done | bytes 9248 | tf_op jit(solution)/shard_map/ppermute | solution.py:76
  30.3 1.5 %attend.1.refs_0_ = bf16[4,4096]{1,0:T(4,128)(2,1)S(1)} custom-call(s32[4]{0:T(128)S(1)} %copy-done.3, bf16[4,2,4,288]{3,2,1,0:T(4,128)(2,1)S(1)} %get-tuple-element.13.near_ref, bf16[2,4,288]{2,1,0:T(4,128)(2,1)S(1)} %collective-permute-done.12.back_ref, bf16[2,2,4,288]{3,2,1,0:T(4,128)(2,1)S(1)} %collective-permute-done.13.refs_0_, ...), custom_call_target="tpu_custom_call" | custom-call | tf_op jit(solution)/shard_map/attend/pallas_call | solution.py:288
  31.8 0.4 collective-permute-start.18
  32.2 2.6 %collective-permute-start.16 = (bf16[4,4096]{1,0:T(4,128)(2,1)S(1)}, bf16[4,4096]{1,0:T(4,128)(2,1)S(1)}, u32[]{:S(2)}, u32[]{:S(2)}) collective-permute-start(bf16[4,4096]{1,0:T(4,128)(2,1)S(1)} %attend.1.refs_0_), channel_id=1, source_target_pairs={{0,9},{1,8},{2,11},{3,10},{4,13},{5,12},{6,15},{7,14},{8,1},{9,0},... | collective-permute-start | bytes 98312 | tf_op jit(solution)/shard_map/ppermute | solution.py:76
  34.9 1.6 %collective-permute-done.16.theirs_ref = bf16[4,4096]{1,0:T(4,128)(2,1)S(1)} collective-permute-done((bf16[4,4096]{1,0:T(4,128)(2,1)S(1)}, bf16[4,4096]{1,0:T(4,128)(2,1)S(1)}, u32[]{:S(2)}, u32[]{:S(2)}) %collective-permute-start.16) | collective-permute-done | bytes 32800 | tf_op jit(solution)/shard_map/ppermute | solution.py:76
  36.5 1.8 %collective-permute-start.21 = (bf16[8,4096]{1,0:T(8,128)(2,1)S(1)}, bf16[8,4096]{1,0:T(8,128)(2,1)S(1)}, u32[]{:S(2)}, u32[]{:S(2)}) collective-permute-start(bf16[8,4096]{1,0:T(8,128)(2,1)S(1)} %pair.1), channel_id=1, source_target_pairs={{0,7},{1,6},{2,5},{3,4},{4,3},{5,2},{6,1},{7,0},{8,15},{9,14},{10,... | collective-permute-start | bytes 196616 | tf_op jit(solution)/shard_map/ppermute | solution.py:76
  38.4 1.4 %collective-permute-start.19 = (bf16[8,4096]{1,0:T(8,128)(2,1)S(1)}, bf16[8,4096]{1,0:T(8,128)(2,1)S(1)}, u32[]{:S(2)}, u32[]{:S(2)}) collective-permute-start(bf16[8,4096]{1,0:T(8,128)(2,1)S(1)} %pair.1), channel_id=1, source_target_pairs={{0,3},{1,2},{2,1},{3,0},{4,7},{5,6},{6,5},{7,4},{8,11},{9,10},{10,... | collective-permute-start | bytes 196616 | tf_op jit(solution)/shard_map/ppermute | solution.py:76
  39.9 1.0 %collective-permute-done.17.refs_1_ = bf16[4,4096]{1,0:T(4,128)(2,1)S(1)} collective-permute-done((bf16[4,4096]{1,0:T(4,128)(2,1)S(1)}, bf16[4,4096]{1,0:T(4,128)(2,1)S(1)}, u32[]{:S(2)}, u32[]{:S(2)}) %collective-permute-start.17) | collective-permute-done | bytes 32800 | tf_op jit(solution)/shard_map/ppermute | solution.py:71
  41.0 0.6 %collective-permute-done.21.refs_4_ = bf16[8,4096]{1,0:T(8,128)(2,1)S(1)} collective-permute-done((bf16[8,4096]{1,0:T(8,128)(2,1)S(1)}, bf16[8,4096]{1,0:T(8,128)(2,1)S(1)}, u32[]{:S(2)}, u32[]{:S(2)}) %collective-permute-start.21) | collective-permute-done | bytes 65568 | tf_op jit(solution)/shard_map/ppermute | solution.py:76
  41.5 0.7 %collective-permute-done.20.refs_3_ = bf16[8,4096]{1,0:T(8,128)(2,1)S(1)} collective-permute-done((bf16[8,4096]{1,0:T(8,128)(2,1)S(1)}, bf16[8,4096]{1,0:T(8,128)(2,1)S(1)}, u32[]{:S(2)}, u32[]{:S(2)}) %collective-permute-start.20) | collective-permute-done | bytes 65568 | tf_op jit(solution)/shard_map/ppermute | solution.py:76
  42.2 1.0 %collective-permute-done.19.refs_2_ = bf16[8,4096]{1,0:T(8,128)(2,1)S(1)} collective-permute-done((bf16[8,4096]{1,0:T(8,128)(2,1)S(1)}, bf16[8,4096]{1,0:T(8,128)(2,1)S(1)}, u32[]{:S(2)}, u32[]{:S(2)}) %collective-permute-start.19) | collective-permute-done | bytes 65568 | tf_op jit(solution)/shard_map/ppermute | solution.py:76
  43.2 4.6 %output.1 = (bf16[16,2048]{1,0:T(8,128)(2,1)S(1)}, bf16[16,2048]{1,0:T(8,128)(2,1)S(1)}) custom-call(bf16[4,4096]{1,0:T(4,128)(2,1)S(1)} %attend.1.refs_0_, bf16[4,4096]{1,0:T(4,128)(2,1)S(1)} %collective-permute-done.17.refs_1_, bf16[8,4096]{1,0:T(8,128)(2,1)S(1)} %collective-permute-done.19.refs_2_, bf16[8,4096]{1,0:T(8,128)(2,1)S(1)} %collective-permute-done.20.refs_3_, ...), custom_call_target="tpu_custom_call" | custom-call | tf_op jit(solution)/shard_map/output/pallas_call | solution.py:305
  48.0 1.1 %collective-permute-done.22 = bf16[16,2048]{1,0:T(8,128)(2,1)S(1)} collective-permute-done((bf16[16,2048]{1,0:T(8,128)(2,1)S(1)}, bf16[16,2048]{1,0:T(8,128)(2,1)S(1)}, u32[]{:S(2)}, u32[]{:S(2)}) %collective-permute-start.22) | collective-permute-done | bytes 65568 | tf_op jit(solution)/shard_map/ppermute | solution.py:71
  49.1 0.6 %add_convert_fusion = bf16[16,2048]{1,0:T(8,128)(2,1)} fusion(bf16[16,2048]{1,0:T(8,128)(2,1)S(1)} %collective-permute-done.22, bf16[16,2048]{1,0:T(8,128)(2,1)S(1)} %get-tuple-element.19), kind=kLoop, calls=%fused_computation | loop fusion | flops 131072 | bytes 196608 | tf_op jit(solution)/shard_map/convert_element_type | solution.py:314
  (42 shorter events, 1.8 us)
Async XLA Ops:
  0.0 14.3 %copy-start = (bf16[4,288,8192]{2,1,0:T(8,128)(2,1)S(1)}, bf16[4,288,8192]{2,1,0:T(8,128)(2,1)}, u32[]{:S(2)}) copy-start(bf16[4,288,8192]{2,1,0:T(8,128)(2,1)} %refs_8_.3) | copy-start | bytes 56623108
  0.0 4.2 %collective-permute-start.2 = (bf16[4,8192]{1,0:T(4,128)(2,1)}, bf16[4,8192]{1,0:T(4,128)(2,1)S(1)}, u32[]{:S(2)}, u32[]{:S(2)}) collective-permute-start(bf16[4,8192]{1,0:T(4,128)(2,1)} %mine_ref.1), channel_id=1, source_target_pairs={{0,1},{1,0},{2,3},{3,2},{4,5},{5,4},{6,7},{7,6},{8,9},{9,8},{10,11... | collective-permute-start | bytes 196616 | tf_op jit(solution)/shard_map/ppermute | solution.py:71
  0.5 7.8 %collective-permute-start = (bf16[4,8192]{1,0:T(4,128)(2,1)}, bf16[4,8192]{1,0:T(4,128)(2,1)S(1)}, u32[]{:S(2)}, u32[]{:S(2)}) collective-permute-start(bf16[4,8192]{1,0:T(4,128)(2,1)} %mine_ref.1), channel_id=1, source_target_pairs={{0,9},{1,8},{2,11},{3,10},{4,13},{5,12},{6,15},{7,14},{8,1},{9,0},... | collective-permute-start | bytes 196616 | tf_op jit(solution)/shard_map/ppermute | solution.py:76
  4.2 5.7 %collective-permute-start.7 = (bf16[4,8192]{1,0:T(4,128)(2,1)S(1)}, bf16[4,8192]{1,0:T(4,128)(2,1)S(1)}, u32[]{:S(2)}, u32[]{:S(2)}) collective-permute-start(bf16[4,8192]{1,0:T(4,128)(2,1)S(1)} %collective-permute-done.2), channel_id=1, source_target_pairs={{0,7},{1,6},{2,5},{3,4},{4,3},{5,2},{6,1},{7,0},{8,15},{9,14},{10,... | collective-permute-start | bytes 196616 | tf_op jit(solution)/shard_map/ppermute | solution.py:76
  6.3 5.0 %collective-permute-start.5 = (bf16[4,8192]{1,0:T(4,128)(2,1)S(1)}, bf16[4,8192]{1,0:T(4,128)(2,1)S(1)}, u32[]{:S(2)}, u32[]{:S(2)}) collective-permute-start(bf16[4,8192]{1,0:T(4,128)(2,1)S(1)} %collective-permute-done.2), channel_id=1, source_target_pairs={{0,5},{1,4},{2,7},{3,6},{4,1},{5,0},{6,3},{7,2},{8,13},{9,12},{10,... | collective-permute-start | bytes 196616 | tf_op jit(solution)/shard_map/ppermute | solution.py:76
  6.8 5.7 %collective-permute-start.3 = (bf16[4,8192]{1,0:T(4,128)(2,1)S(1)}, bf16[4,8192]{1,0:T(4,128)(2,1)S(1)}, u32[]{:S(2)}, u32[]{:S(2)}) collective-permute-start(bf16[4,8192]{1,0:T(4,128)(2,1)S(1)} %collective-permute-done.2), channel_id=1, source_target_pairs={{0,3},{1,2},{2,1},{3,0},{4,7},{5,6},{6,5},{7,4},{8,11},{9,10},{10,... | collective-permute-start | bytes 196616 | tf_op jit(solution)/shard_map/ppermute | solution.py:76
  8.3 5.0 %collective-permute-start.8 = (bf16[4,8192]{1,0:T(4,128)(2,1)S(1)}, bf16[4,8192]{1,0:T(4,128)(2,1)S(1)}, u32[]{:S(2)}, u32[]{:S(2)}) collective-permute-start(bf16[4,8192]{1,0:T(4,128)(2,1)S(1)} %collective-permute-done), channel_id=1, source_target_pairs={{0,7},{1,6},{2,5},{3,4},{4,3},{5,2},{6,1},{7,0},{8,15},{9,14},{10,... | collective-permute-start | bytes 196616 | tf_op jit(solution)/shard_map/ppermute | solution.py:76
  9.8 4.4 %collective-permute-start.6 = (bf16[4,8192]{1,0:T(4,128)(2,1)S(1)}, bf16[4,8192]{1,0:T(4,128)(2,1)S(1)}, u32[]{:S(2)}, u32[]{:S(2)}) collective-permute-start(bf16[4,8192]{1,0:T(4,128)(2,1)S(1)} %collective-permute-done), channel_id=1, source_target_pairs={{0,5},{1,4},{2,7},{3,6},{4,1},{5,0},{6,3},{7,2},{8,13},{9,12},{10,... | collective-permute-start | bytes 196616 | tf_op jit(solution)/shard_map/ppermute | solution.py:76
  9.8 4.4 %collective-permute-start.4 = (bf16[4,8192]{1,0:T(4,128)(2,1)S(1)}, bf16[4,8192]{1,0:T(4,128)(2,1)S(1)}, u32[]{:S(2)}, u32[]{:S(2)}) collective-permute-start(bf16[4,8192]{1,0:T(4,128)(2,1)S(1)} %collective-permute-done), channel_id=1, source_target_pairs={{0,3},{1,2},{2,1},{3,0},{4,7},{5,6},{6,5},{7,4},{8,11},{9,10},{10,... | collective-permute-start | bytes 196616 | tf_op jit(solution)/shard_map/ppermute | solution.py:76
  11.4 2.9 %collective-permute-start.1 = (bf16[4,8192]{1,0:T(4,128)(2,1)S(1)}, bf16[4,8192]{1,0:T(4,128)(2,1)S(1)}, u32[]{:S(2)}, u32[]{:S(2)}) collective-permute-start(bf16[4,8192]{1,0:T(4,128)(2,1)S(1)} %collective-permute-done), channel_id=1, source_target_pairs={{0,1},{1,0},{2,3},{3,2},{4,5},{5,4},{6,7},{7,6},{8,9},{9,8},{10,11... | collective-permute-start | bytes 196616 | tf_op jit(solution)/shard_map/ppermute | solution.py:71
  11.6 0.8 %copy-start.4 = (bf16[4,8192]{1,0:T(4,128)(2,1)S(1)}, bf16[4,8192]{1,0:T(4,128)(2,1)}, u32[]{:S(2)}) copy-start(bf16[4,8192]{1,0:T(4,128)(2,1)} %mine_ref.1) | copy-start | bytes 196612
  12.5 17.8 %copy-start.1 = (bf16[4,2,512,128]{3,2,1,0:T(8,128)(2,1)S(1)}, bf16[4,2,512,128]{3,2,1,0:T(8,128)(2,1)}, u32[]{:S(2)}) copy-start(bf16[4,2,512,128]{3,2,1,0:T(8,128)(2,1)} %refs_3_.1) | copy-start | bytes 3145732
  12.5 17.8 %copy-start.2 = (bf16[4,2,512,128]{3,2,1,0:T(8,128)(2,1)S(1)}, bf16[4,2,512,128]{3,2,1,0:T(8,128)(2,1)}, u32[]{:S(2)}) copy-start(bf16[4,2,512,128]{3,2,1,0:T(8,128)(2,1)} %refs_4_.1) | copy-start | bytes 3145732
  12.5 17.8 %copy-start.3 = (s32[4]{0:T(128)S(1)}, s32[4]{0:T(128)}, u32[]{:S(2)}) copy-start(s32[4]{0:T(128)} %lengths_ref.1) | copy-start | bytes 52
  12.5 30.7 %slice-start = ((s8[16777216]{0:T(1024)(128)(4,1)}), s8[4194304]{0:T(1024)(128)(4,1)S(1)}, s32[]{:S(2)}) async-start(s8[16777216]{0:T(1024)(128)(4,1)} %bitcast), calls=%async_computation | async-start | bytes 8388608
  12.5 30.7 %slice-start.1 = ((s8[16777216]{0:T(1024)(128)(4,1)}), s8[4194304]{0:T(1024)(128)(4,1)S(1)}, s32[]{:S(2)}) async-start(s8[16777216]{0:T(1024)(128)(4,1)} %bitcast), calls=%async_computation.1 | async-start | bytes 8388608
  16.9 26.3 %slice-start.2 = ((s8[16777216]{0:T(1024)(128)(4,1)}), s8[4194304]{0:T(1024)(128)(4,1)S(1)}, s32[]{:S(2)}) async-start(s8[16777216]{0:T(1024)(128)(4,1)} %bitcast), calls=%async_computation.2 | async-start | bytes 8388608
  16.9 26.3 %slice-start.3 = ((s8[16777216]{0:T(1024)(128)(4,1)}), s8[4194304]{0:T(1024)(128)(4,1)S(1)}, s32[]{:S(2)}) async-start(s8[16777216]{0:T(1024)(128)(4,1)} %bitcast), calls=%async_computation.3 | async-start | bytes 8388608
  16.9 3.4 %collective-permute-start.9 = (bf16[2,32,288]{2,1,0:T(8,128)(2,1)S(1)}, bf16[2,32,288]{2,1,0:T(8,128)(2,1)S(1)}, u32[]{:S(2)}, u32[]{:S(2)}) collective-permute-start(bf16[2,32,288]{2,1,0:T(8,128)(2,1)S(1)} %project.3), channel_id=1, source_target_pairs={{0,1},{1,0},{2,3},{3,2},{4,5},{5,4},{6,7},{7,6},{8,9},{9,8},{10,11... | collective-permute-start | bytes 110600 | tf_op jit(solution)/shard_map/ppermute | solution.py:71
  20.3 4.3 %collective-permute-start.11 = (bf16[4,2,4,288]{3,2,1,0:T(4,128)(2,1)S(1)}, bf16[4,2,4,288]{3,2,1,0:T(4,128)(2,1)S(1)}, u32[]{:S(2)}, u32[]{:S(2)}) collective-permute-start(bf16[4,2,4,288]{3,2,1,0:T(4,128)(2,1)S(1)} %get-tuple-element.14), channel_id=1, source_target_pairs={{0,9},{1,8},{2,11},{3,10},{4,13},{5,12},{6,15},{7,14},{8,1},{9,0},... | collective-permute-start | bytes 55304 | tf_op jit(solution)/shard_map/ppermute | solution.py:76
  22.7 1.9 %collective-permute-start.10 = (bf16[4,2,4,288]{3,2,1,0:T(4,128)(2,1)S(1)}, bf16[4,2,4,288]{3,2,1,0:T(4,128)(2,1)S(1)}, u32[]{:S(2)}, u32[]{:S(2)}) collective-permute-start(bf16[4,2,4,288]{3,2,1,0:T(4,128)(2,1)S(1)} %get-tuple-element.13.near_ref), channel_id=1, source_target_pairs={{0,1},{1,0},{2,3},{3,2},{4,5},{5,4},{6,7},{7,6},{8,9},{9,8},{10,11... | collective-permute-start | bytes 55304 | tf_op jit(solution)/shard_map/ppermute | solution.py:71
  24.6 4.3 %collective-permute-start.13 = (bf16[2,2,4,288]{3,2,1,0:T(4,128)(2,1)S(1)}, bf16[2,2,4,288]{3,2,1,0:T(4,128)(2,1)S(1)}, u32[]{:S(2)}, u32[]{:S(2)}) collective-permute-start(bf16[2,2,4,288]{3,2,1,0:T(4,128)(2,1)S(1)} %get-tuple-element.16), channel_id=1, source_target_pairs={{0,7},{1,6},{2,5},{3,4},{4,3},{5,2},{6,1},{7,0},{8,15},{9,14},{10,... | collective-permute-start | bytes 27656 | tf_op jit(solution)/shard_map/ppermute | solution.py:76
  27.0 3.1 %collective-permute-start.14 = (bf16[2,2,4,288]{3,2,1,0:T(4,128)(2,1)S(1)}, bf16[2,2,4,288]{3,2,1,0:T(4,128)(2,1)S(1)}, u32[]{:S(2)}, u32[]{:S(2)}) collective-permute-start(bf16[2,2,4,288]{3,2,1,0:T(4,128)(2,1)S(1)} %get-tuple-element.17), channel_id=1, source_target_pairs={{0,5},{1,4},{2,7},{3,6},{4,1},{5,0},{6,3},{7,2},{8,13},{9,12},{10,... | collective-permute-start | bytes 27656 | tf_op jit(solution)/shard_map/ppermute | solution.py:76
  27.1 3.1 %collective-permute-start.15 = (bf16[2,2,4,288]{3,2,1,0:T(4,128)(2,1)S(1)}, bf16[2,2,4,288]{3,2,1,0:T(4,128)(2,1)S(1)}, u32[]{:S(2)}, u32[]{:S(2)}) collective-permute-start(bf16[2,2,4,288]{3,2,1,0:T(4,128)(2,1)S(1)} %get-tuple-element.18), channel_id=1, source_target_pairs={{0,3},{1,2},{2,1},{3,0},{4,7},{5,6},{6,5},{7,4},{8,11},{9,10},{10,... | collective-permute-start | bytes 27656 | tf_op jit(solution)/shard_map/ppermute | solution.py:76
  27.7 1.2 %collective-permute-start.12 = (bf16[2,4,288]{2,1,0:T(4,128)(2,1)S(1)}, bf16[2,4,288]{2,1,0:T(4,128)(2,1)S(1)}, u32[]{:S(2)}, u32[]{:S(2)}) collective-permute-start(bf16[2,4,288]{2,1,0:T(4,128)(2,1)S(1)} %get-tuple-element.15), channel_id=1, source_target_pairs={{0,1},{1,0},{2,3},{3,2},{4,5},{5,4},{6,7},{7,6},{8,9},{9,8},{10,11... | collective-permute-start | bytes 13832 | tf_op jit(solution)/shard_map/ppermute | solution.py:71
  31.8 3.1 %collective-permute-start.18 = (bf16[4,4096]{1,0:T(4,128)(2,1)S(1)}, bf16[4,4096]{1,0:T(4,128)(2,1)S(1)}, u32[]{:S(2)}, u32[]{:S(2)}) collective-permute-start(bf16[4,4096]{1,0:T(4,128)(2,1)S(1)} %attend.1.refs_0_), channel_id=1, source_target_pairs={{0,1},{1,0},{2,3},{3,2},{4,5},{5,4},{6,7},{7,6},{8,9},{9,8},{10,11... | collective-permute-start | bytes 98312 | tf_op jit(solution)/shard_map/ppermute | solution.py:71
  32.2 4.3 %collective-permute-start.16 = (bf16[4,4096]{1,0:T(4,128)(2,1)S(1)}, bf16[4,4096]{1,0:T(4,128)(2,1)S(1)}, u32[]{:S(2)}, u32[]{:S(2)}) collective-permute-start(bf16[4,4096]{1,0:T(4,128)(2,1)S(1)} %attend.1.refs_0_), channel_id=1, source_target_pairs={{0,9},{1,8},{2,11},{3,10},{4,13},{5,12},{6,15},{7,14},{8,1},{9,0},... | collective-permute-start | bytes 98312 | tf_op jit(solution)/shard_map/ppermute | solution.py:76
  36.5 5.0 %collective-permute-start.21 = (bf16[8,4096]{1,0:T(8,128)(2,1)S(1)}, bf16[8,4096]{1,0:T(8,128)(2,1)S(1)}, u32[]{:S(2)}, u32[]{:S(2)}) collective-permute-start(bf16[8,4096]{1,0:T(8,128)(2,1)S(1)} %pair.1), channel_id=1, source_target_pairs={{0,7},{1,6},{2,5},{3,4},{4,3},{5,2},{6,1},{7,0},{8,15},{9,14},{10,... | collective-permute-start | bytes 196616 | tf_op jit(solution)/shard_map/ppermute | solution.py:76
  38.3 3.9 %collective-permute-start.20 = (bf16[8,4096]{1,0:T(8,128)(2,1)S(1)}, bf16[8,4096]{1,0:T(8,128)(2,1)S(1)}, u32[]{:S(2)}, u32[]{:S(2)}) collective-permute-start(bf16[8,4096]{1,0:T(8,128)(2,1)S(1)} %pair.1), channel_id=1, source_target_pairs={{0,5},{1,4},{2,7},{3,6},{4,1},{5,0},{6,3},{7,2},{8,13},{9,12},{10,... | collective-permute-start | bytes 196616 | tf_op jit(solution)/shard_map/ppermute | solution.py:76
  38.4 4.8 %collective-permute-start.19 = (bf16[8,4096]{1,0:T(8,128)(2,1)S(1)}, bf16[8,4096]{1,0:T(8,128)(2,1)S(1)}, u32[]{:S(2)}, u32[]{:S(2)}) collective-permute-start(bf16[8,4096]{1,0:T(8,128)(2,1)S(1)} %pair.1), channel_id=1, source_target_pairs={{0,3},{1,2},{2,1},{3,0},{4,7},{5,6},{6,5},{7,4},{8,11},{9,10},{10,... | collective-permute-start | bytes 196616 | tf_op jit(solution)/shard_map/ppermute | solution.py:76
  39.7 1.2 %collective-permute-start.17 = (bf16[4,4096]{1,0:T(4,128)(2,1)S(1)}, bf16[4,4096]{1,0:T(4,128)(2,1)S(1)}, u32[]{:S(2)}, u32[]{:S(2)}) collective-permute-start(bf16[4,4096]{1,0:T(4,128)(2,1)S(1)} %collective-permute-done.16.theirs_ref), channel_id=1, source_target_pairs={{0,1},{1,0},{2,3},{3,2},{4,5},{5,4},{6,7},{7,6},{8,9},{9,8},{10,11... | collective-permute-start | bytes 98312 | tf_op jit(solution)/shard_map/ppermute | solution.py:71
  47.8 1.3 %collective-permute-start.22 = (bf16[16,2048]{1,0:T(8,128)(2,1)S(1)}, bf16[16,2048]{1,0:T(8,128)(2,1)S(1)}, u32[]{:S(2)}, u32[]{:S(2)}) collective-permute-start(bf16[16,2048]{1,0:T(8,128)(2,1)S(1)} %get-tuple-element.20), channel_id=1, source_target_pairs={{0,1},{1,0},{2,3},{3,2},{4,5},{5,4},{6,7},{7,6},{8,9},{9,8},{10,11... | collective-permute-start | bytes 196616 | tf_op jit(solution)/shard_map/ppermute | solution.py:71
